TPU v7x, 256 devices: a whole 4x4x8 slice. The times are simulated.
256 devices in a mesh: row: 16 (over z, core), dev: 16 (over x, y).
Axes of the slice: x: 4, y: 4, z: 8, core: 2. Of those that a mesh axis runs over, the one named last changes fastest.
Arguments:
- primary: bfloat16 [3, 64, 262144], P(None, None, ('row', 'dev')), may hold values from -6 to 6
- conductivity: bfloat16 [64, 262144], P(None, ('row', 'dev')), may hold values from 0.19921875 to 2
- anchor_x: int32 [16, 16], P('row'), may hold values from 0 to 464
- owner: int32 [16, 16], P('row'), may hold values from 0 to 15, as said below
- gate_index: int32 [30], replicated, may hold values from 0 to 63
- misfit: float32 [16, 16, 30], P('row'), may hold values from -1.2 to 1.2
Outputs:
- gradient: float32 [64, 262144], P(None, ('row', 'dev'))
- adjoint_field: float32 [512, 3, 40, 2304], P(('row', 'dev'))
Inputs may be any that keep to these rules, and one draw needn't show every extreme that they name: `owner`: in every block no device owns more than 2 footprints, and some device owns exactly 2.
All inputs are finite; a program needn't handle non-finite values.
Results may differ from a plain program's by a relative error of at most 0.0003.
Values may be sent and summed in bfloat16 or wider, within the bound.
No kernel may reach another device: no remote copies, remote signals or barrier semaphores. Data moves between devices by JAX's collectives and lax.ppermute only.
A program may use at most 128 MiB of HBM per device.

v0:
```python
import jax
import jax.numpy as jnp
from jax import lax
from jax.sharding import PartitionSpec as P

TX = 32
TY = 32
FZ = 40
FP = 48
GATES = 30
NTIMES = 64
STEPS = 2
MOST = 2


step_size = 0.05


def extended_2(array, sides, width):
    for axis, dim in sides:
        peers, length = (lax.axis_size(axis), array.shape[dim])
        up = [(i, (i + 1) % peers) for i in range(peers - 1)]
        down = [(j, i) for i, j in up]
        last = lax.slice_in_dim(array, length - width, length, axis=dim)
        leading = lax.slice_in_dim(array, 0, width, axis=dim)
        before = lax.ppermute(last, axis, up)
        after = lax.ppermute(leading, axis, down)
        array = jnp.concatenate([before, array, after], axis=dim)
    return array


def forward_diff(field, axis):
    size = field.shape[axis]
    ahead = jnp.concatenate(
        [
            lax.slice_in_dim(field, 1, size, axis=axis),
            jnp.zeros_like(lax.slice_in_dim(field, 0, 1, axis=axis)),
        ],
        axis,
    )
    return ahead - field


def adjoint_diff(field, axis):
    size = field.shape[axis]
    behind = jnp.concatenate(
        [
            jnp.zeros_like(lax.slice_in_dim(field, 0, 1, axis=axis)),
            lax.slice_in_dim(field, 0, size - 1, axis=axis),
        ],
        axis,
    )
    return behind - field


def curl_curl(lam):
    vx, vy, vz = (lam[0], lam[1], lam[2])
    wx = forward_diff(vz, 1) - forward_diff(vy, 0)
    wy = forward_diff(vx, 0) - forward_diff(vz, 2)
    wz = forward_diff(vy, 2) - forward_diff(vx, 1)
    ux = adjoint_diff(wy, 0) - adjoint_diff(wz, 1)
    uy = adjoint_diff(wz, 2) - adjoint_diff(wx, 0)
    uz = adjoint_diff(wx, 1) - adjoint_diff(wy, 2)
    return jnp.stack([ux, uy, uz], 0)


def footprint(window, residues, times):
    field = window[:3]
    sigma = window[3]

    def add_gate(g, acc):
        return acc + residues[g] * jnp.exp(-sigma * times[g])

    weight = lax.fori_loop(0, GATES, add_gate, jnp.zeros_like(sigma))
    lam = weight[None] * field
    for step in range(STEPS):
        lam = lam - step_size * (curl_curl(lam) + sigma[None] * lam)
    local = jnp.sum(lam * field, axis=0)
    return (lam, local)


def regularize(conductivity):
    logs = jnp.log(conductivity.astype(jnp.float32))
    delta = logs[1:] - logs[:-1]
    zero_row = jnp.zeros_like(logs[:1])
    return jnp.concatenate([zero_row, delta], 0) - jnp.concatenate([delta, zero_row], 0)


def per_device(primary, conductivity, anchor_x, owner, gate_index, misfit):
    halo_rows = (FP - TY) // 2
    width_x = TX * lax.axis_size("dev")
    times = 0.1 * jnp.float32(15.0) ** (gate_index.astype(jnp.float32) / jnp.float32(NTIMES - 1))
    tile = jnp.concatenate([primary[:, :FZ], conductivity[None, :FZ]], axis=0)
    band = extended_2(tile, (("row", 2),), halo_rows * TX)
    band = band.reshape(4, FZ, FP, TX)
    device = lax.axis_index("dev")
    anchors = anchor_x[0]
    owners = owner[0]
    residues = misfit[0]
    count = owners.shape[0]
    index = jnp.arange(count, dtype=jnp.int32)
    same = owners[:, None] == owners[None, :]
    rank = jnp.sum((same & (index[None, :] < index[:, None])).astype(jnp.int32), axis=1)
    slot_ids = jnp.arange(MOST, dtype=jnp.int32)
    pick = ((owners[None, :] == device) & (rank[None, :] == slot_ids[:, None])).astype(jnp.int32)
    slot_anchor = jnp.sum(pick * anchors[None, :], axis=1)
    slot_res = jnp.dot(pick.astype(jnp.float32), residues, precision=lax.Precision.HIGHEST)
    offsets = jnp.arange(FP, dtype=jnp.int32)
    whole = lax.all_gather(band, "dev", axis=3, tiled=True)

    def cut(anchor):
        zero = jnp.zeros((), jnp.int32)
        return lax.dynamic_slice(whole, (zero, zero, zero, anchor), (4, FZ, FP, FP))

    windows = jax.vmap(cut)(slot_anchor).astype(jnp.float32)

    def solve_slot(item):
        window, res = item
        return footprint(window, res, times)

    lams, locals_ = lax.map(solve_slot, (windows, slot_res))
    adjoint_field = lams.reshape(MOST, 3, FZ, FP * FP)
    columns = jnp.arange(width_x, dtype=jnp.int32)
    chooser = (
        columns[None, :, None] == slot_anchor[:, None, None] + offsets[None, None, :]
    ).astype(jnp.float32)
    summed = lax.psum(
        jnp.einsum("szyw,sxw->xzy", locals_, chooser, precision=lax.Precision.HIGHEST), "dev"
    )
    shares = lax.dynamic_slice_in_dim(summed, device * TX, TX, 0)
    extended = extended_2(shares, (("row", 2),), halo_rows)
    own = extended[:, :, 2 * halo_rows : 2 * halo_rows + TY]
    upper = jnp.pad(extended[:, :, :halo_rows], ((0, 0), (0, 0), (0, TY - halo_rows)))
    lower = jnp.pad(
        extended[:, :, FP + halo_rows : FP + 2 * halo_rows], ((0, 0), (0, 0), (TY - halo_rows, 0))
    )
    data = (own + upper + lower).transpose(1, 2, 0).reshape(FZ, TY * TX)
    gradient = regularize(conductivity)
    gradient = gradient.at[:FZ].add(data)
    return (gradient, adjoint_field)


def solution(mesh):
    in_specs = (
        P(None, None, ("row", "dev")),
        P(None, ("row", "dev")),
        P("row", None),
        P("row", None),
        P(),
        P("row", None, None),
    )
    out_specs = (P(None, ("row", "dev")), P(("row", "dev"), None, None, None))
    return jax.shard_map(
        per_device, mesh=mesh, in_specs=in_specs, out_specs=out_specs, check_vma=False
    )
```

profile of v0, /device:TPU:96, one launch (start us, length us, event | category | flops | bytes accessed | tf_op | source)
XLA Modules:
  0.0 613.0 jit_solution(2946544009939345107)
XLA Ops:
  9.1 1.9 collective-permute-start
  11.0 3.6 collective-permute-start.1
  14.9 2.1 collective-permute-done.1
  18.3 3.5 copy.22
  23.0 140.0 %all-gather.2.cloned.1.call-done = bf16[4,40,48,512]{2,1,0,3:T(8,128)(2,1)} async-done(((bf16[4,40,48,32]{2,1,0,3:T(8,128)(2,1)}), bf16[4,40,48,512]{2,1,0,3:T(8,128)(2,1)}) %all-gather.2.cloned.1.call-update) | async-done | bytes 7864336 | tf_op jit(solution)/shard_map/all_gather | solution.py:109
  163.0 10.0 %gather_fusion = bf16[2,4,40,48,48]{3,2,1,4,0:T(8,128)(2,1)} fusion(bf16[4,40,48,512]{2,1,0,3:T(8,128)(2,1)} %all-gather.2.cloned.1.call-done, s32[2]{0:T(128)S(1)} %fusion.29), kind=kCustom, calls=%fused_computation | custom fusion | bytes 2949152 | tf_op jit(solution)/shard_map/vmap()/gather | solution.py:113
  173.0 6.2 %convert_element_type.27 = f32[2,4,40,48,48]{3,2,1,4,0:T(8,128)} convert(bf16[2,4,40,48,48]{3,2,1,4,0:T(8,128)(2,1)} %gather_fusion) | non-fusion elementwise | flops 737280 | bytes 4423680 | tf_op jit(solution)/shard_map/convert_element_type | solution.py:115
  179.2 231.2 %while.30 = (s32[]{:T(128)}, f32[2,3,40,48,48]{4,3,2,1,0:T(8,128)}, f32[2,40,48,48]{3,2,0,1:T(8,128)}, f32[2,30]{1,0:T(2,128)S(1)}, f32[2,4,40,48,48]{3,2,1,4,0:...) while((s32[]{:T(128)}, f32[2,3,40,48,48]{4,3,2,1,0:T(8,128)}, ...), condition=%wide.region_6.7_spmd, body=%wide.region_2.6_spmd.sunk | while | flops 13639686 | bytes 71541896 | solution.py:121
  181.0 90.5 %while.31 = (s32[]{:T(128)}, f32[40,48,48]{2,1,0:T(8,128)S(1)}, f32[30]{0:T(128)S(1)}, f32[30]{0:T(128)S(1)}, f32[40,48,48]{2,1,0:T(8,128)S(1)}, /*index=5*/s32[]{:T(128)}, s32[]{:T(128)}) while((s32[]{:T(128)}, f32[40,48,48]{2,1,0:T(8,128)S(1)}, f32[30]{0:T(128)S(1)}, f32[30]{0:T(128)S(1)}, f32[40,48,48]{2,1,0:T(8,128)S(1)}, ...), condition=%wide.region_4.4_spmd.clone, body=%wide.region_3.3_spmd.clone.sunk | while | flops 368643 | bytes 1106039 | solution.py:74
  182.2 1.7 select_add_fusion.2
  185.3 1.7 select_add_fusion.2
  188.3 1.7 select_add_fusion.2
  191.3 1.7 select_add_fusion.2
  194.3 1.7 select_add_fusion.2
  200.3 1.7 select_add_fusion.2
  203.4 1.7 select_add_fusion.2
  206.4 1.7 select_add_fusion.2
  209.4 1.7 select_add_fusion.2
  212.4 1.7 select_add_fusion.2
  218.4 1.7 select_add_fusion.2
  221.4 1.7 select_add_fusion.2
  224.5 1.7 select_add_fusion.2
  227.5 1.7 select_add_fusion.2
  230.5 1.7 select_add_fusion.2
  236.5 1.7 select_add_fusion.2
  239.5 1.7 select_add_fusion.2
  242.6 1.7 select_add_fusion.2
  245.6 1.7 select_add_fusion.2
  248.6 1.7 select_add_fusion.2
  251.6 1.7 select_add_fusion.2
  257.6 1.7 select_add_fusion.2
  260.6 1.7 select_add_fusion.2
  263.7 1.7 select_add_fusion.2
  266.7 1.7 select_add_fusion.2
  271.4 3.8 constant_dynamic-slice_fusion.7
  275.2 4.8 copy.42
  279.9 2.2 bitcast_multiply_fusion.2
  292.5 2.4 fusion.38
  296.5 90.5 %while.31 = (s32[]{:T(128)}, f32[40,48,48]{2,1,0:T(8,128)S(1)}, f32[30]{0:T(128)S(1)}, f32[30]{0:T(128)S(1)}, f32[40,48,48]{2,1,0:T(8,128)S(1)}, /*index=5*/s32[]{:T(128)}, s32[]{:T(128)}) while((s32[]{:T(128)}, f32[40,48,48]{2,1,0:T(8,128)S(1)}, f32[30]{0:T(128)S(1)}, f32[30]{0:T(128)S(1)}, f32[40,48,48]{2,1,0:T(8,128)S(1)}, ...), condition=%wide.region_4.4_spmd.clone, body=%wide.region_3.3_spmd.clone.sunk | while | flops 368643 | bytes 1106039 | solution.py:74
  387.0 3.8 constant_dynamic-slice_fusion.7
  390.8 4.8 copy.42
  395.5 2.2 bitcast_multiply_fusion.2
  408.0 2.4 fusion.38
  410.4 8.5 %convolution_bitcast_fusion = f32[512,40,48]{2,0,1:T(8,128)} fusion(f32[2,40,48,48]{3,2,0,1:T(8,128)} %get-tuple-element.175, s32[2,48]{1,0:T(2,128)S(1)} %copy-done.7), kind=kOutput, calls=%fused_computation.46 | convolution fusion | flops 1132560384 | bytes 4669824 | tf_op jit(solution)/shard_map/szyw,sxw->xzy/dot_general | solution.py:128
  419.9 168.7 %all-reduce.30.cloned.1.call-done = f32[512,40,48]{2,0,1:T(8,128)} async-done(((f32[512,40,48]{2,0,1:T(8,128)}), f32[512,40,48]{2,0,1:T(8,128)}) %all-reduce.30.cloned.1.call-update) | async-done | bytes 3932176 | tf_op jit(solution)/shard_map/psum | solution.py:127
  590.5 1.9 collective-permute-start.2
  592.8 3.6 collective-permute-start.3
  596.5 5.7 reshape.98
  (272 shorter events, 172.2 us)
Async XLA Ops:
  7.2 15.8 %copy-start = (f32[1,16,30]{2,1,0:T(8,128)S(1)}, f32[1,16,30]{2,1,0:T(8,128)}, u32[]{:S(2)}) copy-start(f32[1,16,30]{2,1,0:T(8,128)} %param.17) | copy-start | bytes 5764
  7.2 155.8 %all-gather.2.cloned.1.call-start = ((), (), s32[]{:S(2)}) async-start(), calls=%async_computation | async-start | bytes 22282240 | tf_op jit(solution)/shard_map/all_gather | solution.py:109
  9.1 5.8 collective-permute-start
  11.0 5.9 collective-permute-start.1
  17.0 4.9 copy-start.9
  17.0 5.1 copy-start.8
  17.0 5.3 copy-start.10
  21.9 566.7 %all-reduce.30.cloned.1.call-start = ((), (), s32[]{:S(2)}) async-start(), calls=%async_computation.1 | async-start | bytes 20971520 | tf_op jit(solution)/shard_map/psum | solution.py:127
  179.2 231.2 %copy-start.7 = (s32[2,48]{1,0:T(2,128)S(1)}, s32[2,48]{1,0:T(2,128)}, u32[]{:S(2)}) copy-start(s32[2,48]{1,0:T(2,128)} %iota_add_fusion) | copy-start | bytes 1156
  284.1 1.8 copy-start.2
  289.5 1.6 copy-start.3
  291.2 1.3 copy-start.4
  399.6 1.8 copy-start.2
  405.1 1.6 copy-start.3
  406.8 1.3 copy-start.4
  418.9 0.9 copy-start.5
  590.5 11.7 %collective-permute-start.2 = (f32[32,40,8]{1,2,0:T(8,128)S(1)}, f32[32,40,8]{1,2,0:T(8,128)S(1)}, u32[]{:S(2)}, u32[]{:S(2)}) collective-permute-start(f32[32,40,8]{1,2,0:T(8,128)S(1)} %copy.25), channel_id=1, source_target_pairs={{0,16},{16,32},{32,48},{48,64},{64,80},{80,96},{96,112},{112,128},... | collective-permute-start | bytes 122888 | tf_op jit(solution)/shard_map/ppermute | solution.py:26
  592.8 10.0 %collective-permute-start.3 = (f32[32,40,8]{1,2,0:T(8,128)S(1)}, f32[32,40,8]{1,2,0:T(8,128)S(1)}, u32[]{:S(2)}, u32[]{:S(2)}) collective-permute-start(f32[32,40,8]{1,2,0:T(8,128)S(1)} %copy.27), channel_id=1, source_target_pairs={{16,0},{32,16},{48,32},{64,48},{80,64},{96,80},{112,96},{128,112},... | collective-permute-start | bytes 122888 | tf_op jit(solution)/shard_map/ppermute | solution.py:27
  602.2 4.0 copy-start.1
  605.5 0.7 copy-start.6
Sparse Core Ops, SparseCore 0:
  22.0 140.9 all-gather.1
  419.1 169.4 all-reduce.29
where the time goes:
time: 617 us; the launch traced here: 613 us
  waiting for transfers between devices  311 us (50%)
  local copies, waits for them, and re-layouts  134 us (22%)
  other arithmetic  132 us (21%)
  between operations  14.3 us (2%)
  starting transfers between devices  11.2 us (2%)
  matrix products  8.62 us (1%)
    psum x1, waiting for transfers between devices, per_device(): lax.psum(jnp.einsum('szyw,sxw->xzy', locals_, chooser, precision=lax.Prec...  169 us
    all_gather x1, waiting for transfers between devices, per_device(): whole = lax.all_gather(band, 'dev', axis=3, tiled=True)  140 us
    add x60, other arithmetic, add_gate(): return acc + residues[g] * jnp.exp(-sigma * times[g])  103 us
    dynamic_slice x120, local copies, waits for them, and re-layouts, add_gate(): return acc + residues[g] * jnp.exp(-sigma * times[g])  76.2 us
    while x16, local copies, waits for them, and re-layouts  14.6 us
  transfers between devices with their start and end apart: 6, of which 4 were waited for; matrix products, arithmetic and copies ran while one was open for 1% of the time, Pallas kernels for 0%

commit v1 on v0

v1 whole, which is shorter than its diff:
```python
import jax
import jax.numpy as jnp
from jax import lax
from jax.experimental import pallas as pl
from jax.experimental.pallas import tpu as pltpu
from jax.sharding import PartitionSpec as P

TX = 32
TY = 32
FZ = 40
FP = 48
GATES = 30
NTIMES = 64
STEPS = 2
MOST = 2
FOOT_ROW = 16
HALO = 8
N_DEV = 16
STEP = 0.05

LANES = FP * FP
QROWS = 12
QIN = QROWS * TX
BLOCK = MOST * QROWS * FP
BAND = FP * TX
LOG2E = 1.4426950408889634
LN15 = 2.70805020110221


def lane_iota(rows):
    return lax.broadcasted_iota(jnp.int32, (rows, 128), 1)


def cut_kernel(anchor, owner, tiles, out, count):
    for e in range(N_DEV):
        count[e] = 0
    lane = lane_iota(8)
    rows = []
    for v in range(5):
        at = lane + 128 * v
        y = sum((at >= FP * j).astype(jnp.int32) for j in range(1, QROWS + 1))
        rows.append((y, at - FP * y))

    def one(f, carry):
        o, e = anchor[0, f], owner[0, f]
        k = count[e]
        count[e] = k + 1
        d0, s = o // TX, o % TX
        full = pl.multiple_of(640 * k, 128)
        for v in range(5):
            y_of, x_of = rows[v]
            code = y_of * 4 + lax.shift_right_logical(x_of + s, 5)
            acc = jnp.zeros((FZ, 128), jnp.float32)
            for y in range(QROWS):
                if FP * y >= 128 * (v + 1) or FP * (y + 1) <= 128 * v:
                    continue
                for t in range(3):
                    src = tiles[jnp.minimum(d0 + t, N_DEV - 1), :, 128 * (y // 4) : 128 * (y // 4) + 128]
                    shift = (FP * y - TX * (y % 4) + TX * t - s) % 128
                    turned = pltpu.roll(src.astype(jnp.float32), shift, 1)
                    mask = code == 4 * y + t
                    acc = jnp.where(jnp.concatenate([mask] * 5, 0), turned, acc)
            if v < 4:
                out[e, :, pl.ds(full + 128 * v, 128)] = acc.astype(jnp.bfloat16)
            else:
                held = out[e, :, 512:640].astype(jnp.float32)
                low = lane_iota(FZ) < 64
                first = jnp.where(k == 0, acc, held)
                out[e, :, 512:640] = jnp.where(low, first, pltpu.roll(acc, 64, 1)).astype(jnp.bfloat16)
        return carry

    lax.fori_loop(0, FOOT_ROW, one, 0)


def solve_kernel(me_ref, anchor, owner, gates, misfit, parts, lam_out, canvas, window, lam, curl, local, x_masks):
    me = me_ref[0]
    cnt = jnp.int32(0)
    mine = [jnp.int32(0), jnp.int32(0)]
    for f in range(FOOT_ROW):
        hit = owner[0, f] == me
        for k in range(MOST):
            mine[k] = jnp.where(hit & (cnt == k), f, mine[k])
        cnt = cnt + hit.astype(jnp.int32)

    canvas[...] = jnp.zeros_like(canvas)
    lam[:, FZ:, :] = jnp.zeros((3, 8, LANES), jnp.float32)
    curl[:, :8, :] = jnp.zeros((3, 8, LANES), jnp.float32)
    x_of = lax.broadcasted_iota(jnp.int32, (8, LANES), 1) % FP
    x_masks[0] = (x_of != FP - 1).astype(jnp.float32)
    x_masks[1] = (x_of != 0).astype(jnp.float32)
    times = 0.1 * jnp.exp((LN15 / (NTIMES - 1)) * gates[...].astype(jnp.float32))
    scaled = -LOG2E * times
    all_lanes = lax.broadcasted_iota(jnp.int32, (8, LANES), 1)
    last_y = all_lanes >= LANES - FP
    first_y = all_lanes < FP

    def ahead_x(v):
        return pltpu.roll(v, LANES - 1, 1) * x_masks[0]

    def behind_x(v):
        return pltpu.roll(v, 1, 1) * x_masks[1]

    def ahead_y(v):
        return jnp.where(last_y, 0.0, pltpu.roll(v, LANES - FP, 1))

    def behind_y(v):
        return jnp.where(first_y, 0.0, pltpu.roll(v, FP, 1))

    for k in range(MOST):

        @pl.when(cnt <= k)
        def _(k=k):
            lam_out[k] = jnp.zeros((3, FZ, LANES), jnp.float32)

        @pl.when(cnt > k)
        def _(k=k):
            f = mine[k]
            o = anchor[0, f]
            low = lane_iota(FZ) < 64
            for c in range(4):
                for half in range(2):
                    base = 1152 * half
                    p, q = 4 * c + 2 * half, 4 * c + 2 * half + 1
                    full = slice(640 * k, 640 * k + 512)
                    pf = parts[p, :, full].astype(jnp.float32)
                    qf = pltpu.roll(parts[q, :, full].astype(jnp.float32), 64, 1)
                    ph = parts[p, :, 512:640].astype(jnp.float32)
                    qh = parts[q, :, 512:640].astype(jnp.float32)
                    if k == 0:
                        qh = pltpu.roll(qh, 64, 1)
                    else:
                        ph = pltpu.roll(ph, 64, 1)
                    window[c, :, base : base + 512] = pf
                    window[c, :, base + 512 : base + 640] = jnp.where(low, ph, qf[:, :128])
                    window[c, :, base + 640 : base + 1024] = qf[:, 128:]
                    window[c, :, base + 1024 : base + 1152] = jnp.where(low, qf[:, :128], qh)
            residue = misfit[pl.ds(f, 1), :]
            t_of = [jnp.broadcast_to(scaled[:, g : g + 1], (8, 128)) for g in range(GATES)]
            r_of = [jnp.broadcast_to(residue[:, g : g + 1], (8, 128)) for g in range(GATES)]

            def weigh(i, carry):
                z = pl.ds(pl.multiple_of(8 * i, 8), 8)
                for c0 in range(0, LANES, 384):
                    at = slice(c0, c0 + 384)
                    sigma = window[3, z, at]
                    weight = jnp.zeros_like(sigma)
                    for g in range(GATES):
                        t3 = jnp.concatenate([t_of[g]] * 3, 1)
                        r3 = jnp.concatenate([r_of[g]] * 3, 1)
                        weight = weight + r3 * jnp.exp2(sigma * t3)
                    for c in range(3):
                        lam[c, z, at] = weight * window[c, z, at]
                return carry

            lax.fori_loop(0, FZ // 8, weigh, 0)

            def step(n, carry):
                for i in range(FZ // 8):
                    z = slice(8 * i, 8 * i + 8)
                    up = slice(8 * i + 1, 8 * i + 9)
                    vx, vy, vz = lam[0, z, :], lam[1, z, :], lam[2, z, :]
                    at = slice(8 * i + 8, 8 * i + 16)
                    curl[0, at, :] = (ahead_y(vz) - vz) - (lam[1, up, :] - vy)
                    curl[1, at, :] = (lam[0, up, :] - vx) - (ahead_x(vz) - vz)
                    curl[2, at, :] = (ahead_x(vy) - vy) - (ahead_y(vx) - vx)
                for i in range(FZ // 8):
                    z = slice(8 * i, 8 * i + 8)
                    at = slice(8 * i + 8, 8 * i + 16)
                    down = slice(8 * i + 7, 8 * i + 15)
                    wx, wy, wz = curl[0, at, :], curl[1, at, :], curl[2, at, :]
                    ux = (curl[1, down, :] - wy) - (behind_y(wz) - wz)
                    uy = (behind_x(wz) - wz) - (curl[0, down, :] - wx)
                    uz = (behind_y(wx) - wx) - (behind_x(wy) - wy)
                    sigma = window[3, z, :]
                    for c, u in enumerate((ux, uy, uz)):
                        v = lam[c, z, :]
                        lam[c, z, :] = v - STEP * (u + sigma * v)
                return carry

            lax.fori_loop(0, STEPS, step, 0)
            for i in range(FZ // 8):
                z = slice(8 * i, 8 * i + 8)
                total = None
                for c in range(3):
                    v = lam[c, z, :]
                    lam_out[k, c, z, :] = v
                    term = v * window[c, z, :]
                    total = term if total is None else total + term
                local[z, :] = total
            d0, s = o // TX, o % TX
            lane = lane_iota(8)
            row_in, x_in = lane // TX, lane % TX

            def place(t, carry):
                d = jnp.minimum(d0 + t, N_DEV - 1)
                xw = x_in + (TX * t - s)
                inside = (xw >= 0) & (xw < FP)
                for v in range(FP // 4):
                    acc = canvas[d, :, 128 * v : 128 * v + 128]
                    for j in range(4):
                        y = 4 * v + j
                        a = FP * y // 128
                        spill = 128 * (a + 1) - FP * y
                        shift = (TX * j - FP * y + s - TX * t) % 128
                        for b in range(2 if spill < FP else 1):
                            mask = inside & (row_in == j)
                            if spill < FP:
                                mask = mask & ((xw >= spill) if b else (xw < spill))
                            src = local[:, 128 * (a + b) : 128 * (a + b) + 128]
                            turned = pltpu.roll(src, shift, 1)
                            acc = acc + jnp.where(jnp.concatenate([mask] * 5, 0), turned, 0.0)
                    canvas[d, :, 128 * v : 128 * v + 128] = acc
                return carry

            lax.fori_loop(0, 3, place, 0)


def regularize(conductivity):
    logs = jnp.log(conductivity.astype(jnp.float32))
    delta = logs[1:] - logs[:-1]
    zero_row = jnp.zeros_like(logs[:1])
    return jnp.concatenate([zero_row, delta], 0) - jnp.concatenate([delta, zero_row], 0)


def neighbours(first, last, axis):
    peers = lax.axis_size(axis)
    up = [(i, i + 1) for i in range(peers - 1)]
    down = [(i + 1, i) for i in range(peers - 1)]
    return lax.ppermute(last, axis, up), lax.ppermute(first, axis, down)


SMEM = pl.BlockSpec(memory_space=pltpu.SMEM)
VMEM = pl.BlockSpec(memory_space=pltpu.VMEM)
LIMIT = 48 * 2**20


def per_device(primary, conductivity, anchor_x, owner, gate_index, misfit):
    me = lax.axis_index("dev").astype(jnp.int32).reshape(1)
    tile = jnp.concatenate([primary[:, :FZ], conductivity[None, :FZ]], axis=0)
    halo = HALO * TX
    before, after = neighbours(tile[..., :halo], tile[..., -halo:], "row")
    chunks = [
        jnp.concatenate([before, tile[..., : QIN - halo]], -1),
        tile[..., QIN - halo : 2 * QIN - halo],
        tile[..., 2 * QIN - halo : 3 * QIN - halo],
        jnp.concatenate([tile[..., 3 * QIN - halo :], after], -1),
    ]
    spread = jnp.stack(chunks, 1).reshape(N_DEV, FZ, QIN)
    spread = lax.all_to_all(spread, "dev", 0, 0, tiled=True)
    windows = pl.pallas_call(
        cut_kernel,
        out_shape=jax.ShapeDtypeStruct((N_DEV, FZ, BLOCK), jnp.bfloat16),
        in_specs=[SMEM, SMEM, VMEM],
        out_specs=VMEM,
        scratch_shapes=[pltpu.SMEM((N_DEV,), jnp.int32)],
        compiler_params=pltpu.CompilerParams(vmem_limit_bytes=LIMIT),
        name="cut",
    )(anchor_x, owner, spread)
    parts = lax.all_to_all(windows, "dev", 0, 0, tiled=True)
    adjoint_field, canvas = pl.pallas_call(
        solve_kernel,
        out_shape=(
            jax.ShapeDtypeStruct((MOST, 3, FZ, LANES), jnp.float32),
            jax.ShapeDtypeStruct((N_DEV, FZ, BAND), jnp.float32),
        ),
        in_specs=[SMEM, SMEM, SMEM, VMEM, VMEM, VMEM],
        out_specs=(VMEM, VMEM),
        scratch_shapes=[
            pltpu.VMEM((4, FZ, LANES), jnp.float32),
            pltpu.VMEM((3, FZ + 8, LANES), jnp.float32),
            pltpu.VMEM((3, FZ + 8, LANES), jnp.float32),
            pltpu.VMEM((FZ, LANES), jnp.float32),
            pltpu.VMEM((2, 8, LANES), jnp.float32),
        ],
        compiler_params=pltpu.CompilerParams(vmem_limit_bytes=LIMIT),
        name="solve",
    )(me, anchor_x, owner, gate_index.reshape(1, GATES), misfit[0], parts)
    summed = jnp.sum(lax.all_to_all(canvas, "dev", 0, 0, tiled=True), axis=0)
    from_before, from_after = neighbours(summed[:, :halo], summed[:, -halo:], "row")
    data = summed[:, halo:-halo]
    data = data + jnp.pad(from_before, ((0, 0), (0, TX * TY - halo)))
    data = data + jnp.pad(from_after, ((0, 0), (TX * TY - halo, 0)))
    gradient = regularize(conductivity)
    gradient = gradient + jnp.pad(data, ((0, gradient.shape[0] - FZ), (0, 0)))
    return gradient, adjoint_field


def solution(mesh):
    in_specs = (
        P(None, None, ("row", "dev")),
        P(None, ("row", "dev")),
        P("row", None),
        P("row", None),
        P(),
        P("row", None, None),
    )
    out_specs = (P(None, ("row", "dev")), P(("row", "dev"), None, None, None))
    return jax.shard_map(
        per_device, mesh=mesh, in_specs=in_specs, out_specs=out_specs, check_vma=False
    )
```

time: 617 us -> 154 us (0.25)
  the two profiles are of different devices: /device:TPU:96 before, /device:TPU:157 now
where the time goes in v1:
time: 154 us
  waiting for transfers between devices  68 us (44%)
  starting transfers between devices  56.7 us (37%)
  blocking collectives  13 us (8%)
  Pallas kernels  8.03 us (5%)
  local copies, waits for them, and re-layouts  3.8 us (2%)
  other arithmetic  3.35 us (2%)
    all_to_all x1, waiting for transfers between devices, per_device(): summed = jnp.sum(lax.all_to_all(canvas, 'dev', 0, 0, tiled=True), axis=0)  44.4 us
    ppermute x4, starting transfers between devices, neighbours(): return (lax.ppermute(last, axis, up), lax.ppermute(first, axis, down))  31.9 us
    all_to_all x1, starting transfers between devices, per_device(): summed = jnp.sum(lax.all_to_all(canvas, 'dev', 0, 0, tiled=True), axis=0)  17.7 us
    all_to_all x1, waiting for transfers between devices, per_device(): parts = lax.all_to_all(windows, 'dev', 0, 0, tiled=True)  16.5 us
    all_to_all x1, blocking collectives, per_device(): spread = lax.all_to_all(spread, 'dev', 0, 0, tiled=True)  13 us
    ppermute x4, waiting for transfers between devices, neighbours(): return (lax.ppermute(last, axis, up), lax.ppermute(first, axis, down))  7.08 us
    all_to_all x1, starting transfers between devices, per_device(): parts = lax.all_to_all(windows, 'dev', 0, 0, tiled=True)  7.07 us
    pallas_call x1, Pallas kernels, per_device(): pl.pallas_call(cut_kernel, out_shape=jax.ShapeDtypeStruct((N_DEV, FZ, BLO...  5.69 us
  transfers between devices with their start and end apart: 6, of which 4 were waited for; matrix products, arithmetic and copies ran while one was open for 0% of the time, Pallas kernels for 0%

profile of v1, /device:TPU:157, one launch (start us, length us, event | category | flops | bytes accessed | tf_op | source)
XLA Modules:
  0.0 153.6 jit_solution(5580358437645683527)
XLA Ops:
  0.6 1.0 slice.41
  1.6 0.9 slice_bitcast_fusion
  2.5 3.2 %collective-permute-start = (bf16[4,40,256]{2,1,0:T(8,128)(2,1)S(1)}, bf16[4,40,256]{2,1,0:T(8,128)(2,1)S(1)}, u32[]{:S(2)}, u32[]{:S(2)}) collective-permute-start(bf16[4,40,256]{2,1,0:T(8,128)(2,1)S(1)} %get-tuple-element.6), channel_id=1, source_target_pairs={{0,16},{16,32},{32,48},{48,64},{64,80},{80,96},{96,112},{112,128},... | collective-permute-start | bytes 245768 | tf_op jit(solution)/shard_map/ppermute | solution.py:229
  5.7 0.0 copy-start.2
  5.7 0.0 copy-start.3
  5.7 1.9 %collective-permute-start.1 = (bf16[4,40,256]{2,1,0:T(8,128)(2,1)S(1)}, bf16[4,40,256]{2,1,0:T(8,128)(2,1)S(1)}, u32[]{:S(2)}, u32[]{:S(2)}) collective-permute-start(bf16[4,40,256]{2,1,0:T(8,128)(2,1)S(1)} %get-tuple-element.7), channel_id=1, source_target_pairs={{16,0},{32,16},{48,32},{64,48},{80,64},{96,80},{112,96},{128,112},... | collective-permute-start | bytes 245768 | tf_op jit(solution)/shard_map/ppermute | solution.py:229
  7.7 0.0 collective-permute-done
  7.8 3.7 %collective-permute-done.1 = bf16[4,40,256]{2,1,0:T(8,128)(2,1)S(1)} collective-permute-done((bf16[4,40,256]{2,1,0:T(8,128)(2,1)S(1)}, bf16[4,40,256]{2,1,0:T(8,128)(2,1)S(1)}, u32[]{:S(2)}, u32[]{:S(2)}) %collective-permute-start.1) | collective-permute-done | bytes 81952 | tf_op jit(solution)/shard_map/ppermute | solution.py:229
  11.5 0.1 pad_maximum_fusion
  11.6 0.1 copy.8
  11.7 13.0 %all_to_all.15.tiles = bf16[16,40,384]{2,1,0:T(8,128)(2,1)S(1)} all-to-all(bf16[16,40,384]{2,1,0:T(8,128)(2,1)S(1)} %bitcast.16), channel_id=1, replica_groups=mesh['row'=16,'dev'=16] {'dev'}, dimensions={0} | all-to-all | bytes 983040 | tf_op jit(solution)/shard_map/all_to_all | solution.py:249
  24.7 0.0 copy-done.2
  24.7 0.0 copy-done.3
  24.7 0.0 copy-start.1
  24.7 0.0 copy-start.4
  24.7 5.7 %cut.1 = bf16[16,40,1152]{2,1,0:T(8,128)(2,1)} custom-call(s32[1,16]{1,0:T(1,128)S(1)} %copy-done.2, s32[1,16]{1,0:T(1,128)S(1)} %copy-done.3, bf16[16,40,384]{2,1,0:T(8,128)(2,1)S(1)} %all_to_all.15.tiles), custom_call_target="tpu_custom_call" | custom-call | tf_op jit(solution)/shard_map/cut/pallas_call | solution.py:250
  30.4 7.1 %all-to-all-start.1 = ((bf16[16,40,1152]{2,1,0:T(8,128)(2,1)}), bf16[16,40,1152]{2,1,0:T(8,128)(2,1)S(1)}, u32[]{:S(2)}, u32[]{:S(2)}) async-start(bf16[16,40,1152]{2,1,0:T(8,128)(2,1)} %cut.1), calls=%async_computation.1 | async-start | bytes 2949120 | tf_op jit(solution)/shard_map/all_to_all | solution.py:259
  37.4 16.5 %all-to-all-done.1.parts = bf16[16,40,1152]{2,1,0:T(8,128)(2,1)S(1)} async-done(((bf16[16,40,1152]{2,1,0:T(8,128)(2,1)}), bf16[16,40,1152]{2,1,0:T(8,128)(2,1)S(1)}, u32[]{:S(2)}, u32[]{:S(2)}) %all-to-all-start.1) | async-done | bytes 1474592 | tf_op jit(solution)/shard_map/all_to_all | solution.py:259
  53.9 0.0 copy-done.1
  53.9 0.0 copy-done.4
  53.9 2.3 %solve.1 = (f32[2,3,40,2304]{3,2,1,0:T(8,128)}, f32[16,40,1536]{2,1,0:T(8,128)S(1)}) custom-call(s32[1]{0:T(128)} %bitcast.me_ref, s32[1,16]{1,0:T(1,128)S(1)} %copy-done.2, s32[1,16]{1,0:T(1,128)S(1)} %copy-done.3, s32[1,30]{1,0:T(1,128)S(1)} %bitcast.15, f32[16,30]{1,0:T(8,128)S(1)} %bitcast.14, bf16[16,40,1152]{2,1,0:T(8,128)(2,1)S(1)} %all-to-all-done.1.parts), custom_call_target="tpu_custom_call" | custom-call | tf_op jit(solution)/shard_map/solve/pallas_call | solution.py:260
  56.3 0.0 copy-start
  56.3 1.9 %copy-done = f32[16,40,1536]{2,1,0:T(8,128)} copy-done((f32[16,40,1536]{2,1,0:T(8,128)}, f32[16,40,1536]{2,1,0:T(8,128)S(1)}, u32[]{:S(2)}) %copy-start) | copy-done | bytes 3932184
  58.1 0.0 copy-start.5
  58.1 17.7 %all-to-all-start.2 = ((f32[16,40,1536]{2,1,0:T(8,128)}), f32[16,40,1536]{2,1,0:T(8,128)}, u32[]{:S(2)}, u32[]{:S(2)}) async-start(f32[16,40,1536]{2,1,0:T(8,128)} %copy-done), calls=%async_computation.2 | async-start | bytes 7864320 | tf_op jit(solution)/shard_map/all_to_all | solution.py:278
  75.8 0.0 copy-done.5
  75.9 44.4 %all-to-all-done.2 = f32[16,40,1536]{2,1,0:T(8,128)} async-done(((f32[16,40,1536]{2,1,0:T(8,128)}), f32[16,40,1536]{2,1,0:T(8,128)}, u32[]{:S(2)}, u32[]{:S(2)}) %all-to-all-start.2) | async-done | bytes 3932192 | tf_op jit(solution)/shard_map/all_to_all | solution.py:278
  120.3 2.3 %reduce_sum.9 = f32[40,1536]{1,0:T(8,128)S(1)} reduce(f32[16,40,1536]{2,1,0:T(8,128)} %all-to-all-done.2, f32[]{:T(128)} %constant.2.clone.1), dimensions={0}, to_apply=%region_0.0 | reduce | flops 921600 | bytes 4177924 | tf_op jit(solution)/shard_map/reduce_sum | solution.py:278
  122.7 24.9 %collective-permute-start.2 = (f32[40,256]{1,0:T(8,128)S(1)}, f32[40,256]{1,0:T(8,128)S(1)}, u32[]{:S(2)}, u32[]{:S(2)}) collective-permute-start(f32[40,256]{1,0:T(8,128)S(1)} %get-tuple-element.12), channel_id=1, source_target_pairs={{0,16},{16,32},{32,48},{48,64},{64,80},{80,96},{96,112},{112,128},... | collective-permute-start | bytes 122888 | tf_op jit(solution)/shard_map/ppermute | solution.py:229
  147.6 1.9 %collective-permute-start.3 = (f32[40,256]{1,0:T(8,128)S(1)}, f32[40,256]{1,0:T(8,128)S(1)}, u32[]{:S(2)}, u32[]{:S(2)}) collective-permute-start(f32[40,256]{1,0:T(8,128)S(1)} %get-tuple-element.13), channel_id=1, source_target_pairs={{16,0},{32,16},{48,32},{64,48},{80,64},{96,80},{112,96},{128,112},... | collective-permute-start | bytes 122888 | tf_op jit(solution)/shard_map/ppermute | solution.py:229
  149.5 0.0 collective-permute-done.2
  149.5 3.3 %collective-permute-done.3 = f32[40,256]{1,0:T(8,128)S(1)} collective-permute-done((f32[40,256]{1,0:T(8,128)S(1)}, f32[40,256]{1,0:T(8,128)S(1)}, u32[]{:S(2)}, u32[]{:S(2)}) %collective-permute-start.3) | collective-permute-done | bytes 40992 | tf_op jit(solution)/shard_map/ppermute | solution.py:229
  152.9 0.7 pad_add_fusion
  (9 shorter events, 0.2 us)
Async XLA Ops:
  2.5 5.2 %collective-permute-start = (bf16[4,40,256]{2,1,0:T(8,128)(2,1)S(1)}, bf16[4,40,256]{2,1,0:T(8,128)(2,1)S(1)}, u32[]{:S(2)}, u32[]{:S(2)}) collective-permute-start(bf16[4,40,256]{2,1,0:T(8,128)(2,1)S(1)} %get-tuple-element.6), channel_id=1, source_target_pairs={{0,16},{16,32},{32,48},{48,64},{64,80},{80,96},{96,112},{112,128},... | collective-permute-start | bytes 245768 | tf_op jit(solution)/shard_map/ppermute | solution.py:229
  5.7 18.9 %copy-start.2 = (s32[1,16]{1,0:T(1,128)S(1)}, s32[1,16]{1,0:T(1,128)}, u32[]{:S(2)}) copy-start(s32[1,16]{1,0:T(1,128)} %anchor.3) | copy-start | bytes 196
  5.7 18.9 %copy-start.3 = (s32[1,16]{1,0:T(1,128)S(1)}, s32[1,16]{1,0:T(1,128)}, u32[]{:S(2)}) copy-start(s32[1,16]{1,0:T(1,128)} %owner.3) | copy-start | bytes 196
  5.7 5.8 %collective-permute-start.1 = (bf16[4,40,256]{2,1,0:T(8,128)(2,1)S(1)}, bf16[4,40,256]{2,1,0:T(8,128)(2,1)S(1)}, u32[]{:S(2)}, u32[]{:S(2)}) collective-permute-start(bf16[4,40,256]{2,1,0:T(8,128)(2,1)S(1)} %get-tuple-element.7), channel_id=1, source_target_pairs={{16,0},{32,16},{48,32},{64,48},{80,64},{96,80},{112,96},{128,112},... | collective-permute-start | bytes 245768 | tf_op jit(solution)/shard_map/ppermute | solution.py:229
  24.7 29.2 %copy-start.1 = (f32[1,16,30]{2,1,0:T(8,128)S(1)}, f32[1,16,30]{2,1,0:T(8,128)}, u32[]{:S(2)}) copy-start(f32[1,16,30]{2,1,0:T(8,128)} %param.11) | copy-start | bytes 5764
  24.7 29.2 %copy-start.4 = (s32[30]{0:T(128)S(1)}, s32[30]{0:T(128)}, u32[]{:S(2)}) copy-start(s32[30]{0:T(128)} %param.10) | copy-start | bytes 364
  30.4 23.5 %all-to-all-start.1 = ((bf16[16,40,1152]{2,1,0:T(8,128)(2,1)}), bf16[16,40,1152]{2,1,0:T(8,128)(2,1)S(1)}, u32[]{:S(2)}, u32[]{:S(2)}) async-start(bf16[16,40,1152]{2,1,0:T(8,128)(2,1)} %cut.1), calls=%async_computation.1 | async-start | bytes 2949120 | tf_op jit(solution)/shard_map/all_to_all | solution.py:259
  56.3 1.9 %copy-start = (f32[16,40,1536]{2,1,0:T(8,128)}, f32[16,40,1536]{2,1,0:T(8,128)S(1)}, u32[]{:S(2)}) copy-start(f32[16,40,1536]{2,1,0:T(8,128)S(1)} %get-tuple-element.4) | copy-start | bytes 11796484
  58.1 17.7 %copy-start.5 = (bf16[64,1024]{1,0:T(8,128)(2,1)S(1)}, bf16[64,1024]{1,0:T(8,128)(2,1)}, u32[]{:S(2)}) copy-start(bf16[64,1024]{1,0:T(8,128)(2,1)} %param.7) | copy-start | bytes 393220
  58.1 62.2 %all-to-all-start.2 = ((f32[16,40,1536]{2,1,0:T(8,128)}), f32[16,40,1536]{2,1,0:T(8,128)}, u32[]{:S(2)}, u32[]{:S(2)}) async-start(f32[16,40,1536]{2,1,0:T(8,128)} %copy-done), calls=%async_computation.2 | async-start | bytes 7864320 | tf_op jit(solution)/shard_map/all_to_all | solution.py:278
  122.7 26.9 %collective-permute-start.2 = (f32[40,256]{1,0:T(8,128)S(1)}, f32[40,256]{1,0:T(8,128)S(1)}, u32[]{:S(2)}, u32[]{:S(2)}) collective-permute-start(f32[40,256]{1,0:T(8,128)S(1)} %get-tuple-element.12), channel_id=1, source_target_pairs={{0,16},{16,32},{32,48},{48,64},{64,80},{80,96},{96,112},{112,128},... | collective-permute-start | bytes 122888 | tf_op jit(solution)/shard_map/ppermute | solution.py:229
  147.6 5.3 %collective-permute-start.3 = (f32[40,256]{1,0:T(8,128)S(1)}, f32[40,256]{1,0:T(8,128)S(1)}, u32[]{:S(2)}, u32[]{:S(2)}) collective-permute-start(f32[40,256]{1,0:T(8,128)S(1)} %get-tuple-element.13), channel_id=1, source_target_pairs={{16,0},{32,16},{48,32},{64,48},{80,64},{96,80},{112,96},{128,112},... | collective-permute-start | bytes 122888 | tf_op jit(solution)/shard_map/ppermute | solution.py:229

commit v2 on v0

v2 whole, which is shorter than its diff:
```python
import jax
import jax.numpy as jnp
from jax import lax
from jax.experimental import pallas as pl
from jax.experimental.pallas import tpu as pltpu
from jax.sharding import PartitionSpec as P

TX = 32
TY = 32
FZ = 40
FP = 48
GATES = 30
NTIMES = 64
STEPS = 2
MOST = 2
FOOT_ROW = 16
HALO = 8
N_DEV = 16
STEP = 0.05

LANES = FP * FP
QROWS = 12
QIN = QROWS * TX
CUT = 640
RROWS = 3
BACK = 896
UNROLL = 4
LOG2E = 1.4426950408889634
LN15 = 2.70805020110221


def turn(v, by):
    return pltpu.roll(v, by % 128, 1)


def lane_iota(rows):
    return lax.broadcasted_iota(jnp.int32, (rows, 128), 1)


def tall(mask):
    return jnp.concatenate([mask] * (FZ // 8), 0)


def assign(owner, table, seconds):
    for e in range(N_DEV):
        table[0, e] = -1
        table[1, e] = -1
    for f in range(FOOT_ROW):
        e = owner[0, f]
        held, other = table[0, e], table[1, e]
        table[0, e] = jnp.where(held >= 0, held, f)
        table[1, e] = jnp.where(held >= 0, f, other)
    n = jnp.int32(0)
    for e in range(N_DEV):
        other = table[1, e]
        seconds[n] = other
        n = n + (other >= 0).astype(jnp.int32)
    n = jnp.int32(0)
    for e in range(N_DEV):
        held = table[0, e]
        table[2, e] = (held >= 0).astype(jnp.int32)
        table[0, e] = jnp.where(held >= 0, held, seconds[n])
        n = n + (held < 0).astype(jnp.int32)


def cut_kernel(anchor, owner, tiles, out, second, table, seconds):
    assign(owner, table, seconds)
    row_in = lane_iota(8) // TX
    picks = []
    for v in range(5):
        at = lane_iota(8) + 128 * v
        y = sum((at >= FP * j).astype(jnp.int32) for j in range(1, QROWS + 1))
        picks.append((y, at - FP * y))

    def one(e, carry):
        f = table[0, e]
        o, w = anchor[0, f], owner[0, f]
        d0, s = o // TX, o % TX
        made = [jnp.zeros((FZ, 128), jnp.float32) for _ in range(5)]
        codes = [8 * (y // 4) + y % 4 + 2 * lax.shift_right_logical(x + s, 5) for y, x in picks]
        for m in range(QROWS // 4):
            tile = [
                tiles[jnp.minimum(d0 + t, N_DEV - 1), :, 128 * m : 128 * m + 128].astype(jnp.float32) for t in range(3)
            ]
            for n in range(8):
                from_t = [t for t in range(3) if 0 <= n - 2 * t < 4]
                src = tile[from_t[0]]
                for t in from_t[1:]:
                    src = jnp.where(tall(row_in == n - 2 * t), tile[t], src)
                turned = turn(src, 192 * m + 16 * n - s)
                rows = [(n - 2 * t, t) for t in from_t]
                for v in range(5):
                    if any(
                        192 * m + FP * j + max(0, TX * t - 31) < 128 * (v + 1)
                        and 192 * m + FP * j + min(FP, TX * (t + 1)) > 128 * v
                        for j, t in rows
                    ):
                        made[v] = jnp.where(tall(codes[v] == 8 * m + n), turned, made[v])
        for v in range(5):
            out[e, :, 128 * v : 128 * v + 128] = made[v].astype(jnp.bfloat16)

        @pl.when(table[1, w] == f)
        def _():
            second[w] = out[e]

        return carry

    lax.fori_loop(0, N_DEV, one, 0)


def adjoint(f, gates, misfit, parts, window, lam, curl, x_masks):
    lam[:, FZ:, :] = jnp.zeros((3, 8, LANES), jnp.float32)
    curl[:, :8, :] = jnp.zeros((3, 8, LANES), jnp.float32)
    x_of = lax.broadcasted_iota(jnp.int32, (8, LANES), 1) % FP
    x_masks[0] = (x_of != FP - 1).astype(jnp.float32)
    x_masks[1] = (x_of != 0).astype(jnp.float32)
    times = 0.1 * jnp.exp((LN15 / (NTIMES - 1)) * gates[...].astype(jnp.float32))
    scaled = -LOG2E * times
    all_lanes = lax.broadcasted_iota(jnp.int32, (8, LANES), 1)
    last_y = all_lanes >= LANES - FP
    first_y = all_lanes < FP

    def ahead_x(v):
        return pltpu.roll(v, LANES - 1, 1) * x_masks[0]

    def behind_x(v):
        return pltpu.roll(v, 1, 1) * x_masks[1]

    def ahead_y(v):
        return jnp.where(last_y, 0.0, pltpu.roll(v, LANES - FP, 1))

    def behind_y(v):
        return jnp.where(first_y, 0.0, pltpu.roll(v, FP, 1))

    low = lane_iota(FZ) < 64
    for c in range(4):
        for half in range(2):
            base = 1152 * half
            p, q = 4 * c + 2 * half, 4 * c + 2 * half + 1
            pf = parts[p, :, :512].astype(jnp.float32)
            qf = pltpu.roll(parts[q, :, :512].astype(jnp.float32), 64, 1)
            ph = parts[p, :, 512:640].astype(jnp.float32)
            qh = turn(parts[q, :, 512:640].astype(jnp.float32), 64)
            window[c, :, base : base + 512] = pf
            window[c, :, base + 512 : base + 640] = jnp.where(low, ph, qf[:, :128])
            window[c, :, base + 640 : base + 1024] = qf[:, 128:]
            window[c, :, base + 1024 : base + 1152] = jnp.where(low, qf[:, :128], qh)
    residue = misfit[pl.ds(f, 1), :]
    t_of = [jnp.broadcast_to(scaled[:, g : g + 1], (8, 128)) for g in range(GATES)]
    r_of = [jnp.broadcast_to(residue[:, g : g + 1], (8, 128)) for g in range(GATES)]

    def weigh(i, carry):
        z = pl.ds(pl.multiple_of(8 * i, 8), 8)
        for c0 in range(0, LANES, 384):
            at = slice(c0, c0 + 384)
            sigma = window[3, z, at]
            weight = jnp.zeros_like(sigma)
            for g in range(GATES):
                t3 = jnp.concatenate([t_of[g]] * 3, 1)
                r3 = jnp.concatenate([r_of[g]] * 3, 1)
                weight = weight + r3 * jnp.exp2(sigma * t3)
            for c in range(3):
                lam[c, z, at] = weight * window[c, z, at]
        return carry

    lax.fori_loop(0, FZ // 8, weigh, 0)

    def step(n, carry):
        for i in range(FZ // 8):
            z = slice(8 * i, 8 * i + 8)
            up = slice(8 * i + 1, 8 * i + 9)
            vx, vy, vz = lam[0, z, :], lam[1, z, :], lam[2, z, :]
            at = slice(8 * i + 8, 8 * i + 16)
            curl[0, at, :] = (ahead_y(vz) - vz) - (lam[1, up, :] - vy)
            curl[1, at, :] = (lam[0, up, :] - vx) - (ahead_x(vz) - vz)
            curl[2, at, :] = (ahead_x(vy) - vy) - (ahead_y(vx) - vx)
        for i in range(FZ // 8):
            z = slice(8 * i, 8 * i + 8)
            at = slice(8 * i + 8, 8 * i + 16)
            down = slice(8 * i + 7, 8 * i + 15)
            wx, wy, wz = curl[0, at, :], curl[1, at, :], curl[2, at, :]
            ux = (curl[1, down, :] - wy) - (behind_y(wz) - wz)
            uy = (behind_x(wz) - wz) - (curl[0, down, :] - wx)
            uz = (behind_y(wx) - wx) - (behind_x(wy) - wy)
            sigma = window[3, z, :]
            for c, u in enumerate((ux, uy, uz)):
                v = lam[c, z, :]
                lam[c, z, :] = v - STEP * (u + sigma * v)
        return carry

    lax.fori_loop(0, STEPS, step, 0)


def solve_kernel(me, table, gates, misfit, parts, second, adjoint_out, back, window, lam, curl, local, x_masks, sem):
    f, own = table[0, me[0]], table[2, me[0]]
    adjoint(f, gates, misfit, parts, window, lam, curl, x_masks)
    for i in range(FZ // 8):
        z = slice(8 * i, 8 * i + 8)
        total = None
        for c in range(3):
            v = lam[c, z, :]
            lam[c, z, :] = jnp.where(own == 1, v, 0.0)
            term = v * window[c, z, :]
            total = term if total is None else total + term
        local[z, :] = total
    copy = pltpu.make_async_copy(lam.at[:, :FZ, :], adjoint_out.at[0], sem)
    copy.start()
    lane = lane_iota(FZ)
    for j in range(N_DEV):
        a, r = 144 * j // 128, 144 * j % 128
        both = [local[:, 128 * (a + b) : 128 * (a + b) + 128] for b in range(2)]
        high = [v.astype(jnp.bfloat16).astype(jnp.float32) for v in both]
        rest = [turn(v - h, 80 - r) for v, h in zip(both, high)]
        high = [turn(h, 64 - r) for h in high]
        back[j, :, :512] = second[j, :, :512]
        v4 = jnp.where(lane - 64 < 128 - r, high[0], high[1])
        v4 = jnp.where(lane < 64, second[j, :, 512:640].astype(jnp.float32), v4)
        v5 = jnp.where(lane + 64 < 128 - r, high[0], high[1])
        v5 = jnp.where(lane < 80, v5, jnp.where(lane - 80 < 128 - r, rest[0], rest[1]))
        v6 = jnp.where(lane + 48 < 128 - r, rest[0], rest[1])
        for b, v in enumerate((v4, v5, v6)):
            back[j, :, 512 + 128 * b : 640 + 128 * b] = v.astype(jnp.bfloat16)
    copy.wait()


def second_kernel(me, table, gates, misfit, parts, adjoint_in, adjoint_out, window, lam, curl, x_masks, sem):
    del adjoint_in
    f = table[1, me[0]]

    @pl.when(f >= 0)
    def _():
        adjoint(f, gates, misfit, parts, window, lam, curl, x_masks)

    @pl.when(f < 0)
    def _():
        lam[:, :FZ, :] = jnp.zeros((3, FZ, LANES), jnp.float32)

    copy = pltpu.make_async_copy(lam.at[:, :FZ, :], adjoint_out.at[1], sem)
    copy.start()
    copy.wait()


def scatter_kernel(anchor, table, back, out):
    out[...] = jnp.zeros_like(out)
    lane = lane_iota(FZ)
    row_in, x_in = lane_iota(8) // TX, lane_iota(8) % TX

    def one(e, carry):
        o = anchor[0, table[0, e]]
        d0, s = o // TX, o % TX
        v4, v5, v6 = (back[e, :, 512 + 128 * b : 640 + 128 * b].astype(jnp.float32) for b in range(3))
        r5, s6 = turn(v5, 64), turn(v6, 48)
        first = jnp.where(lane < 64, turn(v4, 64), r5) + jnp.where(lane < 48, turn(v5, 48), s6)
        rest = r5 + s6
        moved = [turn(first, s - 16 * n) for n in range(6)] + [turn(jnp.where(lane < 16, rest, first), s - 96)]
        spilt = {2: turn(rest, s - 32), 4: turn(rest, s - 64), 6: moved[6]}
        for t in range(3):
            xw = x_in + (TX * t - s)
            inside = (xw >= 0) & (xw < FP)
            add = jnp.where(tall(inside & (row_in == 0)), moved[2 * t], 0.0)
            add = jnp.where(tall(inside & (row_in == 1)), moved[2 * t + 1], add)
            add = jnp.where(tall(inside & (row_in == 2) & (xw < 32)), moved[2 * t + 2], add)
            add = jnp.where(tall(inside & (row_in == 2) & (xw >= 32)), spilt[2 * t + 2], add)
            d = jnp.minimum(d0 + t, N_DEV - 1)
            out[d] = out[d] + add
        return carry

    lax.fori_loop(0, N_DEV, one, 0, unroll=UNROLL)


def join_kernel(sums, first, own, last):
    lane = lane_iota(FZ)
    made = []
    for g in range(0, N_DEV, 4):
        a = sums[g]
        b, c, d = (turn(sums[g + n], 128 - 32 * n) for n in range(1, 4))
        made += [jnp.where(lane < 96, a, b), jnp.where(lane < 64, b, c), jnp.where(lane < 32, c, d)]
    for n in range(2):
        first[:, 128 * n : 128 * n + 128] = made[n]
        last[:, 128 * n : 128 * n + 128] = made[10 + n]
    for n in range(8):
        own[:, 128 * n : 128 * n + 128] = made[2 + n]


def regularize(conductivity):
    logs = jnp.log(conductivity.astype(jnp.float32))
    delta = logs[1:] - logs[:-1]
    zero_row = jnp.zeros_like(logs[:1])
    return jnp.concatenate([zero_row, delta], 0) - jnp.concatenate([delta, zero_row], 0)


def neighbours(first, last, axis):
    peers = lax.axis_size(axis)
    up = [(i, i + 1) for i in range(peers - 1)]
    down = [(i + 1, i) for i in range(peers - 1)]
    return lax.ppermute(last, axis, up), lax.ppermute(first, axis, down)


SMEM = pl.BlockSpec(memory_space=pltpu.SMEM)
VMEM = pl.BlockSpec(memory_space=pltpu.VMEM)
ANY = pl.BlockSpec(memory_space=pl.ANY)
PARAMS = pltpu.CompilerParams(vmem_limit_bytes=40 * 2**20)
F32 = jnp.float32
WORK = [
    pltpu.VMEM((4, FZ, LANES), F32),
    pltpu.VMEM((3, FZ + 8, LANES), F32),
    pltpu.VMEM((3, FZ + 8, LANES), F32),
]
MASKS = pltpu.VMEM((2, 8, LANES), F32)


def exchange(blocks):
    return lax.all_to_all(blocks, "dev", 0, 0, tiled=True)


def per_device(primary, conductivity, anchor_x, owner, gate_index, misfit):
    me = lax.axis_index("dev").astype(jnp.int32).reshape(1)
    gates, residues = gate_index.reshape(1, GATES), misfit[0]
    tile = jnp.concatenate([primary[:, :FZ], conductivity[None, :FZ]], axis=0)
    halo = HALO * TX
    before, after = neighbours(tile[..., :halo], tile[..., -halo:], "row")
    chunks = [
        jnp.concatenate([before, tile[..., : QIN - halo]], -1),
        tile[..., QIN - halo : 2 * QIN - halo],
        tile[..., 2 * QIN - halo : 3 * QIN - halo],
        jnp.concatenate([tile[..., 3 * QIN - halo :], after], -1),
    ]
    spread = exchange(jnp.stack(chunks, 1).reshape(N_DEV, FZ, QIN))
    cut_shape = jax.ShapeDtypeStruct((N_DEV, FZ, CUT), jnp.bfloat16)
    windows, second, table = pl.pallas_call(
        cut_kernel,
        out_shape=(cut_shape, cut_shape, jax.ShapeDtypeStruct((3, N_DEV), jnp.int32)),
        in_specs=[SMEM, SMEM, VMEM],
        out_specs=(VMEM, VMEM, SMEM),
        scratch_shapes=[pltpu.SMEM((N_DEV + 1,), jnp.int32)],
        compiler_params=PARAMS,
        name="cut",
    )(anchor_x, owner, spread)
    adjoint_shape = jax.ShapeDtypeStruct((MOST, 3, FZ, LANES), F32)
    field, back = pl.pallas_call(
        solve_kernel,
        out_shape=(adjoint_shape, jax.ShapeDtypeStruct((N_DEV, FZ, BACK), jnp.bfloat16)),
        in_specs=[SMEM, SMEM, VMEM, VMEM, VMEM, VMEM],
        out_specs=(ANY, VMEM),
        scratch_shapes=[*WORK, pltpu.VMEM((FZ, LANES), F32), MASKS, pltpu.SemaphoreType.DMA],
        compiler_params=PARAMS,
        name="solve",
    )(me, table, gates, residues, exchange(windows), second)
    back = exchange(back)
    columns = pl.pallas_call(
        scatter_kernel,
        out_shape=jax.ShapeDtypeStruct((N_DEV, FZ, 128), F32),
        in_specs=[SMEM, SMEM, VMEM],
        out_specs=VMEM,
        compiler_params=PARAMS,
        name="scatter",
    )(anchor_x, table, back)
    adjoint_field = pl.pallas_call(
        second_kernel,
        out_shape=adjoint_shape,
        in_specs=[SMEM, SMEM, VMEM, VMEM, VMEM, ANY],
        out_specs=ANY,
        scratch_shapes=[*WORK, MASKS, pltpu.SemaphoreType.DMA],
        input_output_aliases={5: 0},
        compiler_params=PARAMS,
        cost_estimate=pl.CostEstimate(flops=2 * 10**7, bytes_accessed=4 * 10**6, transcendentals=3 * 10**6),
        name="second",
    )(me, table, gates, residues, back, field)
    sums, adjoint_field = lax.optimization_barrier((exchange(columns), adjoint_field))
    half = jax.ShapeDtypeStruct((FZ, halo), F32)
    first, own, last = pl.pallas_call(
        join_kernel,
        out_shape=(half, jax.ShapeDtypeStruct((FZ, TX * TY), F32), half),
        in_specs=[VMEM],
        out_specs=(VMEM, VMEM, VMEM),
        compiler_params=PARAMS,
        name="join",
    )(sums)
    from_before, from_after = neighbours(first, last, "row")
    data = own + jnp.pad(from_before, ((0, 0), (0, TX * TY - halo)))
    data = data + jnp.pad(from_after, ((0, 0), (TX * TY - halo, 0)))
    gradient = regularize(conductivity)
    gradient = gradient + jnp.pad(data, ((0, gradient.shape[0] - FZ), (0, 0)))
    return gradient, adjoint_field


def solution(mesh):
    in_specs = (
        P(None, None, ("row", "dev")),
        P(None, ("row", "dev")),
        P("row", None),
        P("row", None),
        P(),
        P("row", None, None),
    )
    out_specs = (P(None, ("row", "dev")), P(("row", "dev"), None, None, None))
    return jax.shard_map(
        per_device, mesh=mesh, in_specs=in_specs, out_specs=out_specs, check_vma=False
    )
```

time: 617 us -> 107 us (0.17)
  the two profiles are of different devices: /device:TPU:96 before, /device:TPU:1 now
where the time goes in v2:
time: 107 us
  blocking collectives  37.2 us (35%)
  waiting for transfers between devices  27.5 us (26%)
  starting transfers between devices  23.2 us (22%)
  Pallas kernels  15 us (14%)
  local copies, waits for them, and re-layouts  1.94 us (2%)
    all_to_all x2, blocking collectives, exchange(): return lax.all_to_all(blocks, 'dev', 0, 0, tiled=True)  37.2 us
    all_to_all x2, waiting for transfers between devices, exchange(): return lax.all_to_all(blocks, 'dev', 0, 0, tiled=True)  20.4 us
    ppermute x4, starting transfers between devices, neighbours(): return (lax.ppermute(last, axis, up), lax.ppermute(first, axis, down))  16 us
    all_to_all x2, starting transfers between devices, exchange(): return lax.all_to_all(blocks, 'dev', 0, 0, tiled=True)  7.17 us
    ppermute x4, waiting for transfers between devices, neighbours(): return (lax.ppermute(last, axis, up), lax.ppermute(first, axis, down))  7.08 us
    pallas_call x1, Pallas kernels, per_device(): pl.pallas_call(solve_kernel, out_shape=(adjoint_shape, jax.ShapeDtypeStru...  5.65 us
    pallas_call x1, Pallas kernels, per_device(): pl.pallas_call(cut_kernel, out_shape=(cut_shape, cut_shape, jax.ShapeDtyp...  4.32 us
    pallas_call x1, Pallas kernels, per_device(): pl.pallas_call(scatter_kernel, out_shape=jax.ShapeDtypeStruct((N_DEV, FZ,...  3.21 us
  transfers between devices with their start and end apart: 6, of which 4 were waited for; matrix products, arithmetic and copies ran while one was open for 0% of the time, Pallas kernels for 2%

profile of v2, /device:TPU:1, one launch (start us, length us, event | category | flops | bytes accessed | tf_op | source)
XLA Modules:
  0.0 106.6 jit_solution(11725547204810145527)
XLA Ops:
  0.6 1.0 slice.32
  1.6 0.9 slice_bitcast_fusion
  2.5 4.9 %collective-permute-start = (bf16[4,40,256]{2,1,0:T(8,128)(2,1)S(1)}, bf16[4,40,256]{2,1,0:T(8,128)(2,1)S(1)}, u32[]{:S(2)}, u32[]{:S(2)}) collective-permute-start(bf16[4,40,256]{2,1,0:T(8,128)(2,1)S(1)} %get-tuple-element.22), channel_id=1, source_target_pairs={{0,16},{16,32},{32,48},{48,64},{64,80},{80,96},{96,112},{112,128},... | collective-permute-start | bytes 245768 | tf_op jit(solution)/shard_map/ppermute | solution.py:296
  7.5 0.0 copy-start.1
  7.5 0.0 copy-start.3
  7.5 1.9 %collective-permute-start.1 = (bf16[4,40,256]{2,1,0:T(8,128)(2,1)S(1)}, bf16[4,40,256]{2,1,0:T(8,128)(2,1)S(1)}, u32[]{:S(2)}, u32[]{:S(2)}) collective-permute-start(bf16[4,40,256]{2,1,0:T(8,128)(2,1)S(1)} %get-tuple-element.23), channel_id=1, source_target_pairs={{16,0},{32,16},{48,32},{64,48},{80,64},{96,80},{112,96},{128,112},... | collective-permute-start | bytes 245768 | tf_op jit(solution)/shard_map/ppermute | solution.py:296
  9.5 0.0 collective-permute-done
  9.5 3.7 %collective-permute-done.1 = bf16[4,40,256]{2,1,0:T(8,128)(2,1)S(1)} collective-permute-done((bf16[4,40,256]{2,1,0:T(8,128)(2,1)S(1)}, bf16[4,40,256]{2,1,0:T(8,128)(2,1)S(1)}, u32[]{:S(2)}, u32[]{:S(2)}) %collective-permute-start.1) | collective-permute-done | bytes 81952 | tf_op jit(solution)/shard_map/ppermute | solution.py:296
  13.3 0.1 pad_maximum_fusion
  13.3 0.0 copy-start
  13.4 0.0 copy-start.2
  13.4 0.1 copy.9
  13.4 16.1 %all_to_all.20.tiles = bf16[16,40,384]{2,1,0:T(8,128)(2,1)S(1)} all-to-all(bf16[16,40,384]{2,1,0:T(8,128)(2,1)S(1)} %bitcast.18), channel_id=1, replica_groups=mesh['row'=16,'dev'=16] {'dev'}, dimensions={0} | all-to-all | bytes 983040 | tf_op jit(solution)/shard_map/all_to_all | solution.py:313
  29.6 0.0 copy-done.1
  29.6 0.0 copy-done.3
  29.6 4.3 %cut.1 = (bf16[16,40,640]{2,1,0:T(8,128)(2,1)}, bf16[16,40,640]{2,1,0:T(8,128)(2,1)S(1)}, s32[3,16]{1,0:T(4,128)S(1)}) custom-call(s32[1,16]{1,0:T(1,128)S(1)} %copy-done.1, s32[1,16]{1,0:T(1,128)S(1)} %copy-done.3, bf16[16,40,384]{2,1,0:T(8,128)(2,1)S(1)} %all_to_all.20.tiles), custom_call_target="tpu_custom_call" | custom-call | tf_op jit(solution)/shard_map/cut/pallas_call | solution.py:330
  33.9 3.6 %all-to-all-start.1 = ((bf16[16,40,640]{2,1,0:T(8,128)(2,1)}), bf16[16,40,640]{2,1,0:T(8,128)(2,1)S(1)}, u32[]{:S(2)}, u32[]{:S(2)}) async-start(bf16[16,40,640]{2,1,0:T(8,128)(2,1)} %get-tuple-element.13), calls=%async_computation.1 | async-start | bytes 1638400 | tf_op jit(solution)/shard_map/all_to_all | solution.py:313
  37.5 14.4 %all-to-all-done.1.parts = bf16[16,40,640]{2,1,0:T(8,128)(2,1)S(1)} async-done(((bf16[16,40,640]{2,1,0:T(8,128)(2,1)}), bf16[16,40,640]{2,1,0:T(8,128)(2,1)S(1)}, u32[]{:S(2)}, u32[]{:S(2)}) %all-to-all-start.1) | async-done | bytes 819232 | tf_op jit(solution)/shard_map/all_to_all | solution.py:313
  51.9 0.0 copy-done
  51.9 0.0 copy-done.2
  51.9 5.7 %solve.1 = (f32[2,3,40,2304]{3,2,1,0:T(8,128)}, bf16[16,40,896]{2,1,0:T(8,128)(2,1)S(1)}) custom-call(s32[1]{0:T(128)} %bitcast.6.me, s32[3,16]{1,0:T(4,128)S(1)} %get-tuple-element.12.table, s32[1,30]{1,0:T(1,128)S(1)} %bitcast.16, f32[16,30]{1,0:T(8,128)S(1)} %bitcast.14, bf16[16,40,640]{2,1,0:T(8,128)(2,1)S(1)} %all-to-all-done.1.parts, ...), custom_call_target="tpu_custom_call" | custom-call | tf_op jit(solution)/shard_map/solve/pallas_call | solution.py:340
  57.6 0.0 copy-start.4
  57.6 21.0 %all_to_all.21.back.parts = bf16[16,40,896]{2,1,0:T(8,128)(2,1)S(1)} all-to-all(bf16[16,40,896]{2,1,0:T(8,128)(2,1)S(1)} %get-tuple-element.15), channel_id=1, replica_groups=mesh['row'=16,'dev'=16] {'dev'}, dimensions={0} | all-to-all | bytes 2293760 | tf_op jit(solution)/shard_map/all_to_all | solution.py:313
  78.6 3.2 %scatter.1 = f32[16,40,128]{2,1,0:T(8,128)} custom-call(s32[1,16]{1,0:T(1,128)S(1)} %copy-done.1, s32[3,16]{1,0:T(4,128)S(1)} %get-tuple-element.12.table, bf16[16,40,896]{2,1,0:T(8,128)(2,1)S(1)} %all_to_all.21.back.parts), custom_call_target="tpu_custom_call" | custom-call | tf_op jit(solution)/shard_map/scatter/pallas_call | solution.py:350
  81.8 3.5 %all-to-all-start.3 = ((f32[16,40,128]{2,1,0:T(8,128)}), f32[16,40,128]{2,1,0:T(8,128)S(1)}, u32[]{:S(2)}, u32[]{:S(2)}) async-start(f32[16,40,128]{2,1,0:T(8,128)} %scatter.1), calls=%async_computation.3 | async-start | bytes 655360 | tf_op jit(solution)/shard_map/all_to_all | solution.py:313
  85.4 0.0 copy-done.4
  85.4 1.6 %second.1 = f32[2,3,40,2304]{3,2,1,0:T(8,128)} custom-call(s32[1]{0:T(128)} %bitcast.6.me, s32[3,16]{1,0:T(4,128)S(1)} %get-tuple-element.12.table, s32[1,30]{1,0:T(1,128)S(1)} %bitcast.17, f32[16,30]{1,0:T(8,128)S(1)} %bitcast.15, bf16[16,40,896]{2,1,0:T(8,128)(2,1)S(1)} %all_to_all.21.back.parts, ...), custom_call_target="tpu_custom_call", output_to_operand_aliasing={{}: (5, {})} | custom-call | flops 20000000 | bytes 4000000 | tf_op jit(solution)/shard_map/second/pallas_call | solution.py:358
  87.1 6.0 %all-to-all-done.3.sums = f32[16,40,128]{2,1,0:T(8,128)S(1)} async-done(((f32[16,40,128]{2,1,0:T(8,128)}), f32[16,40,128]{2,1,0:T(8,128)S(1)}, u32[]{:S(2)}, u32[]{:S(2)}) %all-to-all-start.3) | async-done | bytes 327712 | tf_op jit(solution)/shard_map/all_to_all | solution.py:313
  93.1 0.1 join.1
  93.2 7.3 %collective-permute-start.2 = (f32[40,256]{1,0:T(8,128)S(1)}, f32[40,256]{1,0:T(8,128)S(1)}, u32[]{:S(2)}, u32[]{:S(2)}) collective-permute-start(f32[40,256]{1,0:T(8,128)S(1)} %get-tuple-element.19), channel_id=1, source_target_pairs={{0,16},{16,32},{32,48},{48,64},{64,80},{80,96},{96,112},{112,128},... | collective-permute-start | bytes 122888 | tf_op jit(solution)/shard_map/ppermute | solution.py:296
  100.5 1.9 %collective-permute-start.3 = (f32[40,256]{1,0:T(8,128)S(1)}, f32[40,256]{1,0:T(8,128)S(1)}, u32[]{:S(2)}, u32[]{:S(2)}) collective-permute-start(f32[40,256]{1,0:T(8,128)S(1)} %get-tuple-element.20), channel_id=1, source_target_pairs={{16,0},{32,16},{48,32},{64,48},{80,64},{96,80},{112,96},{128,112},... | collective-permute-start | bytes 122888 | tf_op jit(solution)/shard_map/ppermute | solution.py:296
  102.5 0.0 collective-permute-done.2
  102.5 3.3 %collective-permute-done.3 = f32[40,256]{1,0:T(8,128)S(1)} collective-permute-done((f32[40,256]{1,0:T(8,128)S(1)}, f32[40,256]{1,0:T(8,128)S(1)}, u32[]{:S(2)}, u32[]{:S(2)}) %collective-permute-start.3) | collective-permute-done | bytes 40992 | tf_op jit(solution)/shard_map/ppermute | solution.py:296
  105.8 0.8 pad_add_fusion
  (8 shorter events, 0.2 us)
Async XLA Ops:
  2.5 7.0 %collective-permute-start = (bf16[4,40,256]{2,1,0:T(8,128)(2,1)S(1)}, bf16[4,40,256]{2,1,0:T(8,128)(2,1)S(1)}, u32[]{:S(2)}, u32[]{:S(2)}) collective-permute-start(bf16[4,40,256]{2,1,0:T(8,128)(2,1)S(1)} %get-tuple-element.22), channel_id=1, source_target_pairs={{0,16},{16,32},{32,48},{48,64},{64,80},{80,96},{96,112},{112,128},... | collective-permute-start | bytes 245768 | tf_op jit(solution)/shard_map/ppermute | solution.py:296
  7.5 22.1 %copy-start.1 = (s32[1,16]{1,0:T(1,128)S(1)}, s32[1,16]{1,0:T(1,128)}, u32[]{:S(2)}) copy-start(s32[1,16]{1,0:T(1,128)} %anchor.3) | copy-start | bytes 196
  7.5 22.1 %copy-start.3 = (s32[1,16]{1,0:T(1,128)S(1)}, s32[1,16]{1,0:T(1,128)}, u32[]{:S(2)}) copy-start(s32[1,16]{1,0:T(1,128)} %owner.1) | copy-start | bytes 196
  7.5 5.8 %collective-permute-start.1 = (bf16[4,40,256]{2,1,0:T(8,128)(2,1)S(1)}, bf16[4,40,256]{2,1,0:T(8,128)(2,1)S(1)}, u32[]{:S(2)}, u32[]{:S(2)}) collective-permute-start(bf16[4,40,256]{2,1,0:T(8,128)(2,1)S(1)} %get-tuple-element.23), channel_id=1, source_target_pairs={{16,0},{32,16},{48,32},{64,48},{80,64},{96,80},{112,96},{128,112},... | collective-permute-start | bytes 245768 | tf_op jit(solution)/shard_map/ppermute | solution.py:296
  13.3 38.6 %copy-start = (f32[1,16,30]{2,1,0:T(8,128)S(1)}, f32[1,16,30]{2,1,0:T(8,128)}, u32[]{:S(2)}) copy-start(f32[1,16,30]{2,1,0:T(8,128)} %param.11) | copy-start | bytes 5764
  13.4 38.6 %copy-start.2 = (s32[30]{0:T(128)S(1)}, s32[30]{0:T(128)}, u32[]{:S(2)}) copy-start(s32[30]{0:T(128)} %param.10) | copy-start | bytes 364
  33.9 18.0 %all-to-all-start.1 = ((bf16[16,40,640]{2,1,0:T(8,128)(2,1)}), bf16[16,40,640]{2,1,0:T(8,128)(2,1)S(1)}, u32[]{:S(2)}, u32[]{:S(2)}) async-start(bf16[16,40,640]{2,1,0:T(8,128)(2,1)} %get-tuple-element.13), calls=%async_computation.1 | async-start | bytes 1638400 | tf_op jit(solution)/shard_map/all_to_all | solution.py:313
  57.6 27.8 %copy-start.4 = (bf16[64,1024]{1,0:T(8,128)(2,1)S(1)}, bf16[64,1024]{1,0:T(8,128)(2,1)}, u32[]{:S(2)}) copy-start(bf16[64,1024]{1,0:T(8,128)(2,1)} %param.7) | copy-start | bytes 393220
  81.8 11.3 %all-to-all-start.3 = ((f32[16,40,128]{2,1,0:T(8,128)}), f32[16,40,128]{2,1,0:T(8,128)S(1)}, u32[]{:S(2)}, u32[]{:S(2)}) async-start(f32[16,40,128]{2,1,0:T(8,128)} %scatter.1), calls=%async_computation.3 | async-start | bytes 655360 | tf_op jit(solution)/shard_map/all_to_all | solution.py:313
  93.2 9.2 %collective-permute-start.2 = (f32[40,256]{1,0:T(8,128)S(1)}, f32[40,256]{1,0:T(8,128)S(1)}, u32[]{:S(2)}, u32[]{:S(2)}) collective-permute-start(f32[40,256]{1,0:T(8,128)S(1)} %get-tuple-element.19), channel_id=1, source_target_pairs={{0,16},{16,32},{32,48},{48,64},{64,80},{80,96},{96,112},{112,128},... | collective-permute-start | bytes 122888 | tf_op jit(solution)/shard_map/ppermute | solution.py:296
  100.5 5.3 %collective-permute-start.3 = (f32[40,256]{1,0:T(8,128)S(1)}, f32[40,256]{1,0:T(8,128)S(1)}, u32[]{:S(2)}, u32[]{:S(2)}) collective-permute-start(f32[40,256]{1,0:T(8,128)S(1)} %get-tuple-element.20), channel_id=1, source_target_pairs={{16,0},{32,16},{48,32},{64,48},{80,64},{96,80},{112,96},{128,112},... | collective-permute-start | bytes 122888 | tf_op jit(solution)/shard_map/ppermute | solution.py:296

commit v3 on v2

--- a/solution.py
+++ b/solution.py
@@ -24,7 +24,8 @@
 CUT = 640
 RROWS = 3
 BACK = 896
-UNROLL = 4
+DEPTH = 48
+UNROLL = 2
 LOG2E = 1.4426950408889634
 LN15 = 2.70805020110221
 
@@ -41,7 +42,7 @@
     return jnp.concatenate([mask] * (FZ // 8), 0)
 
 
-def assign(owner, table, seconds):
+def assign_kernel(owner, table, seconds):
     for e in range(N_DEV):
         table[0, e] = -1
         table[1, e] = -1
@@ -63,8 +64,34 @@
         n = n + (held < 0).astype(jnp.int32)
 
 
-def cut_kernel(anchor, owner, tiles, out, second, table, seconds):
-    assign(owner, table, seconds)
+def edge_kernel(primary, conductivity, first, last, held, sems):
+    width = first.shape[-1]
+    copies = []
+    for n, start in enumerate((0, conductivity.shape[-1] - width)):
+        at = slice(start, start + width)
+        copies.append(pltpu.make_async_copy(primary.at[:, :DEPTH, at], held.at[n, :3], sems.at[2 * n]))
+        copies.append(pltpu.make_async_copy(conductivity.at[:DEPTH, at], held.at[n, 3], sems.at[2 * n + 1]))
+    for copy in copies:
+        copy.start()
+    for copy in copies:
+        copy.wait()
+    first[...] = held[0, :, :FZ, :]
+    last[...] = held[1, :, :FZ, :]
+
+
+def tile_kernel(primary, conductivity, out, held, sems):
+    copies = [
+        pltpu.make_async_copy(primary.at[:, :DEPTH], held.at[:3], sems.at[0]),
+        pltpu.make_async_copy(conductivity.at[:DEPTH], held.at[3], sems.at[1]),
+    ]
+    for copy in copies:
+        copy.start()
+    for copy in copies:
+        copy.wait()
+    out[...] = held[:, :FZ, :]
+
+
+def cut_kernel(anchor, owner, table, tiles, out, second):
     row_in = lane_iota(8) // TX
     picks = []
     for v in range(5):
@@ -191,7 +218,9 @@
     lax.fori_loop(0, STEPS, step, 0)
 
 
-def solve_kernel(me, table, gates, misfit, parts, second, adjoint_out, back, window, lam, curl, local, x_masks, sem):
+def solve_kernel(me, table, gates, misfit, parts, second, lam_out, back_to, window, lam, curl, local, back, x_masks, sems):
+    windows = pltpu.make_async_copy(second.at[:, :, :512], back_to.at[:, :, :512], sems.at[0])
+    windows.start()
     f, own = table[0, me[0]], table[2, me[0]]
     adjoint(f, gates, misfit, parts, window, lam, curl, x_masks)
     for i in range(FZ // 8):
@@ -199,32 +228,36 @@
         total = None
         for c in range(3):
             v = lam[c, z, :]
-            lam[c, z, :] = jnp.where(own == 1, v, 0.0)
+            lam_out[c, z, :] = jnp.where(own == 1, v, 0.0)
             term = v * window[c, z, :]
             total = term if total is None else total + term
         local[z, :] = total
-    copy = pltpu.make_async_copy(lam.at[:, :FZ, :], adjoint_out.at[0], sem)
-    copy.start()
     lane = lane_iota(FZ)
+    copies = [windows]
     for j in range(N_DEV):
         a, r = 144 * j // 128, 144 * j % 128
         both = [local[:, 128 * (a + b) : 128 * (a + b) + 128] for b in range(2)]
         high = [v.astype(jnp.bfloat16).astype(jnp.float32) for v in both]
         rest = [turn(v - h, 80 - r) for v, h in zip(both, high)]
         high = [turn(h, 64 - r) for h in high]
-        back[j, :, :512] = second[j, :, :512]
         v4 = jnp.where(lane - 64 < 128 - r, high[0], high[1])
         v4 = jnp.where(lane < 64, second[j, :, 512:640].astype(jnp.float32), v4)
         v5 = jnp.where(lane + 64 < 128 - r, high[0], high[1])
         v5 = jnp.where(lane < 80, v5, jnp.where(lane - 80 < 128 - r, rest[0], rest[1]))
         v6 = jnp.where(lane + 48 < 128 - r, rest[0], rest[1])
         for b, v in enumerate((v4, v5, v6)):
-            back[j, :, 512 + 128 * b : 640 + 128 * b] = v.astype(jnp.bfloat16)
-    copy.wait()
-
-
-def second_kernel(me, table, gates, misfit, parts, adjoint_in, adjoint_out, window, lam, curl, x_masks, sem):
-    del adjoint_in
+            back[j, :, 128 * b : 128 * b + 128] = v.astype(jnp.bfloat16)
+        if j % 4 == 3:
+            some = slice(j - 3, j + 1)
+            copies.append(pltpu.make_async_copy(back.at[some], back_to.at[some, :, 512:], sems.at[1 + j // 4]))
+            copies[-1].start()
+    for copy in copies:
+        copy.wait()
+
+
+def second_kernel(me, table, gates, misfit, parts, own, adjoint_out, window, lam, curl, x_masks, sems):
+    first = pltpu.make_async_copy(own, adjoint_out.at[0], sems.at[0])
+    first.start()
     f = table[1, me[0]]
 
     @pl.when(f >= 0)
@@ -235,9 +268,17 @@
     def _():
         lam[:, :FZ, :] = jnp.zeros((3, FZ, LANES), jnp.float32)
 
-    copy = pltpu.make_async_copy(lam.at[:, :FZ, :], adjoint_out.at[1], sem)
+    copy = pltpu.make_async_copy(lam.at[:, :FZ, :], adjoint_out.at[1], sems.at[1])
     copy.start()
     copy.wait()
+    first.wait()
+
+
+def regularize_kernel(conductivity, out):
+    logs = jnp.log(conductivity[...].astype(jnp.float32))
+    delta = logs[1:] - logs[:-1]
+    zero_row = jnp.zeros_like(logs[:1])
+    out[...] = jnp.concatenate([zero_row, delta], 0) - jnp.concatenate([delta, zero_row], 0)
 
 
 def scatter_kernel(anchor, table, back, out):
@@ -282,13 +323,6 @@
         own[:, 128 * n : 128 * n + 128] = made[2 + n]
 
 
-def regularize(conductivity):
-    logs = jnp.log(conductivity.astype(jnp.float32))
-    delta = logs[1:] - logs[:-1]
-    zero_row = jnp.zeros_like(logs[:1])
-    return jnp.concatenate([zero_row, delta], 0) - jnp.concatenate([delta, zero_row], 0)
-
-
 def neighbours(first, last, axis):
     peers = lax.axis_size(axis)
     up = [(i, i + 1) for i in range(peers - 1)]
@@ -299,8 +333,10 @@
 SMEM = pl.BlockSpec(memory_space=pltpu.SMEM)
 VMEM = pl.BlockSpec(memory_space=pltpu.VMEM)
 ANY = pl.BlockSpec(memory_space=pl.ANY)
-PARAMS = pltpu.CompilerParams(vmem_limit_bytes=40 * 2**20)
+PARAMS = pltpu.CompilerParams(vmem_limit_bytes=24 * 2**20)
 F32 = jnp.float32
+WIDE = 60 * 2**20
+SMALL = pl.CostEstimate(flops=10**6, bytes_accessed=10**6, transcendentals=10**5)
 WORK = [
     pltpu.VMEM((4, FZ, LANES), F32),
     pltpu.VMEM((3, FZ + 8, LANES), F32),
@@ -316,37 +352,83 @@
 def per_device(primary, conductivity, anchor_x, owner, gate_index, misfit):
     me = lax.axis_index("dev").astype(jnp.int32).reshape(1)
     gates, residues = gate_index.reshape(1, GATES), misfit[0]
-    tile = jnp.concatenate([primary[:, :FZ], conductivity[None, :FZ]], axis=0)
     halo = HALO * TX
-    before, after = neighbours(tile[..., :halo], tile[..., -halo:], "row")
+    half = jax.ShapeDtypeStruct((4, FZ, halo), jnp.bfloat16)
+    first, last = pl.pallas_call(
+        edge_kernel,
+        out_shape=(half, half),
+        in_specs=[ANY, ANY],
+        out_specs=(VMEM, VMEM),
+        scratch_shapes=[pltpu.VMEM((2, 4, DEPTH, halo), jnp.bfloat16), pltpu.SemaphoreType.DMA((4,))],
+        compiler_params=pltpu.CompilerParams(vmem_limit_bytes=WIDE),
+        name="edges",
+    )(primary, conductivity)
+    before, after = neighbours(first, last, "row")
+    tile = pl.pallas_call(
+        tile_kernel,
+        out_shape=jax.ShapeDtypeStruct((4, FZ, TX * TY), jnp.bfloat16),
+        in_specs=[ANY, ANY],
+        out_specs=VMEM,
+        scratch_shapes=[pltpu.VMEM((4, DEPTH, TX * TY), jnp.bfloat16), pltpu.SemaphoreType.DMA((2,))],
+        compiler_params=PARAMS,
+        cost_estimate=SMALL,
+        name="tile",
+    )(primary, conductivity)
     chunks = [
         jnp.concatenate([before, tile[..., : QIN - halo]], -1),
         tile[..., QIN - halo : 2 * QIN - halo],
         tile[..., 2 * QIN - halo : 3 * QIN - halo],
         jnp.concatenate([tile[..., 3 * QIN - halo :], after], -1),
     ]
-    spread = exchange(jnp.stack(chunks, 1).reshape(N_DEV, FZ, QIN))
+    spread, owner = lax.optimization_barrier((jnp.stack(chunks, 1).reshape(N_DEV, FZ, QIN), owner))
+    table = pl.pallas_call(
+        assign_kernel,
+        out_shape=jax.ShapeDtypeStruct((3, N_DEV), jnp.int32),
+        in_specs=[SMEM],
+        out_specs=SMEM,
+        scratch_shapes=[pltpu.SMEM((N_DEV + 1,), jnp.int32)],
+        compiler_params=PARAMS,
+        cost_estimate=SMALL,
+        name="assign",
+    )(owner)
     cut_shape = jax.ShapeDtypeStruct((N_DEV, FZ, CUT), jnp.bfloat16)
-    windows, second, table = pl.pallas_call(
+    windows, second = pl.pallas_call(
         cut_kernel,
-        out_shape=(cut_shape, cut_shape, jax.ShapeDtypeStruct((3, N_DEV), jnp.int32)),
-        in_specs=[SMEM, SMEM, VMEM],
-        out_specs=(VMEM, VMEM, SMEM),
-        scratch_shapes=[pltpu.SMEM((N_DEV + 1,), jnp.int32)],
+        out_shape=(cut_shape, cut_shape),
+        in_specs=[SMEM, SMEM, SMEM, VMEM],
+        out_specs=(VMEM, VMEM),
         compiler_params=PARAMS,
         name="cut",
-    )(anchor_x, owner, spread)
-    adjoint_shape = jax.ShapeDtypeStruct((MOST, 3, FZ, LANES), F32)
-    field, back = pl.pallas_call(
+    )(anchor_x, owner, table, exchange(spread))
+    lam, back = pl.pallas_call(
         solve_kernel,
-        out_shape=(adjoint_shape, jax.ShapeDtypeStruct((N_DEV, FZ, BACK), jnp.bfloat16)),
+        out_shape=(
+            jax.ShapeDtypeStruct((3, FZ, LANES), F32),
+            jax.ShapeDtypeStruct((N_DEV, FZ, BACK), jnp.bfloat16),
+        ),
         in_specs=[SMEM, SMEM, VMEM, VMEM, VMEM, VMEM],
-        out_specs=(ANY, VMEM),
-        scratch_shapes=[*WORK, pltpu.VMEM((FZ, LANES), F32), MASKS, pltpu.SemaphoreType.DMA],
+        out_specs=(VMEM, ANY),
+        scratch_shapes=[
+            *WORK,
+            pltpu.VMEM((FZ, LANES), F32),
+            pltpu.VMEM((N_DEV, FZ, BACK - 512), jnp.bfloat16),
+            MASKS,
+            pltpu.SemaphoreType.DMA((5,)),
+        ],
         compiler_params=PARAMS,
         name="solve",
     )(me, table, gates, residues, exchange(windows), second)
-    back = exchange(back)
+    back, layers = lax.optimization_barrier((back, conductivity))
+    smooth = pl.pallas_call(
+        regularize_kernel,
+        out_shape=jax.ShapeDtypeStruct(conductivity.shape, F32),
+        in_specs=[VMEM],
+        out_specs=VMEM,
+        compiler_params=PARAMS,
+        cost_estimate=SMALL,
+        name="regularize",
+    )(layers)
+    back, smooth = lax.optimization_barrier((exchange(back), smooth))
     columns = pl.pallas_call(
         scatter_kernel,
         out_shape=jax.ShapeDtypeStruct((N_DEV, FZ, 128), F32),
@@ -357,15 +439,14 @@
     )(anchor_x, table, back)
     adjoint_field = pl.pallas_call(
         second_kernel,
-        out_shape=adjoint_shape,
+        out_shape=jax.ShapeDtypeStruct((MOST, 3, FZ, LANES), F32),
         in_specs=[SMEM, SMEM, VMEM, VMEM, VMEM, ANY],
         out_specs=ANY,
-        scratch_shapes=[*WORK, MASKS, pltpu.SemaphoreType.DMA],
-        input_output_aliases={5: 0},
+        scratch_shapes=[*WORK, MASKS, pltpu.SemaphoreType.DMA((2,))],
         compiler_params=PARAMS,
         cost_estimate=pl.CostEstimate(flops=2 * 10**7, bytes_accessed=4 * 10**6, transcendentals=3 * 10**6),
         name="second",
-    )(me, table, gates, residues, back, field)
+    )(me, table, gates, residues, back, lam)
     sums, adjoint_field = lax.optimization_barrier((exchange(columns), adjoint_field))
     half = jax.ShapeDtypeStruct((FZ, halo), F32)
     first, own, last = pl.pallas_call(
@@ -379,8 +460,7 @@
     from_before, from_after = neighbours(first, last, "row")
     data = own + jnp.pad(from_before, ((0, 0), (0, TX * TY - halo)))
     data = data + jnp.pad(from_after, ((0, 0), (TX * TY - halo, 0)))
-    gradient = regularize(conductivity)
-    gradient = gradient + jnp.pad(data, ((0, gradient.shape[0] - FZ), (0, 0)))
+    gradient = smooth + jnp.pad(data, ((0, smooth.shape[0] - FZ), (0, 0)))
     return gradient, adjoint_field
 
 

time: 107 us -> 108 us (level)
  blocking collectives: 37.2 us -> 0 us
  waiting for transfers between devices: 27.5 us -> 52.9 us
  starting transfers between devices: 23.2 us -> 32.1 us
  Pallas kernels: 15 us -> 18.1 us
    all_to_all x2 -> x0, blocking collectives: 37.2 us -> none  [exchange(): return lax.all_to_all(blocks, 'dev', 0, 0, tiled=True)]
    all_to_all x2 -> x4, waiting for transfers between devices: 20.4 us -> 47.7 us  [exchange(): return lax.all_to_all(blocks, 'dev', 0, 0, tiled=True)]
    all_to_all x2 -> x4, starting transfers between devices: 7.17 us -> 17.8 us  [exchange(): return lax.all_to_all(blocks, 'dev', 0, 0, tiled=True)]
    pallas_call x3 -> x7, Pallas kernels: 11.6 us -> 14.8 us  [the longest x1 5.43 us: per_device(): pl.pallas_call(solve_kernel, out_shape=(jax.ShapeDtypeStruct((3, FZ, LANE...]
    unnamed x10 -> x14, local copies, waits for them, and re-layouts: 0.03 us -> 1.93 us
    ppermute x4, waiting for transfers between devices: 7.08 us -> 5.24 us  [neighbours(): return (lax.ppermute(last, axis, up), lax.ppermute(first, axis, down))]
    ppermute x4, starting transfers between devices: 16 us -> 14.4 us  [neighbours(): return (lax.ppermute(last, axis, up), lax.ppermute(first, axis, down))]
  transfers between devices with their start and end apart: 6 -> 8, of which waited for: 4 -> 6; matrix products, arithmetic and copies ran while one was open for 0% -> 0% of each run, Pallas kernels for 2% -> 3%
where the time goes in v3:
time: 108 us
  waiting for transfers between devices  52.9 us (49%)
  starting transfers between devices  32.1 us (30%)
  Pallas kernels  18.1 us (17%)
  local copies, waits for them, and re-layouts  2.8 us (3%)
    all_to_all x4, waiting for transfers between devices, exchange(): return lax.all_to_all(blocks, 'dev', 0, 0, tiled=True)  47.7 us
    all_to_all x4, starting transfers between devices, exchange(): return lax.all_to_all(blocks, 'dev', 0, 0, tiled=True)  17.8 us
    ppermute x4, starting transfers between devices, neighbours(): return (lax.ppermute(last, axis, up), lax.ppermute(first, axis, down))  14.4 us
    pallas_call x1, Pallas kernels, per_device(): pl.pallas_call(solve_kernel, out_shape=(jax.ShapeDtypeStruct((3, FZ, LANE...  5.43 us
    ppermute x4, waiting for transfers between devices, neighbours(): return (lax.ppermute(last, axis, up), lax.ppermute(first, axis, down))  5.24 us
    pallas_call x1, Pallas kernels, per_device(): pl.pallas_call(cut_kernel, out_shape=(cut_shape, cut_shape), in_specs=[SM...  4.16 us
    pallas_call x1, Pallas kernels, per_device(): pl.pallas_call(scatter_kernel, out_shape=jax.ShapeDtypeStruct((N_DEV, FZ,...  3.23 us
  transfers between devices with their start and end apart: 8, of which 6 were waited for; matrix products, arithmetic and copies ran while one was open for 0% of the time, Pallas kernels for 3%

profile of v3, /device:TPU:1, one launch (start us, length us, event | category | flops | bytes accessed | tf_op | source)
XLA Modules:
  0.0 107.7 jit_solution(9081890409460537441)
XLA Ops:
  0.6 1.7 %edges.1 = (bf16[4,40,256]{2,1,0:T(8,128)(2,1)}, bf16[4,40,256]{2,1,0:T(8,128)(2,1)}) custom-call(bf16[3,64,1024]{2,1,0:T(8,128)(2,1)} %primary.3, bf16[64,1024]{1,0:T(8,128)(2,1)} %conductivity.4), custom_call_target="tpu_custom_call" | custom-call | tf_op jit(solution)/shard_map/edges/pallas_call | solution.py:357
  2.3 4.9 %collective-permute-start = (bf16[4,40,256]{2,1,0:T(8,128)(2,1)}, bf16[4,40,256]{2,1,0:T(8,128)(2,1)S(1)}, u32[]{:S(2)}, u32[]{:S(2)}) collective-permute-start(bf16[4,40,256]{2,1,0:T(8,128)(2,1)} %get-tuple-element.19), channel_id=1, source_target_pairs={{0,16},{16,32},{32,48},{48,64},{64,80},{80,96},{96,112},{112,128},... | collective-permute-start | bytes 245768 | tf_op jit(solution)/shard_map/ppermute | solution.py:330
  7.2 1.9 %collective-permute-start.1 = (bf16[4,40,256]{2,1,0:T(8,128)(2,1)}, bf16[4,40,256]{2,1,0:T(8,128)(2,1)S(1)}, u32[]{:S(2)}, u32[]{:S(2)}) collective-permute-start(bf16[4,40,256]{2,1,0:T(8,128)(2,1)} %get-tuple-element.20), channel_id=1, source_target_pairs={{16,0},{32,16},{48,32},{64,48},{80,64},{96,80},{112,96},{128,112},... | collective-permute-start | bytes 245768 | tf_op jit(solution)/shard_map/ppermute | solution.py:330
  9.2 0.0 copy-start
  9.2 1.0 copy-done
  10.2 0.0 copy-start.1
  10.2 0.9 copy-done.1
  11.1 0.2 tile.1
  11.3 0.0 collective-permute-done
  11.3 1.9 %collective-permute-done.1 = bf16[4,40,256]{2,1,0:T(8,128)(2,1)S(1)} collective-permute-done((bf16[4,40,256]{2,1,0:T(8,128)(2,1)}, bf16[4,40,256]{2,1,0:T(8,128)(2,1)S(1)}, u32[]{:S(2)}, u32[]{:S(2)}) %collective-permute-start.1) | collective-permute-done | bytes 81952 | tf_op jit(solution)/shard_map/ppermute | solution.py:330
  13.2 0.1 pad_maximum_fusion
  13.3 0.0 copy-start.6
  13.3 0.0 copy-start.4
  13.3 0.8 copy.8
  14.2 6.8 %all-to-all-start = ((bf16[16,40,384]{2,1,0:T(8,128)(2,1)}), bf16[16,40,384]{2,1,0:T(8,128)(2,1)S(1)}, u32[]{:S(2)}, u32[]{:S(2)}) async-start(bf16[16,40,384]{2,1,0:T(8,128)(2,1)} %bitcast.5), calls=%async_computation | async-start | bytes 983040 | tf_op jit(solution)/shard_map/all_to_all | solution.py:349
  20.9 0.0 copy-done.6
  20.9 0.0 copy-start.3
  20.9 0.0 copy-start.5
  21.0 1.4 %assign.1.table = s32[3,16]{1,0:T(4,128)S(1)} custom-call(s32[1,16]{1,0:T(1,128)S(1)} %copy-done.6), custom_call_target="tpu_custom_call" | custom-call | flops 1000000 | bytes 1000000 | tf_op jit(solution)/shard_map/assign/pallas_call | solution.py:384
  22.3 8.2 %all-to-all-done.tiles = bf16[16,40,384]{2,1,0:T(8,128)(2,1)S(1)} async-done(((bf16[16,40,384]{2,1,0:T(8,128)(2,1)}), bf16[16,40,384]{2,1,0:T(8,128)(2,1)S(1)}, u32[]{:S(2)}, u32[]{:S(2)}) %all-to-all-start) | async-done | bytes 491552 | tf_op jit(solution)/shard_map/all_to_all | solution.py:349
  30.5 0.0 copy-done.4
  30.5 4.2 %cut.1 = (bf16[16,40,640]{2,1,0:T(8,128)(2,1)}, bf16[16,40,640]{2,1,0:T(8,128)(2,1)S(1)}) custom-call(s32[1,16]{1,0:T(1,128)S(1)} %copy-done.4, s32[1,16]{1,0:T(1,128)S(1)} %copy-done.6, s32[3,16]{1,0:T(4,128)S(1)} %assign.1.table, bf16[16,40,384]{2,1,0:T(8,128)(2,1)S(1)} %all-to-all-done.tiles), custom_call_target="tpu_custom_call" | custom-call | tf_op jit(solution)/shard_map/cut/pallas_call | solution.py:395
  34.7 3.6 %all-to-all-start.1 = ((bf16[16,40,640]{2,1,0:T(8,128)(2,1)}), bf16[16,40,640]{2,1,0:T(8,128)(2,1)S(1)}, u32[]{:S(2)}, u32[]{:S(2)}) async-start(bf16[16,40,640]{2,1,0:T(8,128)(2,1)} %get-tuple-element.23), calls=%async_computation.1 | async-start | bytes 1638400 | tf_op jit(solution)/shard_map/all_to_all | solution.py:349
  38.3 14.4 %all-to-all-done.1.parts = bf16[16,40,640]{2,1,0:T(8,128)(2,1)S(1)} async-done(((bf16[16,40,640]{2,1,0:T(8,128)(2,1)}), bf16[16,40,640]{2,1,0:T(8,128)(2,1)S(1)}, u32[]{:S(2)}, u32[]{:S(2)}) %all-to-all-start.1) | async-done | bytes 819232 | tf_op jit(solution)/shard_map/all_to_all | solution.py:349
  52.7 0.0 copy-done.3
  52.7 0.0 copy-done.5
  52.7 5.4 %solve.1 = (f32[3,40,2304]{2,1,0:T(8,128)S(1)}, bf16[16,40,896]{2,1,0:T(8,128)(2,1)}) custom-call(s32[1]{0:T(128)} %bitcast.me, s32[3,16]{1,0:T(4,128)S(1)} %assign.1.table, s32[1,30]{1,0:T(1,128)S(1)} %bitcast.14, f32[16,30]{1,0:T(8,128)S(1)} %bitcast.12, bf16[16,40,640]{2,1,0:T(8,128)(2,1)S(1)} %all-to-all-done.1.parts, ...), custom_call_target="tpu_custom_call" | custom-call | tf_op jit(solution)/shard_map/solve/pallas_call | solution.py:403
  58.1 0.0 copy-start.2
  58.1 3.8 %all-to-all-start.2 = ((bf16[16,40,896]{2,1,0:T(8,128)(2,1)}), bf16[16,40,896]{2,1,0:T(8,128)(2,1)S(1)}, u32[]{:S(2)}, u32[]{:S(2)}) async-start(bf16[16,40,896]{2,1,0:T(8,128)(2,1)} %get-tuple-element.26), calls=%async_computation.2 | async-start | bytes 2293760 | tf_op jit(solution)/shard_map/all_to_all | solution.py:349
  62.0 0.0 copy-done.2
  62.0 0.1 regularize.1
  62.1 19.3 %all-to-all-done.2.back.parts = bf16[16,40,896]{2,1,0:T(8,128)(2,1)S(1)} async-done(((bf16[16,40,896]{2,1,0:T(8,128)(2,1)}), bf16[16,40,896]{2,1,0:T(8,128)(2,1)S(1)}, u32[]{:S(2)}, u32[]{:S(2)}) %all-to-all-start.2) | async-done | bytes 1146912 | tf_op jit(solution)/shard_map/all_to_all | solution.py:349
  81.4 3.2 %scatter.1 = f32[16,40,128]{2,1,0:T(8,128)} custom-call(s32[1,16]{1,0:T(1,128)S(1)} %copy-done.4, s32[3,16]{1,0:T(4,128)S(1)} %assign.1.table, bf16[16,40,896]{2,1,0:T(8,128)(2,1)S(1)} %all-to-all-done.2.back.parts), custom_call_target="tpu_custom_call" | custom-call | tf_op jit(solution)/shard_map/scatter/pallas_call | solution.py:432
  84.6 3.5 %all-to-all-start.3 = ((f32[16,40,128]{2,1,0:T(8,128)}), f32[16,40,128]{2,1,0:T(8,128)S(1)}, u32[]{:S(2)}, u32[]{:S(2)}) async-start(f32[16,40,128]{2,1,0:T(8,128)} %scatter.1), calls=%async_computation.3 | async-start | bytes 655360 | tf_op jit(solution)/shard_map/all_to_all | solution.py:349
  88.2 1.9 %second.1 = f32[2,3,40,2304]{3,2,1,0:T(8,128)} custom-call(s32[1]{0:T(128)} %bitcast.me, s32[3,16]{1,0:T(4,128)S(1)} %assign.1.table, s32[1,30]{1,0:T(1,128)S(1)} %bitcast.15, f32[16,30]{1,0:T(8,128)S(1)} %bitcast.13, bf16[16,40,896]{2,1,0:T(8,128)(2,1)S(1)} %all-to-all-done.2.back.parts, f32[3,40,2304]{2,1,0:T(8,128)S(1)} %get-tuple-element.30.own), custom_call_target="tpu_custom_call" | custom-call | flops 20000000 | bytes 4000000 | tf_op jit(solution)/shard_map/second/pallas_call | solution.py:440
  90.1 5.8 %all-to-all-done.3.sums = f32[16,40,128]{2,1,0:T(8,128)S(1)} async-done(((f32[16,40,128]{2,1,0:T(8,128)}), f32[16,40,128]{2,1,0:T(8,128)S(1)}, u32[]{:S(2)}, u32[]{:S(2)}) %all-to-all-start.3) | async-done | bytes 327712 | tf_op jit(solution)/shard_map/all_to_all | solution.py:349
  95.9 0.1 join.1
  96.0 5.6 %collective-permute-start.2 = (f32[40,256]{1,0:T(8,128)S(1)}, f32[40,256]{1,0:T(8,128)S(1)}, u32[]{:S(2)}, u32[]{:S(2)}) collective-permute-start(f32[40,256]{1,0:T(8,128)S(1)} %get-tuple-element.33), channel_id=1, source_target_pairs={{0,16},{16,32},{32,48},{48,64},{64,80},{80,96},{96,112},{112,128},... | collective-permute-start | bytes 122888 | tf_op jit(solution)/shard_map/ppermute | solution.py:330
  101.7 1.9 %collective-permute-start.3 = (f32[40,256]{1,0:T(8,128)S(1)}, f32[40,256]{1,0:T(8,128)S(1)}, u32[]{:S(2)}, u32[]{:S(2)}) collective-permute-start(f32[40,256]{1,0:T(8,128)S(1)} %get-tuple-element.34), channel_id=1, source_target_pairs={{16,0},{32,16},{48,32},{64,48},{80,64},{96,80},{112,96},{128,112},... | collective-permute-start | bytes 122888 | tf_op jit(solution)/shard_map/ppermute | solution.py:330
  103.6 0.0 collective-permute-done.2
  103.6 3.4 %collective-permute-done.3 = f32[40,256]{1,0:T(8,128)S(1)} collective-permute-done((f32[40,256]{1,0:T(8,128)S(1)}, f32[40,256]{1,0:T(8,128)S(1)}, u32[]{:S(2)}, u32[]{:S(2)}) %collective-permute-start.3) | collective-permute-done | bytes 40992 | tf_op jit(solution)/shard_map/ppermute | solution.py:330
  107.0 0.7 pad_add_fusion
  (5 shorter events, 0.1 us)
Async XLA Ops:
  2.3 9.0 %collective-permute-start = (bf16[4,40,256]{2,1,0:T(8,128)(2,1)}, bf16[4,40,256]{2,1,0:T(8,128)(2,1)S(1)}, u32[]{:S(2)}, u32[]{:S(2)}) collective-permute-start(bf16[4,40,256]{2,1,0:T(8,128)(2,1)} %get-tuple-element.19), channel_id=1, source_target_pairs={{0,16},{16,32},{32,48},{48,64},{64,80},{80,96},{96,112},{112,128},... | collective-permute-start | bytes 245768 | tf_op jit(solution)/shard_map/ppermute | solution.py:330
  7.2 6.0 %collective-permute-start.1 = (bf16[4,40,256]{2,1,0:T(8,128)(2,1)}, bf16[4,40,256]{2,1,0:T(8,128)(2,1)S(1)}, u32[]{:S(2)}, u32[]{:S(2)}) collective-permute-start(bf16[4,40,256]{2,1,0:T(8,128)(2,1)} %get-tuple-element.20), channel_id=1, source_target_pairs={{16,0},{32,16},{48,32},{64,48},{80,64},{96,80},{112,96},{128,112},... | collective-permute-start | bytes 245768 | tf_op jit(solution)/shard_map/ppermute | solution.py:330
  9.2 1.0 copy-start
  10.2 0.9 copy-start.1
  13.3 7.6 %copy-start.6 = (s32[1,16]{1,0:T(1,128)S(1)}, s32[1,16]{1,0:T(1,128)}, u32[]{:S(2)}) copy-start(s32[1,16]{1,0:T(1,128)} %owner.1) | copy-start | bytes 196
  13.3 17.2 %copy-start.4 = (s32[1,16]{1,0:T(1,128)S(1)}, s32[1,16]{1,0:T(1,128)}, u32[]{:S(2)}) copy-start(s32[1,16]{1,0:T(1,128)} %anchor.3) | copy-start | bytes 196
  14.2 16.3 %all-to-all-start = ((bf16[16,40,384]{2,1,0:T(8,128)(2,1)}), bf16[16,40,384]{2,1,0:T(8,128)(2,1)S(1)}, u32[]{:S(2)}, u32[]{:S(2)}) async-start(bf16[16,40,384]{2,1,0:T(8,128)(2,1)} %bitcast.5), calls=%async_computation | async-start | bytes 983040 | tf_op jit(solution)/shard_map/all_to_all | solution.py:349
  20.9 31.8 %copy-start.3 = (f32[1,16,30]{2,1,0:T(8,128)S(1)}, f32[1,16,30]{2,1,0:T(8,128)}, u32[]{:S(2)}) copy-start(f32[1,16,30]{2,1,0:T(8,128)} %param.11) | copy-start | bytes 5764
  20.9 31.7 %copy-start.5 = (s32[30]{0:T(128)S(1)}, s32[30]{0:T(128)}, u32[]{:S(2)}) copy-start(s32[30]{0:T(128)} %param.10) | copy-start | bytes 364
  34.7 18.0 %all-to-all-start.1 = ((bf16[16,40,640]{2,1,0:T(8,128)(2,1)}), bf16[16,40,640]{2,1,0:T(8,128)(2,1)S(1)}, u32[]{:S(2)}, u32[]{:S(2)}) async-start(bf16[16,40,640]{2,1,0:T(8,128)(2,1)} %get-tuple-element.23), calls=%async_computation.1 | async-start | bytes 1638400 | tf_op jit(solution)/shard_map/all_to_all | solution.py:349
  58.1 3.9 %copy-start.2 = (bf16[64,1024]{1,0:T(8,128)(2,1)S(1)}, bf16[64,1024]{1,0:T(8,128)(2,1)}, u32[]{:S(2)}) copy-start(bf16[64,1024]{1,0:T(8,128)(2,1)} %conductivity.4) | copy-start | bytes 393220
  58.1 23.3 %all-to-all-start.2 = ((bf16[16,40,896]{2,1,0:T(8,128)(2,1)}), bf16[16,40,896]{2,1,0:T(8,128)(2,1)S(1)}, u32[]{:S(2)}, u32[]{:S(2)}) async-start(bf16[16,40,896]{2,1,0:T(8,128)(2,1)} %get-tuple-element.26), calls=%async_computation.2 | async-start | bytes 2293760 | tf_op jit(solution)/shard_map/all_to_all | solution.py:349
  84.6 11.3 %all-to-all-start.3 = ((f32[16,40,128]{2,1,0:T(8,128)}), f32[16,40,128]{2,1,0:T(8,128)S(1)}, u32[]{:S(2)}, u32[]{:S(2)}) async-start(f32[16,40,128]{2,1,0:T(8,128)} %scatter.1), calls=%async_computation.3 | async-start | bytes 655360 | tf_op jit(solution)/shard_map/all_to_all | solution.py:349
  96.0 7.5 %collective-permute-start.2 = (f32[40,256]{1,0:T(8,128)S(1)}, f32[40,256]{1,0:T(8,128)S(1)}, u32[]{:S(2)}, u32[]{:S(2)}) collective-permute-start(f32[40,256]{1,0:T(8,128)S(1)} %get-tuple-element.33), channel_id=1, source_target_pairs={{0,16},{16,32},{32,48},{48,64},{64,80},{80,96},{96,112},{112,128},... | collective-permute-start | bytes 122888 | tf_op jit(solution)/shard_map/ppermute | solution.py:330
  101.7 5.3 %collective-permute-start.3 = (f32[40,256]{1,0:T(8,128)S(1)}, f32[40,256]{1,0:T(8,128)S(1)}, u32[]{:S(2)}, u32[]{:S(2)}) collective-permute-start(f32[40,256]{1,0:T(8,128)S(1)} %get-tuple-element.34), channel_id=1, source_target_pairs={{16,0},{32,16},{48,32},{64,48},{80,64},{96,80},{112,96},{128,112},... | collective-permute-start | bytes 122888 | tf_op jit(solution)/shard_map/ppermute | solution.py:330

commit v4 on v3

v4 whole, which is shorter than its diff:
```python
import jax
import jax.numpy as jnp
from jax import lax
from jax.experimental import pallas as pl
from jax.experimental.pallas import tpu as pltpu
from jax.sharding import PartitionSpec as P

TX = 32
TY = 32
FZ = 40
FP = 48
GATES = 30
NTIMES = 64
STEPS = 2
MOST = 2
FOOT_ROW = 16
HALO = 8
N_DEV = 16
STEP = 0.05

LANES = FP * FP
OWN_ROWS = 8
QIN = 384
CUT = 640
BACK = 896
DEPTH = 48
UNROLL = 8
CUT_UNROLL = 8
LOG2E = 1.4426950408889634
LN15 = 2.70805020110221


def turn(v, by):
    return pltpu.roll(v, by % 128, 1)


def lane_iota(rows):
    return lax.broadcasted_iota(jnp.int32, (rows, 128), 1)


def tall(mask):
    return jnp.concatenate([mask] * (FZ // 8), 0)


def assign(owner, table, seconds):
    for e in range(N_DEV):
        table[0, e] = -1
        table[1, e] = -1
    for f in range(FOOT_ROW):
        e = owner[0, f]
        held, other = table[0, e], table[1, e]
        table[0, e] = jnp.where(held >= 0, held, f)
        table[1, e] = jnp.where(held >= 0, f, other)
    n = jnp.int32(0)
    for e in range(N_DEV):
        other = table[1, e]
        seconds[n] = other
        n = n + (other >= 0).astype(jnp.int32)
    n = jnp.int32(0)
    for e in range(N_DEV):
        held = table[0, e]
        table[2, e] = (held >= 0).astype(jnp.int32)
        table[0, e] = jnp.where(held >= 0, held, seconds[n])
        n = n + (held < 0).astype(jnp.int32)


def tile_kernel(primary, conductivity, out, held, sems):
    copies = [
        pltpu.make_async_copy(primary.at[:, :DEPTH], held.at[:3], sems.at[0]),
        pltpu.make_async_copy(conductivity.at[:DEPTH], held.at[3], sems.at[1]),
    ]
    for copy in copies:
        copy.start()
    for copy in copies:
        copy.wait()
    for c in range(4):
        for q, start in enumerate((768, 896, 0, 128)):
            out[4 * c + q, :, :256] = held[c, :FZ, 256 * q : 256 * q + 256]
            out[4 * c + q, :, 256:] = held[c, :FZ, start : start + 128]


def cut_rows(tiles, o, count):
    d0, s = o // TX, o % TX
    row_in = lane_iota(8) // TX
    made, codes = [], []
    for v in range(-(-FP * count // 128)):
        at = lane_iota(8) + 128 * v
        y = sum((at >= FP * j).astype(jnp.int32) for j in range(1, count + 1))
        codes.append(8 * (y // 4) + y % 4 + 2 * lax.shift_right_logical(at - FP * y + s, 5))
        made.append(jnp.zeros((FZ, 128), jnp.float32))
    for m in range(count // 4):
        tile = [tiles(jnp.minimum(d0 + t, N_DEV - 1), m).astype(jnp.float32) for t in range(3)]
        for n in range(8):
            from_t = [t for t in range(3) if 0 <= n - 2 * t < 4]
            src = tile[from_t[0]]
            for t in from_t[1:]:
                src = jnp.where(tall(row_in == n - 2 * t), tile[t], src)
            turned = turn(src, 192 * m + 16 * n - s)
            rows = [(192 * m + FP * (n - 2 * t), t) for t in from_t]
            for v in range(len(made)):
                if any(
                    at + max(0, TX * t - 31) < 128 * (v + 1) and at + min(FP, TX * (t + 1)) > 128 * v for at, t in rows
                ):
                    made[v] = jnp.where(tall(codes[v] == 8 * m + n), turned, made[v])
    return [v.astype(jnp.bfloat16) for v in made]


def cut_own_kernel(anchor, owner, tiles, out, table, seconds):
    assign(owner, table, seconds)

    def one(e, carry):
        o = anchor[0, table[0, e]]
        made = cut_rows(lambda d, m: tiles[d, :, 128 * m : 128 * m + 128], o, OWN_ROWS)
        for v, lanes in enumerate(made):
            out[e, :, 128 * v : 128 * v + 128] = lanes
        return carry

    lax.fori_loop(0, N_DEV, one, 0, unroll=CUT_UNROLL)


def cut_halo_kernel(anchor, owner, table, tiles, own, out, second):
    def one(e, carry):
        f = table[0, e]
        w = owner[0, f]
        out[e, :, :384] = own[e]
        made = cut_rows(lambda d, m: tiles[d], anchor[0, f], 4)
        out[e, :, 384:512], out[e, :, 512:640] = made
        place = jnp.where(table[1, w] == f, w, N_DEV)
        second[place, :, :384] = own[e]
        second[place, :, 384:512], second[place, :, 512:640] = made
        return carry

    lax.fori_loop(0, N_DEV, one, 0, unroll=CUT_UNROLL)


def adjoint(f, gates, misfit, parts, window, lam, curl, x_masks):
    lam[:, FZ:, :] = jnp.zeros((3, 8, LANES), jnp.float32)
    curl[:, :8, :] = jnp.zeros((3, 8, LANES), jnp.float32)
    x_of = lax.broadcasted_iota(jnp.int32, (8, LANES), 1) % FP
    x_masks[0] = (x_of != FP - 1).astype(jnp.float32)
    x_masks[1] = (x_of != 0).astype(jnp.float32)
    times = 0.1 * jnp.exp((LN15 / (NTIMES - 1)) * gates[...].astype(jnp.float32))
    scaled = -LOG2E * times
    all_lanes = lax.broadcasted_iota(jnp.int32, (8, LANES), 1)
    last_y = all_lanes >= LANES - FP
    first_y = all_lanes < FP

    def ahead_x(v):
        return pltpu.roll(v, LANES - 1, 1) * x_masks[0]

    def behind_x(v):
        return pltpu.roll(v, 1, 1) * x_masks[1]

    def ahead_y(v):
        return jnp.where(last_y, 0.0, pltpu.roll(v, LANES - FP, 1))

    def behind_y(v):
        return jnp.where(first_y, 0.0, pltpu.roll(v, FP, 1))

    low = lane_iota(FZ) < 64
    for c in range(4):
        for q in range(4):
            window[c, :, 384 * q + 384 : 384 * q + 768] = parts[4 * c + q, :, :384].astype(jnp.float32)
        for base, p in ((0, 4 * c), (1920, 4 * c + 2)):
            head, rest = (parts[p, :, n : n + 128].astype(jnp.float32) for n in (384, 512))
            then, last = (turn(parts[p + 1, :, n : n + 128].astype(jnp.float32), 64) for n in (384, 512))
            window[c, :, base : base + 128] = head
            window[c, :, base + 128 : base + 256] = jnp.where(low, rest, then)
            window[c, :, base + 256 : base + 384] = jnp.where(low, then, last)
    residue = misfit[pl.ds(f, 1), :]
    t_of = [jnp.broadcast_to(scaled[:, g : g + 1], (8, 128)) for g in range(GATES)]
    r_of = [jnp.broadcast_to(residue[:, g : g + 1], (8, 128)) for g in range(GATES)]

    def weigh(i, carry):
        z = pl.ds(pl.multiple_of(8 * i, 8), 8)
        for c0 in range(0, LANES, 384):
            at = slice(c0, c0 + 384)
            sigma = window[3, z, at]
            weight = jnp.zeros_like(sigma)
            for g in range(GATES):
                t3 = jnp.concatenate([t_of[g]] * 3, 1)
                r3 = jnp.concatenate([r_of[g]] * 3, 1)
                weight = weight + r3 * jnp.exp2(sigma * t3)
            for c in range(3):
                lam[c, z, at] = weight * window[c, z, at]
        return carry

    lax.fori_loop(0, FZ // 8, weigh, 0)

    def step(n, carry):
        for i in range(FZ // 8):
            z = slice(8 * i, 8 * i + 8)
            up = slice(8 * i + 1, 8 * i + 9)
            vx, vy, vz = lam[0, z, :], lam[1, z, :], lam[2, z, :]
            at = slice(8 * i + 8, 8 * i + 16)
            curl[0, at, :] = (ahead_y(vz) - vz) - (lam[1, up, :] - vy)
            curl[1, at, :] = (lam[0, up, :] - vx) - (ahead_x(vz) - vz)
            curl[2, at, :] = (ahead_x(vy) - vy) - (ahead_y(vx) - vx)
        for i in range(FZ // 8):
            z = slice(8 * i, 8 * i + 8)
            at = slice(8 * i + 8, 8 * i + 16)
            down = slice(8 * i + 7, 8 * i + 15)
            wx, wy, wz = curl[0, at, :], curl[1, at, :], curl[2, at, :]
            ux = (curl[1, down, :] - wy) - (behind_y(wz) - wz)
            uy = (behind_x(wz) - wz) - (curl[0, down, :] - wx)
            uz = (behind_y(wx) - wx) - (behind_x(wy) - wy)
            sigma = window[3, z, :]
            for c, u in enumerate((ux, uy, uz)):
                v = lam[c, z, :]
                lam[c, z, :] = v - STEP * (u + sigma * v)
        return carry

    lax.fori_loop(0, STEPS, step, 0)


def solve_kernel(me, table, gates, misfit, parts, second, lam_out, back, window, lam, curl, local, x_masks):
    f, own = table[0, me[0]], table[2, me[0]]
    adjoint(f, gates, misfit, parts, window, lam, curl, x_masks)
    for i in range(FZ // 8):
        z = slice(8 * i, 8 * i + 8)
        total = None
        for c in range(3):
            v = lam[c, z, :]
            lam_out[c, z, :] = jnp.where(own == 1, v, 0.0)
            term = v * window[c, z, :]
            total = term if total is None else total + term
        local[z, :] = total
    lane = lane_iota(FZ)
    for j in range(N_DEV):

        def taken(base, high_at, rest_at):
            a, r = base // 128, base % 128
            both = [local[:, 128 * g : 128 * g + 128] for g in (a, min(a + 1, LANES // 128 - 1))]
            high = [v.astype(jnp.bfloat16).astype(jnp.float32) for v in both]
            rest = [turn(v - h, rest_at - r) for v, h in zip(both, high)]
            return [turn(h, high_at - r) for h in high], rest, 128 - r

        high, rest, edge = taken(384 + 96 * j, 64, 80)
        halo_high, halo_rest, halo_edge = taken(FP * (j if j < 8 else 32 + j), 32, 48)
        low = second[j, :, 512:640].astype(jnp.float32)
        v4 = jnp.where(lane < 64, low, jnp.where(lane - 64 < edge, high[0], high[1]))
        v5 = jnp.where(lane - 32 < halo_edge, halo_high[0], halo_high[1])
        v5 = jnp.where(lane < 32, jnp.where(lane + 64 < edge, high[0], high[1]), v5)
        v5 = jnp.where(lane < 80, v5, jnp.where(lane - 80 < edge, rest[0], rest[1]))
        v6 = jnp.where(lane - 48 < halo_edge, halo_rest[0], halo_rest[1])
        v6 = jnp.where(lane < 48, jnp.where(lane + 48 < edge, rest[0], rest[1]), v6)
        back[j, :, :512] = second[j, :, :512]
        for b, v in enumerate((v4, v5, v6)):
            back[j, :, 512 + 128 * b : 640 + 128 * b] = v.astype(jnp.bfloat16)


def second_kernel(me, table, gates, misfit, parts, own, adjoint_out, window, lam, curl, x_masks, sems):
    first = pltpu.make_async_copy(own, adjoint_out.at[0], sems.at[0])
    first.start()
    f = table[1, me[0]]

    @pl.when(f >= 0)
    def _():
        adjoint(f, gates, misfit, parts, window, lam, curl, x_masks)

    @pl.when(f < 0)
    def _():
        lam[:, :FZ, :] = jnp.zeros((3, FZ, LANES), jnp.float32)

    copy = pltpu.make_async_copy(lam.at[:, :FZ, :], adjoint_out.at[1], sems.at[1])
    copy.start()
    copy.wait()
    first.wait()


def regularize_kernel(conductivity, out):
    logs = jnp.log(conductivity[...].astype(jnp.float32))
    delta = logs[1:] - logs[:-1]
    zero_row = jnp.zeros_like(logs[:1])
    out[...] = jnp.concatenate([zero_row, delta], 0) - jnp.concatenate([delta, zero_row], 0)


def add_row(out, row, source, at, o):
    lane = lane_iota(FZ)
    g, s = o // 128, o % 128
    turned = turn(source, o - at)
    out[row, g] = out[row, g] + jnp.where((lane >= s) & (lane < s + FP), turned, 0.0)
    out[row, g + 1] = out[row, g + 1] + jnp.where(lane < s + FP - 128, turned, 0.0)


def scatter_halo_kernel(anchor, table, back, out, rows):
    rows[...] = jnp.zeros_like(rows)

    def one(e, carry):
        v5, v6 = (back[e, :, n : n + 128].astype(jnp.float32) for n in (640, 768))
        add_row(rows, 0, v5 + turn(v6, -16), 32, anchor[0, table[0, e]])
        return carry

    lax.fori_loop(0, N_DEV, one, 0, unroll=UNROLL)
    out[...] = rows[0, :4]


def scatter_own_kernel(anchor, table, back, out):
    out[...] = jnp.zeros_like(out)
    lane = lane_iota(FZ)

    def one(e, carry):
        o = anchor[0, table[0, e]]
        v4, v5, v6 = (back[e, :, 512 + 128 * b : 640 + 128 * b].astype(jnp.float32) for b in range(3))
        both = jnp.where(lane >= 64, v4, v5) + turn(jnp.where(lane >= 80, v5, v6), -16)
        add_row(out, 0, both, 64, o)
        add_row(out, 1, both, 112, o)
        return carry

    lax.fori_loop(0, N_DEV, one, 0, unroll=UNROLL)


def collect_kernel(own, halo, out):
    lane_row = lane_iota(FZ) // TX
    for g in range(4):
        rows = [own[0, g], turn(own[1, g], 32), turn(halo[g], 64)]
        for n in range(4):
            v = jnp.where(lane_row == n, rows[0], rows[2])
            out[4 * g + n] = jnp.where(lane_row == (n + 1) % 4, rows[1], v)


def join_kernel(me, sums, smooth, out):
    lane = lane_iota(FZ)
    base = TX * (me[0] % 4)
    made = []
    for v in range(8):
        even, odd = (turn(sums[2 * v + n], 64 * n - base) for n in range(2))
        made.append(jnp.where(lane < 64, even, odd))
    for j in range(N_DEV):
        v = (24 + j) // 4 if j < 8 else (j - 8) // 4
        halo = turn(sums[j], TX * (j % 4) - 64 - base)
        made[v] = made[v] + jnp.where(lane // TX == j % 4, halo, 0.0)
    for v in range(8):
        at = slice(128 * v, 128 * v + 128)
        out[:FZ, at] = smooth[:FZ, at] + made[v]
    out[FZ:, :] = smooth[FZ:, :]


def to_neighbours(array, goes_up):
    bands, width = lax.axis_size("row"), lax.axis_size("dev")
    pairs = []
    for r in range(bands):
        for d in range(width):
            other = r + 1 if goes_up(d) else r - 1
            if 0 <= other < bands:
                pairs.append((r * width + d, other * width + d))
    return lax.ppermute(array, ("row", "dev"), pairs)


SMEM = pl.BlockSpec(memory_space=pltpu.SMEM)
VMEM = pl.BlockSpec(memory_space=pltpu.VMEM)
ANY = pl.BlockSpec(memory_space=pl.ANY)
PARAMS = pltpu.CompilerParams(vmem_limit_bytes=24 * 2**20)
F32 = jnp.float32
WIDE = 64 * 2**20 - 640 * 2**10
SMALL = pl.CostEstimate(flops=10**6, bytes_accessed=10**6, transcendentals=10**5)
WORK = [
    pltpu.VMEM((4, FZ, LANES), F32),
    pltpu.VMEM((3, FZ + 8, LANES), F32),
    pltpu.VMEM((3, FZ + 8, LANES), F32),
]
MASKS = pltpu.VMEM((2, 8, LANES), F32)


def exchange(blocks):
    return lax.all_to_all(blocks, "dev", 0, 0, tiled=True)


def per_device(primary, conductivity, anchor_x, owner, gate_index, misfit):
    me = lax.axis_index("dev").astype(jnp.int32).reshape(1)
    gates, residues = gate_index.reshape(1, GATES), misfit[0]
    spread = pl.pallas_call(
        tile_kernel,
        out_shape=jax.ShapeDtypeStruct((N_DEV, FZ, QIN), jnp.bfloat16),
        in_specs=[ANY, ANY],
        out_specs=VMEM,
        scratch_shapes=[pltpu.VMEM((4, DEPTH, TX * TY), jnp.bfloat16), pltpu.SemaphoreType.DMA((2,))],
        compiler_params=pltpu.CompilerParams(vmem_limit_bytes=WIDE),
        name="tile",
    )(primary, conductivity)
    tiles = exchange(spread)
    halo_tiles = to_neighbours(tiles[:, :, 256:], lambda d: d % 4 < 2)
    own_cut, table = pl.pallas_call(
        cut_own_kernel,
        out_shape=(
            jax.ShapeDtypeStruct((N_DEV, FZ, 384), jnp.bfloat16),
            jax.ShapeDtypeStruct((3, N_DEV), jnp.int32),
        ),
        in_specs=[SMEM, SMEM, VMEM],
        out_specs=(VMEM, SMEM),
        scratch_shapes=[pltpu.SMEM((N_DEV + 1,), jnp.int32)],
        compiler_params=PARAMS,
        cost_estimate=SMALL,
        name="cut_own",
    )(anchor_x, owner, tiles)
    cut_shape = jax.ShapeDtypeStruct((N_DEV, FZ, CUT), jnp.bfloat16)
    windows, second = pl.pallas_call(
        cut_halo_kernel,
        out_shape=(cut_shape, jax.ShapeDtypeStruct((N_DEV + 1, FZ, CUT), jnp.bfloat16)),
        in_specs=[SMEM, SMEM, SMEM, VMEM, VMEM],
        out_specs=(VMEM, VMEM),
        compiler_params=PARAMS,
        name="cut_halo",
    )(anchor_x, owner, table, halo_tiles, own_cut)
    windows, layers = lax.optimization_barrier((windows, conductivity))
    smooth = pl.pallas_call(
        regularize_kernel,
        out_shape=jax.ShapeDtypeStruct(conductivity.shape, F32),
        in_specs=[VMEM],
        out_specs=VMEM,
        compiler_params=PARAMS,
        cost_estimate=SMALL,
        name="regularize",
    )(layers)
    parts, smooth = lax.optimization_barrier((exchange(windows), smooth))
    lam, back = pl.pallas_call(
        solve_kernel,
        out_shape=(
            jax.ShapeDtypeStruct((3, FZ, LANES), F32),
            jax.ShapeDtypeStruct((N_DEV, FZ, BACK), jnp.bfloat16),
        ),
        in_specs=[SMEM, SMEM, VMEM, VMEM, VMEM, VMEM],
        out_specs=(VMEM, VMEM),
        scratch_shapes=[*WORK, pltpu.VMEM((FZ, LANES), F32), MASKS],
        compiler_params=PARAMS,
        name="solve",
    )(me, table, gates, residues, parts, second)
    back = exchange(back)
    halo_rows = pl.pallas_call(
        scatter_halo_kernel,
        out_shape=jax.ShapeDtypeStruct((4, FZ, 128), F32),
        in_specs=[SMEM, SMEM, VMEM],
        out_specs=VMEM,
        scratch_shapes=[pltpu.VMEM((1, 5, FZ, 128), F32)],
        compiler_params=PARAMS,
        name="scatter_halo",
    )(anchor_x, table, back)
    halo_rows, sums = lax.optimization_barrier((halo_rows, back))
    halo_rows = to_neighbours(halo_rows, lambda d: d >= 8)
    own_rows = pl.pallas_call(
        scatter_own_kernel,
        out_shape=jax.ShapeDtypeStruct((2, 5, FZ, 128), F32),
        in_specs=[SMEM, SMEM, VMEM],
        out_specs=VMEM,
        compiler_params=PARAMS,
        cost_estimate=SMALL,
        name="scatter_own",
    )(anchor_x, table, sums)
    columns = pl.pallas_call(
        collect_kernel,
        out_shape=jax.ShapeDtypeStruct((N_DEV, FZ, 128), F32),
        in_specs=[VMEM, VMEM],
        out_specs=VMEM,
        compiler_params=PARAMS,
        name="collect",
    )(own_rows, halo_rows)
    columns, back = lax.optimization_barrier((columns, back))
    adjoint_field = pl.pallas_call(
        second_kernel,
        out_shape=jax.ShapeDtypeStruct((MOST, 3, FZ, LANES), F32),
        in_specs=[SMEM, SMEM, VMEM, VMEM, VMEM, ANY],
        out_specs=ANY,
        scratch_shapes=[*WORK, MASKS, pltpu.SemaphoreType.DMA((2,))],
        compiler_params=PARAMS,
        cost_estimate=pl.CostEstimate(flops=2 * 10**7, bytes_accessed=4 * 10**6, transcendentals=3 * 10**6),
        name="second",
    )(me, table, gates, residues, back, lam)
    columns, adjoint_field = lax.optimization_barrier((exchange(columns), adjoint_field))
    gradient = pl.pallas_call(
        join_kernel,
        out_shape=jax.ShapeDtypeStruct(conductivity.shape, F32),
        in_specs=[SMEM, VMEM, VMEM],
        out_specs=VMEM,
        compiler_params=PARAMS,
        name="join",
    )(me, columns, smooth)
    return gradient, adjoint_field


def solution(mesh):
    in_specs = (
        P(None, None, ("row", "dev")),
        P(None, ("row", "dev")),
        P("row", None),
        P("row", None),
        P(),
        P("row", None, None),
    )
    out_specs = (P(None, ("row", "dev")), P(("row", "dev"), None, None, None))
    return jax.shard_map(
        per_device, mesh=mesh, in_specs=in_specs, out_specs=out_specs, check_vma=False
    )
```

time: 108 us -> 98.1 us (0.908)
  the two profiles are of different devices: /device:TPU:1 before, /device:TPU:96 now
where the time goes in v4:
time: 98.1 us; the launch traced here: 97.5 us
  blocking collectives  39.6 us (40%)
  waiting for transfers between devices  22.4 us (23%)
  Pallas kernels  20.5 us (21%)
  starting transfers between devices  12.9 us (13%)
  local copies, waits for them, and re-layouts  1.29 us (1%)
    all_to_all x2, blocking collectives, exchange(): return lax.all_to_all(blocks, 'dev', 0, 0, tiled=True)  39.6 us
    all_to_all x2, waiting for transfers between devices, exchange(): return lax.all_to_all(blocks, 'dev', 0, 0, tiled=True)  19 us
    all_to_all x2, starting transfers between devices, exchange(): return lax.all_to_all(blocks, 'dev', 0, 0, tiled=True)  9.1 us
    pallas_call x1, Pallas kernels, per_device(): pl.pallas_call(second_kernel, out_shape=jax.ShapeDtypeStruct((MOST, 3, FZ...  5.44 us
    pallas_call x1, Pallas kernels, per_device(): pl.pallas_call(solve_kernel, out_shape=(jax.ShapeDtypeStruct((3, FZ, LANE...  4.82 us
    ppermute x2, starting transfers between devices, to_neighbours(): return lax.ppermute(array, ('row', 'dev'), pairs)  3.84 us
    ppermute x2, waiting for transfers between devices, to_neighbours(): return lax.ppermute(array, ('row', 'dev'), pairs)  3.35 us
    pallas_call x1, Pallas kernels, per_device(): pl.pallas_call(cut_own_kernel, out_shape=(jax.ShapeDtypeStruct((N_DEV, FZ...  2.33 us
  transfers between devices with their start and end apart: 4, of which 4 were waited for; matrix products, arithmetic and copies ran while one was open for 0% of the time, Pallas kernels for 9%

profile of v4, /device:TPU:96, one launch (start us, length us, event | category | flops | bytes accessed | tf_op | source)
XLA Modules:
  0.0 97.5 jit_solution(5266117230375907032)
XLA Ops:
  0.6 0.0 copy-start.1
  0.6 0.0 copy-start.3
  0.6 1.8 %tile.1 = bf16[16,40,384]{2,1,0:T(8,128)(2,1)} custom-call(bf16[3,64,1024]{2,1,0:T(8,128)(2,1)} %primary.1, bf16[64,1024]{1,0:T(8,128)(2,1)} %conductivity.2), custom_call_target="tpu_custom_call" | custom-call | tf_op jit(solution)/shard_map/tile/pallas_call | solution.py:372
  2.5 18.2 %all_to_all.20.tiles = bf16[16,40,384]{2,1,0:T(8,128)(2,1)S(1)} all-to-all(bf16[16,40,384]{2,1,0:T(8,128)(2,1)} %tile.1), channel_id=1, replica_groups=mesh['row'=16,'dev'=16] {'dev'}, dimensions={0} | all-to-all | bytes 983040 | tf_op jit(solution)/shard_map/all_to_all | solution.py:366
  20.7 1.9 %collective-permute-start = (bf16[16,40,128]{2,1,0:T(8,128)(2,1)S(1)}, bf16[16,40,128]{2,1,0:T(8,128)(2,1)S(1)}, u32[]{:S(2)}, u32[]{:S(2)}) collective-permute-start(bf16[16,40,128]{2,1,0:T(8,128)(2,1)S(1)} %slice.4), channel_id=1, source_target_pairs={{0,16},{1,17},{4,20},{5,21},{8,24},{9,25},{12,28},{13,29},{16,32},... | collective-permute-start | bytes 491528 | tf_op jit(solution)/shard_map/ppermute | solution.py:347
  22.6 0.0 copy-done.1
  22.6 0.0 copy-done.3
  22.7 2.3 %cut_own.1 = (bf16[16,40,384]{2,1,0:T(8,128)(2,1)S(1)}, s32[3,16]{1,0:T(4,128)S(1)}) custom-call(s32[1,16]{1,0:T(1,128)S(1)} %copy-done.1, s32[1,16]{1,0:T(1,128)S(1)} %copy-done.3, bf16[16,40,384]{2,1,0:T(8,128)(2,1)S(1)} %all_to_all.20.tiles), custom_call_target="tpu_custom_call" | custom-call | flops 1000000 | bytes 1000000 | tf_op jit(solution)/shard_map/cut_own/pallas_call | solution.py:383
  25.0 2.3 %collective-permute-done.tiles = bf16[16,40,128]{2,1,0:T(8,128)(2,1)S(1)} collective-permute-done((bf16[16,40,128]{2,1,0:T(8,128)(2,1)S(1)}, bf16[16,40,128]{2,1,0:T(8,128)(2,1)S(1)}, u32[]{:S(2)}, u32[]{:S(2)}) %collective-permute-start) | collective-permute-done | bytes 163872 | tf_op jit(solution)/shard_map/ppermute | solution.py:347
  27.3 0.0 copy-start
  27.3 2.3 %cut_halo.1 = (bf16[16,40,640]{2,1,0:T(8,128)(2,1)}, bf16[17,40,640]{2,1,0:T(8,128)(2,1)S(1)}) custom-call(s32[1,16]{1,0:T(1,128)S(1)} %copy-done.1, s32[1,16]{1,0:T(1,128)S(1)} %copy-done.3, s32[3,16]{1,0:T(4,128)S(1)} %get-tuple-element.18.table, bf16[16,40,128]{2,1,0:T(8,128)(2,1)S(1)} %collective-permute-done.tiles, ...), custom_call_target="tpu_custom_call" | custom-call | tf_op jit(solution)/shard_map/cut_halo/pallas_call | solution.py:397
  29.6 0.0 copy-start.2
  29.6 0.0 copy-start.4
  29.6 3.8 %all-to-all-start.1 = ((bf16[16,40,640]{2,1,0:T(8,128)(2,1)}), bf16[16,40,640]{2,1,0:T(8,128)(2,1)S(1)}, u32[]{:S(2)}, u32[]{:S(2)}) async-start(bf16[16,40,640]{2,1,0:T(8,128)(2,1)} %get-tuple-element.21), calls=%async_computation.1 | async-start | bytes 1638400 | tf_op jit(solution)/shard_map/all_to_all | solution.py:366
  33.4 0.0 copy-done
  33.4 0.1 regularize.1.smooth
  33.5 16.4 %all-to-all-done.1.parts = bf16[16,40,640]{2,1,0:T(8,128)(2,1)S(1)} async-done(((bf16[16,40,640]{2,1,0:T(8,128)(2,1)}), bf16[16,40,640]{2,1,0:T(8,128)(2,1)S(1)}, u32[]{:S(2)}, u32[]{:S(2)}) %all-to-all-start.1) | async-done | bytes 819232 | tf_op jit(solution)/shard_map/all_to_all | solution.py:366
  49.8 0.0 copy-done.2
  49.8 0.0 copy-done.4
  49.8 4.8 %solve.1 = (f32[3,40,2304]{2,1,0:T(8,128)S(1)}, bf16[16,40,896]{2,1,0:T(8,128)(2,1)S(1)}) custom-call(s32[1]{0:T(128)} %bitcast.me, s32[3,16]{1,0:T(4,128)S(1)} %get-tuple-element.18.table, s32[1,30]{1,0:T(1,128)S(1)} %bitcast.5, f32[16,30]{1,0:T(8,128)S(1)} %bitcast.3, bf16[16,40,640]{2,1,0:T(8,128)(2,1)S(1)} %all-to-all-done.1.parts, ...), custom_call_target="tpu_custom_call" | custom-call | tf_op jit(solution)/shard_map/solve/pallas_call | solution.py:416
  54.7 0.0 copy-start.5
  54.7 21.4 %all_to_all.21.back.parts = bf16[16,40,896]{2,1,0:T(8,128)(2,1)S(1)} all-to-all(bf16[16,40,896]{2,1,0:T(8,128)(2,1)S(1)} %get-tuple-element.25), channel_id=1, replica_groups=mesh['row'=16,'dev'=16] {'dev'}, dimensions={0} | all-to-all | bytes 2293760 | tf_op jit(solution)/shard_map/all_to_all | solution.py:366
  76.1 0.0 copy-done.5
  76.1 1.0 %scatter_halo.1 = f32[4,40,128]{2,1,0:T(8,128)S(1)} custom-call(s32[1,16]{1,0:T(1,128)S(1)} %copy-done.1, s32[3,16]{1,0:T(4,128)S(1)} %get-tuple-element.18.table, bf16[16,40,896]{2,1,0:T(8,128)(2,1)S(1)} %all_to_all.21.back.parts), custom_call_target="tpu_custom_call" | custom-call | tf_op jit(solution)/shard_map/scatter_halo/pallas_call | solution.py:429
  77.1 1.9 %collective-permute-start.1 = (f32[4,40,128]{2,1,0:T(8,128)S(1)}, f32[4,40,128]{2,1,0:T(8,128)S(1)}, u32[]{:S(2)}, u32[]{:S(2)}) collective-permute-start(f32[4,40,128]{2,1,0:T(8,128)S(1)} %scatter_halo.1), channel_id=1, source_target_pairs={{8,24},{9,25},{10,26},{11,27},{12,28},{13,29},{14,30},{15,31},{16,... | collective-permute-start | bytes 245768 | tf_op jit(solution)/shard_map/ppermute | solution.py:347
  79.0 1.0 %scatter_own.1.own = f32[2,5,40,128]{3,2,1,0:T(8,128)S(1)} custom-call(s32[1,16]{1,0:T(1,128)S(1)} %copy-done.1, s32[3,16]{1,0:T(4,128)S(1)} %get-tuple-element.18.table, bf16[16,40,896]{2,1,0:T(8,128)(2,1)S(1)} %all_to_all.21.back.parts), custom_call_target="tpu_custom_call" | custom-call | flops 1000000 | bytes 1000000 | tf_op jit(solution)/shard_map/scatter_own/pallas_call | solution.py:440
  80.1 1.0 %collective-permute-done.1.halo = f32[4,40,128]{2,1,0:T(8,128)S(1)} collective-permute-done((f32[4,40,128]{2,1,0:T(8,128)S(1)}, f32[4,40,128]{2,1,0:T(8,128)S(1)}, u32[]{:S(2)}, u32[]{:S(2)}) %collective-permute-start.1) | collective-permute-done | bytes 81952 | tf_op jit(solution)/shard_map/ppermute | solution.py:347
  81.1 0.8 collect.1
  81.9 5.4 %all-to-all-start.3 = ((f32[16,40,128]{2,1,0:T(8,128)}), f32[16,40,128]{2,1,0:T(8,128)S(1)}, u32[]{:S(2)}, u32[]{:S(2)}) async-start(f32[16,40,128]{2,1,0:T(8,128)} %collect.1), calls=%async_computation.3 | async-start | bytes 655360 | tf_op jit(solution)/shard_map/all_to_all | solution.py:366
  87.2 0.0 copy-start.6
  87.3 1.2 %copy-done.6 = f32[3,40,2304]{2,1,0:T(8,128)S(1)} copy-done((f32[3,40,2304]{2,1,0:T(8,128)S(1)}, f32[3,40,2304]{2,1,0:T(8,128)}, u32[]{:S(2)}) %copy-start.6) | copy-done | bytes 1105944
  88.5 5.4 %second.1 = f32[2,3,40,2304]{3,2,1,0:T(8,128)} custom-call(s32[1]{0:T(128)} %bitcast.me, s32[3,16]{1,0:T(4,128)S(1)} %get-tuple-element.18.table, s32[1,30]{1,0:T(1,128)S(1)} %bitcast.6, f32[16,30]{1,0:T(8,128)S(1)} %bitcast.4, bf16[16,40,896]{2,1,0:T(8,128)(2,1)S(1)} %all_to_all.21.back.parts, f32[3,40,2304]{2,1,0:T(8,128)S(1)} %copy-done.6), custom_call_target="tpu_custom_call" | custom-call | flops 20000000 | bytes 4000000 | tf_op jit(solution)/shard_map/second/pallas_call | solution.py:458
  93.9 2.7 %all-to-all-done.3.sums = f32[16,40,128]{2,1,0:T(8,128)S(1)} async-done(((f32[16,40,128]{2,1,0:T(8,128)}), f32[16,40,128]{2,1,0:T(8,128)S(1)}, u32[]{:S(2)}, u32[]{:S(2)}) %all-to-all-start.3) | async-done | bytes 327712 | tf_op jit(solution)/shard_map/all_to_all | solution.py:366
  96.6 0.9 join.1
  (1 shorter events, 0.0 us)
Async XLA Ops:
  0.6 22.0 %copy-start.1 = (s32[1,16]{1,0:T(1,128)S(1)}, s32[1,16]{1,0:T(1,128)}, u32[]{:S(2)}) copy-start(s32[1,16]{1,0:T(1,128)} %anchor.7) | copy-start | bytes 196
  0.6 22.0 %copy-start.3 = (s32[1,16]{1,0:T(1,128)S(1)}, s32[1,16]{1,0:T(1,128)}, u32[]{:S(2)}) copy-start(s32[1,16]{1,0:T(1,128)} %owner.3) | copy-start | bytes 196
  20.7 6.6 %collective-permute-start = (bf16[16,40,128]{2,1,0:T(8,128)(2,1)S(1)}, bf16[16,40,128]{2,1,0:T(8,128)(2,1)S(1)}, u32[]{:S(2)}, u32[]{:S(2)}) collective-permute-start(bf16[16,40,128]{2,1,0:T(8,128)(2,1)S(1)} %slice.4), channel_id=1, source_target_pairs={{0,16},{1,17},{4,20},{5,21},{8,24},{9,25},{12,28},{13,29},{16,32},... | collective-permute-start | bytes 491528 | tf_op jit(solution)/shard_map/ppermute | solution.py:347
  27.3 6.0 %copy-start = (bf16[64,1024]{1,0:T(8,128)(2,1)S(1)}, bf16[64,1024]{1,0:T(8,128)(2,1)}, u32[]{:S(2)}) copy-start(bf16[64,1024]{1,0:T(8,128)(2,1)} %conductivity.2) | copy-start | bytes 393220
  29.6 20.2 %copy-start.2 = (f32[1,16,30]{2,1,0:T(8,128)S(1)}, f32[1,16,30]{2,1,0:T(8,128)}, u32[]{:S(2)}) copy-start(f32[1,16,30]{2,1,0:T(8,128)} %param.11) | copy-start | bytes 5764
  29.6 20.2 %copy-start.4 = (s32[30]{0:T(128)S(1)}, s32[30]{0:T(128)}, u32[]{:S(2)}) copy-start(s32[30]{0:T(128)} %param.10) | copy-start | bytes 364
  29.6 20.2 %all-to-all-start.1 = ((bf16[16,40,640]{2,1,0:T(8,128)(2,1)}), bf16[16,40,640]{2,1,0:T(8,128)(2,1)S(1)}, u32[]{:S(2)}, u32[]{:S(2)}) async-start(bf16[16,40,640]{2,1,0:T(8,128)(2,1)} %get-tuple-element.21), calls=%async_computation.1 | async-start | bytes 1638400 | tf_op jit(solution)/shard_map/all_to_all | solution.py:366
  54.7 21.4 %copy-start.5 = (f32[3,40,2304]{2,1,0:T(8,128)}, f32[3,40,2304]{2,1,0:T(8,128)S(1)}, u32[]{:S(2)}) copy-start(f32[3,40,2304]{2,1,0:T(8,128)S(1)} %get-tuple-element.30.own) | copy-start | bytes 3317764
  77.1 4.0 %collective-permute-start.1 = (f32[4,40,128]{2,1,0:T(8,128)S(1)}, f32[4,40,128]{2,1,0:T(8,128)S(1)}, u32[]{:S(2)}, u32[]{:S(2)}) collective-permute-start(f32[4,40,128]{2,1,0:T(8,128)S(1)} %scatter_halo.1), channel_id=1, source_target_pairs={{8,24},{9,25},{10,26},{11,27},{12,28},{13,29},{14,30},{15,31},{16,... | collective-permute-start | bytes 245768 | tf_op jit(solution)/shard_map/ppermute | solution.py:347
  81.9 14.7 %all-to-all-start.3 = ((f32[16,40,128]{2,1,0:T(8,128)}), f32[16,40,128]{2,1,0:T(8,128)S(1)}, u32[]{:S(2)}, u32[]{:S(2)}) async-start(f32[16,40,128]{2,1,0:T(8,128)} %collect.1), calls=%async_computation.3 | async-start | bytes 655360 | tf_op jit(solution)/shard_map/all_to_all | solution.py:366
  87.2 1.2 %copy-start.6 = (f32[3,40,2304]{2,1,0:T(8,128)S(1)}, f32[3,40,2304]{2,1,0:T(8,128)}, u32[]{:S(2)}) copy-start(f32[3,40,2304]{2,1,0:T(8,128)} %copy-done.5) | copy-start | bytes 3317764

commit v5 on v4

--- a/solution.py
+++ b/solution.py
@@ -14,7 +14,6 @@
 STEPS = 2
 MOST = 2
 FOOT_ROW = 16
-HALO = 8
 N_DEV = 16
 STEP = 0.05
 
@@ -64,19 +63,22 @@
         n = n + (held < 0).astype(jnp.int32)
 
 
-def tile_kernel(primary, conductivity, out, held, sems):
-    copies = [
-        pltpu.make_async_copy(primary.at[:, :DEPTH], held.at[:3], sems.at[0]),
-        pltpu.make_async_copy(conductivity.at[:DEPTH], held.at[3], sems.at[1]),
-    ]
-    for copy in copies:
+def tile_kernel(primary, conductivity, out_to, held, out, sems):
+    arrivals = [pltpu.make_async_copy(primary.at[c, :DEPTH], held.at[c], sems.at[0, c]) for c in range(3)]
+    arrivals.append(pltpu.make_async_copy(conductivity.at[:DEPTH], held.at[3], sems.at[0, 3]))
+    for copy in arrivals:
         copy.start()
-    for copy in copies:
-        copy.wait()
+    leaving = []
     for c in range(4):
+        arrivals[c].wait()
         for q, start in enumerate((768, 896, 0, 128)):
             out[4 * c + q, :, :256] = held[c, :FZ, 256 * q : 256 * q + 256]
             out[4 * c + q, :, 256:] = held[c, :FZ, start : start + 128]
+        some = slice(4 * c, 4 * c + 4)
+        leaving.append(pltpu.make_async_copy(out.at[some], out_to.at[some], sems.at[1, c]))
+        leaving[-1].start()
+    for copy in leaving:
+        copy.wait()
 
 
 def cut_rows(tiles, o, count):
@@ -105,7 +107,17 @@
     return [v.astype(jnp.bfloat16) for v in made]
 
 
-def cut_own_kernel(anchor, owner, tiles, out, table, seconds):
+def in_halves(one, copy_of):
+    half = N_DEV // 2
+    copies = [copy_of(h, slice(half * h, half * h + half)) for h in range(2)]
+    for h, copy in enumerate(copies):
+        lax.fori_loop(half * h, half * h + half, one, 0, unroll=CUT_UNROLL)
+        copy.start()
+    for copy in copies:
+        copy.wait()
+
+
+def cut_own_kernel(anchor, owner, tiles, out, windows, table, seconds, sems):
     assign(owner, table, seconds)
 
     def one(e, carry):
@@ -115,22 +127,23 @@
             out[e, :, 128 * v : 128 * v + 128] = lanes
         return carry
 
-    lax.fori_loop(0, N_DEV, one, 0, unroll=CUT_UNROLL)
-
-
-def cut_halo_kernel(anchor, owner, table, tiles, own, out, second):
+    in_halves(one, lambda h, at: pltpu.make_async_copy(out.at[at], windows.at[at, :, :384], sems.at[h]))
+
+
+def cut_halo_kernel(anchor, owner, table, tiles, own, windows_in, windows, second, out, sems):
+    del windows_in
+
     def one(e, carry):
         f = table[0, e]
         w = owner[0, f]
-        out[e, :, :384] = own[e]
         made = cut_rows(lambda d, m: tiles[d], anchor[0, f], 4)
-        out[e, :, 384:512], out[e, :, 512:640] = made
+        out[e, :, :128], out[e, :, 128:] = made
         place = jnp.where(table[1, w] == f, w, N_DEV)
         second[place, :, :384] = own[e]
         second[place, :, 384:512], second[place, :, 512:640] = made
         return carry
 
-    lax.fori_loop(0, N_DEV, one, 0, unroll=CUT_UNROLL)
+    in_halves(one, lambda h, at: pltpu.make_async_copy(out.at[at], windows.at[at, :, 384:], sems.at[h]))
 
 
 def adjoint(f, gates, misfit, parts, window, lam, curl, x_masks):
@@ -311,12 +324,16 @@
 
 
 def collect_kernel(own, halo, out):
-    lane_row = lane_iota(FZ) // TX
+    lane_row = lane_iota(32) // TX
     for g in range(4):
-        rows = [own[0, g], turn(own[1, g], 32), turn(halo[g], 64)]
+        whole = (own[0, g], own[1, g], halo[g])
+        rows = [turn(v[:32], 32 * n) for n, v in enumerate(whole)]
+        deep = jnp.concatenate([turn(v[32:], 96) for v in whole] + [jnp.zeros((8, 128), jnp.float32)], 0)
         for n in range(4):
-            v = jnp.where(lane_row == n, rows[0], rows[2])
-            out[4 * g + n] = jnp.where(lane_row == (n + 1) % 4, rows[1], v)
+            v = jnp.where(lane_row == n, rows[0], deep)
+            for m in range(1, 3):
+                v = jnp.where(lane_row == (n + m) % 4, rows[m], v)
+            out[4 * g + n] = v
 
 
 def join_kernel(me, sums, smooth, out):
@@ -324,11 +341,16 @@
     base = TX * (me[0] % 4)
     made = []
     for v in range(8):
-        even, odd = (turn(sums[2 * v + n], 64 * n - base) for n in range(2))
-        made.append(jnp.where(lane < 64, even, odd))
+        halves = []
+        for n in range(2):
+            top = turn(sums[2 * v + n], 64 * n - base)
+            even, odd = (turn(sums[2 * v + n, 8 * m : 8 * m + 8], 64 * n + 32 + 32 * m - base) for m in range(2))
+            halves.append(jnp.concatenate([top, jnp.where(lane[:8] % 64 < TX, even, odd)], 0))
+        made.append(jnp.where(lane < 64, halves[0], halves[1]))
     for j in range(N_DEV):
         v = (24 + j) // 4 if j < 8 else (j - 8) // 4
-        halo = turn(sums[j], TX * (j % 4) - 64 - base)
+        at = TX * (j % 4) - base
+        halo = jnp.concatenate([turn(sums[j], at - 64), turn(sums[j, 16:24], at - 96)], 0)
         made[v] = made[v] + jnp.where(lane // TX == j % 4, halo, 0.0)
     for v in range(8):
         at = slice(128 * v, 128 * v + 128)
@@ -373,35 +395,42 @@
         tile_kernel,
         out_shape=jax.ShapeDtypeStruct((N_DEV, FZ, QIN), jnp.bfloat16),
         in_specs=[ANY, ANY],
-        out_specs=VMEM,
-        scratch_shapes=[pltpu.VMEM((4, DEPTH, TX * TY), jnp.bfloat16), pltpu.SemaphoreType.DMA((2,))],
+        out_specs=ANY,
+        scratch_shapes=[
+            pltpu.VMEM((4, DEPTH, TX * TY), jnp.bfloat16),
+            pltpu.VMEM((N_DEV, FZ, QIN), jnp.bfloat16),
+            pltpu.SemaphoreType.DMA((2, 4)),
+        ],
         compiler_params=pltpu.CompilerParams(vmem_limit_bytes=WIDE),
         name="tile",
     )(primary, conductivity)
     tiles = exchange(spread)
     halo_tiles = to_neighbours(tiles[:, :, 256:], lambda d: d % 4 < 2)
-    own_cut, table = pl.pallas_call(
+    cut_shape = jax.ShapeDtypeStruct((N_DEV, FZ, CUT), jnp.bfloat16)
+    own_cut, windows, table = pl.pallas_call(
         cut_own_kernel,
         out_shape=(
             jax.ShapeDtypeStruct((N_DEV, FZ, 384), jnp.bfloat16),
+            cut_shape,
             jax.ShapeDtypeStruct((3, N_DEV), jnp.int32),
         ),
         in_specs=[SMEM, SMEM, VMEM],
-        out_specs=(VMEM, SMEM),
-        scratch_shapes=[pltpu.SMEM((N_DEV + 1,), jnp.int32)],
+        out_specs=(VMEM, ANY, SMEM),
+        scratch_shapes=[pltpu.SMEM((N_DEV + 1,), jnp.int32), pltpu.SemaphoreType.DMA((2,))],
         compiler_params=PARAMS,
         cost_estimate=SMALL,
         name="cut_own",
     )(anchor_x, owner, tiles)
-    cut_shape = jax.ShapeDtypeStruct((N_DEV, FZ, CUT), jnp.bfloat16)
     windows, second = pl.pallas_call(
         cut_halo_kernel,
         out_shape=(cut_shape, jax.ShapeDtypeStruct((N_DEV + 1, FZ, CUT), jnp.bfloat16)),
-        in_specs=[SMEM, SMEM, SMEM, VMEM, VMEM],
-        out_specs=(VMEM, VMEM),
+        in_specs=[SMEM, SMEM, SMEM, VMEM, VMEM, ANY],
+        out_specs=(ANY, VMEM),
+        scratch_shapes=[pltpu.VMEM((N_DEV, FZ, CUT - 384), jnp.bfloat16), pltpu.SemaphoreType.DMA((2,))],
+        input_output_aliases={5: 0},
         compiler_params=PARAMS,
         name="cut_halo",
-    )(anchor_x, owner, table, halo_tiles, own_cut)
+    )(anchor_x, owner, table, halo_tiles, own_cut, windows)
     windows, layers = lax.optimization_barrier((windows, conductivity))
     smooth = pl.pallas_call(
         regularize_kernel,
@@ -448,7 +477,7 @@
     )(anchor_x, table, sums)
     columns = pl.pallas_call(
         collect_kernel,
-        out_shape=jax.ShapeDtypeStruct((N_DEV, FZ, 128), F32),
+        out_shape=jax.ShapeDtypeStruct((N_DEV, 32, 128), F32),
         in_specs=[VMEM, VMEM],
         out_specs=VMEM,
         compiler_params=PARAMS,

time: 98.1 us -> 97.4 us (level)
  Pallas kernels: 20.5 us -> 17.4 us
  waiting for transfers between devices: 22.4 us -> 23.7 us
  blocking collectives: 39.6 us -> 40.7 us
    pallas_call x1, Pallas kernels: 5.44 us -> 1.94 us  [per_device(): pl.pallas_call(second_kernel, out_shape=jax.ShapeDtypeStruct((MOST, 3, FZ...]
    all_to_all x2, waiting for transfers between devices: 19 us -> 21.1 us  [exchange(): return lax.all_to_all(blocks, 'dev', 0, 0, tiled=True)]
    all_to_all x2, blocking collectives: 39.6 us -> 40.7 us  [exchange(): return lax.all_to_all(blocks, 'dev', 0, 0, tiled=True)]
  transfers between devices with their start and end apart: 4 -> 4, of which waited for: 4 -> 4; matrix products, arithmetic and copies ran while one was open for 0% -> 0% of each run, Pallas kernels for 9% -> 6%
where the time goes in v5:
time: 97.4 us; the launch traced here: 96.9 us
  blocking collectives  40.7 us (42%)
  waiting for transfers between devices  23.7 us (24%)
  Pallas kernels  17.4 us (18%)
  starting transfers between devices  12.9 us (13%)
  local copies, waits for them, and re-layouts  1.3 us (1%)
    all_to_all x2, blocking collectives, exchange(): return lax.all_to_all(blocks, 'dev', 0, 0, tiled=True)  40.7 us
    all_to_all x2, waiting for transfers between devices, exchange(): return lax.all_to_all(blocks, 'dev', 0, 0, tiled=True)  21.1 us
    all_to_all x2, starting transfers between devices, exchange(): return lax.all_to_all(blocks, 'dev', 0, 0, tiled=True)  9.07 us
    pallas_call x1, Pallas kernels, per_device(): pl.pallas_call(solve_kernel, out_shape=(jax.ShapeDtypeStruct((3, FZ, LANE...  4.82 us
    ppermute x2, starting transfers between devices, to_neighbours(): return lax.ppermute(array, ('row', 'dev'), pairs)  3.84 us
    pallas_call x1, Pallas kernels, per_device(): pl.pallas_call(cut_own_kernel, out_shape=(jax.ShapeDtypeStruct((N_DEV, FZ...  3.1 us
    ppermute x2, waiting for transfers between devices, to_neighbours(): return lax.ppermute(array, ('row', 'dev'), pairs)  2.59 us
    pallas_call x1, Pallas kernels, per_device(): pl.pallas_call(cut_halo_kernel, out_shape=(cut_shape, jax.ShapeDtypeStruc...  1.95 us
  transfers between devices with their start and end apart: 4, of which 4 were waited for; matrix products, arithmetic and copies ran while one was open for 0% of the time, Pallas kernels for 6%

profile of v5, /device:TPU:96, one launch (start us, length us, event | category | flops | bytes accessed | tf_op | source)
XLA Modules:
  0.0 96.9 jit_solution(11098386684970712019)
XLA Ops:
  0.6 0.0 copy-start.1
  0.6 0.0 copy-start.3
  0.6 1.8 %tile.1 = bf16[16,40,384]{2,1,0:T(8,128)(2,1)} custom-call(bf16[3,64,1024]{2,1,0:T(8,128)(2,1)} %primary.1, bf16[64,1024]{1,0:T(8,128)(2,1)} %conductivity.2), custom_call_target="tpu_custom_call" | custom-call | tf_op jit(solution)/shard_map/tile/pallas_call | solution.py:394
  2.4 18.2 %all_to_all.20.tiles = bf16[16,40,384]{2,1,0:T(8,128)(2,1)S(1)} all-to-all(bf16[16,40,384]{2,1,0:T(8,128)(2,1)} %tile.1), channel_id=1, replica_groups=mesh['row'=16,'dev'=16] {'dev'}, dimensions={0} | all-to-all | bytes 983040 | tf_op jit(solution)/shard_map/all_to_all | solution.py:388
  20.6 1.9 %collective-permute-start = (bf16[16,40,128]{2,1,0:T(8,128)(2,1)S(1)}, bf16[16,40,128]{2,1,0:T(8,128)(2,1)S(1)}, u32[]{:S(2)}, u32[]{:S(2)}) collective-permute-start(bf16[16,40,128]{2,1,0:T(8,128)(2,1)S(1)} %slice.4), channel_id=1, source_target_pairs={{0,16},{1,17},{4,20},{5,21},{8,24},{9,25},{12,28},{13,29},{16,32},... | collective-permute-start | bytes 491528 | tf_op jit(solution)/shard_map/ppermute | solution.py:369
  22.6 0.0 copy-done.1
  22.6 0.0 copy-done.3
  22.6 3.1 %cut_own.1 = (bf16[16,40,384]{2,1,0:T(8,128)(2,1)S(1)}, bf16[16,40,640]{2,1,0:T(8,128)(2,1)}, s32[3,16]{1,0:T(4,128)S(1)}) custom-call(s32[1,16]{1,0:T(1,128)S(1)} %copy-done.1, s32[1,16]{1,0:T(1,128)S(1)} %copy-done.3, bf16[16,40,384]{2,1,0:T(8,128)(2,1)S(1)} %all_to_all.20.tiles), custom_call_target="tpu_custom_call" | custom-call | flops 1000000 | bytes 1000000 | tf_op jit(solution)/shard_map/cut_own/pallas_call | solution.py:410
  25.7 1.6 %collective-permute-done.tiles = bf16[16,40,128]{2,1,0:T(8,128)(2,1)S(1)} collective-permute-done((bf16[16,40,128]{2,1,0:T(8,128)(2,1)S(1)}, bf16[16,40,128]{2,1,0:T(8,128)(2,1)S(1)}, u32[]{:S(2)}, u32[]{:S(2)}) %collective-permute-start) | collective-permute-done | bytes 163872 | tf_op jit(solution)/shard_map/ppermute | solution.py:369
  27.3 2.0 %cut_halo.1 = (bf16[16,40,640]{2,1,0:T(8,128)(2,1)}, bf16[17,40,640]{2,1,0:T(8,128)(2,1)S(1)}) custom-call(s32[1,16]{1,0:T(1,128)S(1)} %copy-done.1, s32[1,16]{1,0:T(1,128)S(1)} %copy-done.3, s32[3,16]{1,0:T(4,128)S(1)} %get-tuple-element.19.table, bf16[16,40,128]{2,1,0:T(8,128)(2,1)S(1)} %collective-permute-done.tiles, ...), custom_call_target="tpu_custom_call", output_to_operand_aliasing={{0}: (5, {})} | custom-call | tf_op jit(solution)/shard_map/cut_halo/pallas_call | solution.py:424
  29.2 0.0 copy-start
  29.3 0.0 copy-start.2
  29.3 0.0 copy-start.4
  29.3 3.8 %all-to-all-start.1 = ((bf16[16,40,640]{2,1,0:T(8,128)(2,1)}), bf16[16,40,640]{2,1,0:T(8,128)(2,1)S(1)}, u32[]{:S(2)}, u32[]{:S(2)}) async-start(bf16[16,40,640]{2,1,0:T(8,128)(2,1)} %get-tuple-element.23), calls=%async_computation.1 | async-start | bytes 1638400 | tf_op jit(solution)/shard_map/all_to_all | solution.py:388
  33.1 0.0 copy-done
  33.1 0.1 regularize.1.smooth
  33.2 15.1 %all-to-all-done.1.parts = bf16[16,40,640]{2,1,0:T(8,128)(2,1)S(1)} async-done(((bf16[16,40,640]{2,1,0:T(8,128)(2,1)}), bf16[16,40,640]{2,1,0:T(8,128)(2,1)S(1)}, u32[]{:S(2)}, u32[]{:S(2)}) %all-to-all-start.1) | async-done | bytes 819232 | tf_op jit(solution)/shard_map/all_to_all | solution.py:388
  48.3 0.0 copy-done.2
  48.3 0.0 copy-done.4
  48.3 4.8 %solve.1 = (f32[3,40,2304]{2,1,0:T(8,128)S(1)}, bf16[16,40,896]{2,1,0:T(8,128)(2,1)S(1)}) custom-call(s32[1]{0:T(128)} %bitcast.me, s32[3,16]{1,0:T(4,128)S(1)} %get-tuple-element.19.table, s32[1,30]{1,0:T(1,128)S(1)} %bitcast.5, f32[16,30]{1,0:T(8,128)S(1)} %bitcast.3, bf16[16,40,640]{2,1,0:T(8,128)(2,1)S(1)} %all-to-all-done.1.parts, ...), custom_call_target="tpu_custom_call" | custom-call | tf_op jit(solution)/shard_map/solve/pallas_call | solution.py:445
  53.1 0.0 copy-start.5
  53.2 22.5 %all_to_all.21.back.parts = bf16[16,40,896]{2,1,0:T(8,128)(2,1)S(1)} all-to-all(bf16[16,40,896]{2,1,0:T(8,128)(2,1)S(1)} %get-tuple-element.27), channel_id=1, replica_groups=mesh['row'=16,'dev'=16] {'dev'}, dimensions={0} | all-to-all | bytes 2293760 | tf_op jit(solution)/shard_map/all_to_all | solution.py:388
  75.7 0.0 copy-done.5
  75.7 1.0 %scatter_halo.1 = f32[4,40,128]{2,1,0:T(8,128)S(1)} custom-call(s32[1,16]{1,0:T(1,128)S(1)} %copy-done.1, s32[3,16]{1,0:T(4,128)S(1)} %get-tuple-element.19.table, bf16[16,40,896]{2,1,0:T(8,128)(2,1)S(1)} %all_to_all.21.back.parts), custom_call_target="tpu_custom_call" | custom-call | tf_op jit(solution)/shard_map/scatter_halo/pallas_call | solution.py:458
  76.7 1.9 %collective-permute-start.1 = (f32[4,40,128]{2,1,0:T(8,128)S(1)}, f32[4,40,128]{2,1,0:T(8,128)S(1)}, u32[]{:S(2)}, u32[]{:S(2)}) collective-permute-start(f32[4,40,128]{2,1,0:T(8,128)S(1)} %scatter_halo.1), channel_id=1, source_target_pairs={{8,24},{9,25},{10,26},{11,27},{12,28},{13,29},{14,30},{15,31},{16,... | collective-permute-start | bytes 245768 | tf_op jit(solution)/shard_map/ppermute | solution.py:369
  78.6 1.0 %scatter_own.1.own = f32[2,5,40,128]{3,2,1,0:T(8,128)S(1)} custom-call(s32[1,16]{1,0:T(1,128)S(1)} %copy-done.1, s32[3,16]{1,0:T(4,128)S(1)} %get-tuple-element.19.table, bf16[16,40,896]{2,1,0:T(8,128)(2,1)S(1)} %all_to_all.21.back.parts), custom_call_target="tpu_custom_call" | custom-call | flops 1000000 | bytes 1000000 | tf_op jit(solution)/shard_map/scatter_own/pallas_call | solution.py:469
  79.7 1.0 %collective-permute-done.1.halo = f32[4,40,128]{2,1,0:T(8,128)S(1)} collective-permute-done((f32[4,40,128]{2,1,0:T(8,128)S(1)}, f32[4,40,128]{2,1,0:T(8,128)S(1)}, u32[]{:S(2)}, u32[]{:S(2)}) %collective-permute-start.1) | collective-permute-done | bytes 81952 | tf_op jit(solution)/shard_map/ppermute | solution.py:369
  80.7 0.8 collect.1
  81.5 5.3 %all-to-all-start.3 = ((f32[16,32,128]{2,1,0:T(8,128)}), f32[16,32,128]{2,1,0:T(8,128)S(1)}, u32[]{:S(2)}, u32[]{:S(2)}) async-start(f32[16,32,128]{2,1,0:T(8,128)} %collect.1), calls=%async_computation.3 | async-start | bytes 524288 | tf_op jit(solution)/shard_map/all_to_all | solution.py:388
  86.8 0.0 copy-start.6
  86.8 1.2 %copy-done.6 = f32[3,40,2304]{2,1,0:T(8,128)S(1)} copy-done((f32[3,40,2304]{2,1,0:T(8,128)S(1)}, f32[3,40,2304]{2,1,0:T(8,128)}, u32[]{:S(2)}) %copy-start.6) | copy-done | bytes 1105944
  88.0 1.9 %second.1 = f32[2,3,40,2304]{3,2,1,0:T(8,128)} custom-call(s32[1]{0:T(128)} %bitcast.me, s32[3,16]{1,0:T(4,128)S(1)} %get-tuple-element.19.table, s32[1,30]{1,0:T(1,128)S(1)} %bitcast.6, f32[16,30]{1,0:T(8,128)S(1)} %bitcast.4, bf16[16,40,896]{2,1,0:T(8,128)(2,1)S(1)} %all_to_all.21.back.parts, f32[3,40,2304]{2,1,0:T(8,128)S(1)} %copy-done.6), custom_call_target="tpu_custom_call" | custom-call | flops 20000000 | bytes 4000000 | tf_op jit(solution)/shard_map/second/pallas_call | solution.py:487
  90.0 6.0 %all-to-all-done.3.sums = f32[16,32,128]{2,1,0:T(8,128)S(1)} async-done(((f32[16,32,128]{2,1,0:T(8,128)}), f32[16,32,128]{2,1,0:T(8,128)S(1)}, u32[]{:S(2)}, u32[]{:S(2)}) %all-to-all-start.3) | async-done | bytes 262176 | tf_op jit(solution)/shard_map/all_to_all | solution.py:388
  96.0 0.9 join.1
  (1 shorter events, 0.0 us)
Async XLA Ops:
  0.6 21.9 %copy-start.1 = (s32[1,16]{1,0:T(1,128)S(1)}, s32[1,16]{1,0:T(1,128)}, u32[]{:S(2)}) copy-start(s32[1,16]{1,0:T(1,128)} %anchor.7) | copy-start | bytes 196
  0.6 21.9 %copy-start.3 = (s32[1,16]{1,0:T(1,128)S(1)}, s32[1,16]{1,0:T(1,128)}, u32[]{:S(2)}) copy-start(s32[1,16]{1,0:T(1,128)} %owner.3) | copy-start | bytes 196
  20.6 6.6 %collective-permute-start = (bf16[16,40,128]{2,1,0:T(8,128)(2,1)S(1)}, bf16[16,40,128]{2,1,0:T(8,128)(2,1)S(1)}, u32[]{:S(2)}, u32[]{:S(2)}) collective-permute-start(bf16[16,40,128]{2,1,0:T(8,128)(2,1)S(1)} %slice.4), channel_id=1, source_target_pairs={{0,16},{1,17},{4,20},{5,21},{8,24},{9,25},{12,28},{13,29},{16,32},... | collective-permute-start | bytes 491528 | tf_op jit(solution)/shard_map/ppermute | solution.py:369
  29.2 3.8 %copy-start = (bf16[64,1024]{1,0:T(8,128)(2,1)S(1)}, bf16[64,1024]{1,0:T(8,128)(2,1)}, u32[]{:S(2)}) copy-start(bf16[64,1024]{1,0:T(8,128)(2,1)} %conductivity.2) | copy-start | bytes 393220
  29.3 19.0 %copy-start.2 = (f32[1,16,30]{2,1,0:T(8,128)S(1)}, f32[1,16,30]{2,1,0:T(8,128)}, u32[]{:S(2)}) copy-start(f32[1,16,30]{2,1,0:T(8,128)} %param.11) | copy-start | bytes 5764
  29.3 19.0 %copy-start.4 = (s32[30]{0:T(128)S(1)}, s32[30]{0:T(128)}, u32[]{:S(2)}) copy-start(s32[30]{0:T(128)} %param.10) | copy-start | bytes 364
  29.3 19.0 %all-to-all-start.1 = ((bf16[16,40,640]{2,1,0:T(8,128)(2,1)}), bf16[16,40,640]{2,1,0:T(8,128)(2,1)S(1)}, u32[]{:S(2)}, u32[]{:S(2)}) async-start(bf16[16,40,640]{2,1,0:T(8,128)(2,1)} %get-tuple-element.23), calls=%async_computation.1 | async-start | bytes 1638400 | tf_op jit(solution)/shard_map/all_to_all | solution.py:388
  53.1 22.6 %copy-start.5 = (f32[3,40,2304]{2,1,0:T(8,128)}, f32[3,40,2304]{2,1,0:T(8,128)S(1)}, u32[]{:S(2)}) copy-start(f32[3,40,2304]{2,1,0:T(8,128)S(1)} %get-tuple-element.32.own) | copy-start | bytes 3317764
  76.7 4.0 %collective-permute-start.1 = (f32[4,40,128]{2,1,0:T(8,128)S(1)}, f32[4,40,128]{2,1,0:T(8,128)S(1)}, u32[]{:S(2)}, u32[]{:S(2)}) collective-permute-start(f32[4,40,128]{2,1,0:T(8,128)S(1)} %scatter_halo.1), channel_id=1, source_target_pairs={{8,24},{9,25},{10,26},{11,27},{12,28},{13,29},{14,30},{15,31},{16,... | collective-permute-start | bytes 245768 | tf_op jit(solution)/shard_map/ppermute | solution.py:369
  81.5 14.5 %all-to-all-start.3 = ((f32[16,32,128]{2,1,0:T(8,128)}), f32[16,32,128]{2,1,0:T(8,128)S(1)}, u32[]{:S(2)}, u32[]{:S(2)}) async-start(f32[16,32,128]{2,1,0:T(8,128)} %collect.1), calls=%async_computation.3 | async-start | bytes 524288 | tf_op jit(solution)/shard_map/all_to_all | solution.py:388
  86.8 1.2 %copy-start.6 = (f32[3,40,2304]{2,1,0:T(8,128)S(1)}, f32[3,40,2304]{2,1,0:T(8,128)}, u32[]{:S(2)}) copy-start(f32[3,40,2304]{2,1,0:T(8,128)} %copy-done.5) | copy-start | bytes 3317764

commit v6 on v5

--- a/solution.py
+++ b/solution.py
@@ -431,17 +431,8 @@
         compiler_params=PARAMS,
         name="cut_halo",
     )(anchor_x, owner, table, halo_tiles, own_cut, windows)
-    windows, layers = lax.optimization_barrier((windows, conductivity))
-    smooth = pl.pallas_call(
-        regularize_kernel,
-        out_shape=jax.ShapeDtypeStruct(conductivity.shape, F32),
-        in_specs=[VMEM],
-        out_specs=VMEM,
-        compiler_params=PARAMS,
-        cost_estimate=SMALL,
-        name="regularize",
-    )(layers)
-    parts, smooth = lax.optimization_barrier((exchange(windows), smooth))
+    windows, me = lax.optimization_barrier((windows, me))
+    parts = exchange(windows)
     lam, back = pl.pallas_call(
         solve_kernel,
         out_shape=(
@@ -483,7 +474,16 @@
         compiler_params=PARAMS,
         name="collect",
     )(own_rows, halo_rows)
-    columns, back = lax.optimization_barrier((columns, back))
+    columns, back, layers = lax.optimization_barrier((columns, back, conductivity))
+    smooth = pl.pallas_call(
+        regularize_kernel,
+        out_shape=jax.ShapeDtypeStruct(conductivity.shape, F32),
+        in_specs=[VMEM],
+        out_specs=VMEM,
+        compiler_params=PARAMS,
+        cost_estimate=SMALL,
+        name="regularize",
+    )(layers)
     adjoint_field = pl.pallas_call(
         second_kernel,
         out_shape=jax.ShapeDtypeStruct((MOST, 3, FZ, LANES), F32),

time: 97.4 us -> 95.5 us (0.980)
  blocking collectives: 40.7 us -> 58.2 us
  waiting for transfers between devices: 23.7 us -> 7.03 us
  starting transfers between devices: 12.9 us -> 9.28 us
  Pallas kernels: 17.4 us -> 19.7 us
  local copies, waits for them, and re-layouts: 1.3 us -> 0.06 us
    all_to_all x2 -> x3, blocking collectives: 40.7 us -> 58.2 us  [exchange(): return lax.all_to_all(blocks, 'dev', 0, 0, tiled=True)]
    all_to_all x2 -> x1, waiting for transfers between devices: 21.1 us -> 3.86 us  [exchange(): return lax.all_to_all(blocks, 'dev', 0, 0, tiled=True)]
    all_to_all x2 -> x1, starting transfers between devices: 9.07 us -> 5.31 us  [exchange(): return lax.all_to_all(blocks, 'dev', 0, 0, tiled=True)]
    pallas_call x1, Pallas kernels: 1.94 us -> 5.4 us  [per_device(): pl.pallas_call(second_kernel, out_shape=jax.ShapeDtypeStruct((MOST, 3, FZ...]
    unnamed x14 -> x10, local copies, waits for them, and re-layouts: 1.27 us -> 0.03 us
  transfers between devices with their start and end apart: 4 -> 3, of which waited for: 4 -> 3; matrix products, arithmetic and copies ran while one was open for 0% -> 0% of each run, Pallas kernels for 6% -> 9%
where the time goes in v6:
time: 95.5 us; the launch traced here: 95 us
  blocking collectives  58.2 us (61%)
  Pallas kernels  19.7 us (21%)
  starting transfers between devices  9.28 us (10%)
  waiting for transfers between devices  7.03 us (7%)
    all_to_all x3, blocking collectives, exchange(): return lax.all_to_all(blocks, 'dev', 0, 0, tiled=True)  58.2 us
    pallas_call x1, Pallas kernels, per_device(): pl.pallas_call(second_kernel, out_shape=jax.ShapeDtypeStruct((MOST, 3, FZ...  5.4 us
    all_to_all x1, starting transfers between devices, exchange(): return lax.all_to_all(blocks, 'dev', 0, 0, tiled=True)  5.31 us
    pallas_call x1, Pallas kernels, per_device(): pl.pallas_call(solve_kernel, out_shape=(jax.ShapeDtypeStruct((3, FZ, LANE...  4.78 us
    ppermute x2, starting transfers between devices, to_neighbours(): return lax.ppermute(array, ('row', 'dev'), pairs)  3.97 us
    all_to_all x1, waiting for transfers between devices, exchange(): return lax.all_to_all(blocks, 'dev', 0, 0, tiled=True)  3.86 us
    ppermute x2, waiting for transfers between devices, to_neighbours(): return lax.ppermute(array, ('row', 'dev'), pairs)  3.17 us
    pallas_call x1, Pallas kernels, per_device(): pl.pallas_call(cut_own_kernel, out_shape=(jax.ShapeDtypeStruct((N_DEV, FZ...  2.51 us
  transfers between devices with their start and end apart: 3, of which 3 were waited for; matrix products, arithmetic and copies ran while one was open for 0% of the time, Pallas kernels for 9%

profile of v6, /device:TPU:96, one launch (start us, length us, event | category | flops | bytes accessed | tf_op | source)
XLA Modules:
  0.0 95.0 jit_solution(16479439452080033328)
XLA Ops:
  0.6 0.0 copy-start.1
  0.6 0.0 copy-start.3
  0.6 1.8 %tile.1 = bf16[16,40,384]{2,1,0:T(8,128)(2,1)} custom-call(bf16[3,64,1024]{2,1,0:T(8,128)(2,1)} %primary.1, bf16[64,1024]{1,0:T(8,128)(2,1)} %conductivity.2), custom_call_target="tpu_custom_call" | custom-call | tf_op jit(solution)/shard_map/tile/pallas_call | solution.py:394
  2.4 18.2 %all_to_all.20.tiles = bf16[16,40,384]{2,1,0:T(8,128)(2,1)S(1)} all-to-all(bf16[16,40,384]{2,1,0:T(8,128)(2,1)} %tile.1), channel_id=1, replica_groups=mesh['row'=16,'dev'=16] {'dev'}, dimensions={0} | all-to-all | bytes 983040 | tf_op jit(solution)/shard_map/all_to_all | solution.py:388
  20.6 1.9 %collective-permute-start = (bf16[16,40,128]{2,1,0:T(8,128)(2,1)S(1)}, bf16[16,40,128]{2,1,0:T(8,128)(2,1)S(1)}, u32[]{:S(2)}, u32[]{:S(2)}) collective-permute-start(bf16[16,40,128]{2,1,0:T(8,128)(2,1)S(1)} %slice.4), channel_id=1, source_target_pairs={{0,16},{1,17},{4,20},{5,21},{8,24},{9,25},{12,28},{13,29},{16,32},... | collective-permute-start | bytes 491528 | tf_op jit(solution)/shard_map/ppermute | solution.py:369
  22.6 0.0 copy-done.1
  22.6 0.0 copy-done.3
  22.6 2.5 %cut_own.1 = (bf16[16,40,384]{2,1,0:T(8,128)(2,1)S(1)}, bf16[16,40,640]{2,1,0:T(8,128)(2,1)S(1)}, s32[3,16]{1,0:T(4,128)S(1)}) custom-call(s32[1,16]{1,0:T(1,128)S(1)} %copy-done.1, s32[1,16]{1,0:T(1,128)S(1)} %copy-done.3, bf16[16,40,384]{2,1,0:T(8,128)(2,1)S(1)} %all_to_all.20.tiles), custom_call_target="tpu_custom_call" | custom-call | flops 1000000 | bytes 1000000 | tf_op jit(solution)/shard_map/cut_own/pallas_call | solution.py:410
  25.1 2.2 %collective-permute-done.tiles = bf16[16,40,128]{2,1,0:T(8,128)(2,1)S(1)} collective-permute-done((bf16[16,40,128]{2,1,0:T(8,128)(2,1)S(1)}, bf16[16,40,128]{2,1,0:T(8,128)(2,1)S(1)}, u32[]{:S(2)}, u32[]{:S(2)}) %collective-permute-start) | collective-permute-done | bytes 163872 | tf_op jit(solution)/shard_map/ppermute | solution.py:369
  27.3 1.4 %cut_halo.1 = (bf16[16,40,640]{2,1,0:T(8,128)(2,1)S(1)}, bf16[17,40,640]{2,1,0:T(8,128)(2,1)S(1)}) custom-call(s32[1,16]{1,0:T(1,128)S(1)} %copy-done.1, s32[1,16]{1,0:T(1,128)S(1)} %copy-done.3, s32[3,16]{1,0:T(4,128)S(1)} %get-tuple-element.18.table, bf16[16,40,128]{2,1,0:T(8,128)(2,1)S(1)} %collective-permute-done.tiles, ...), custom_call_target="tpu_custom_call", output_to_operand_aliasing={{0}: (5, {})} | custom-call | tf_op jit(solution)/shard_map/cut_halo/pallas_call | solution.py:424
  28.7 0.0 copy-start.2
  28.7 0.0 copy-start.4
  28.7 17.4 %all_to_all.21.parts = bf16[16,40,640]{2,1,0:T(8,128)(2,1)S(1)} all-to-all(bf16[16,40,640]{2,1,0:T(8,128)(2,1)S(1)} %get-tuple-element.23), channel_id=1, replica_groups=mesh['row'=16,'dev'=16] {'dev'}, dimensions={0} | all-to-all | bytes 1638400 | tf_op jit(solution)/shard_map/all_to_all | solution.py:388
  46.1 0.0 copy-done.2
  46.1 0.0 copy-done.4
  46.1 4.8 %solve.1 = (f32[3,40,2304]{2,1,0:T(8,128)S(1)}, bf16[16,40,896]{2,1,0:T(8,128)(2,1)S(1)}) custom-call(s32[1]{0:T(128)} %bitcast.me, s32[3,16]{1,0:T(4,128)S(1)} %get-tuple-element.18.table, s32[1,30]{1,0:T(1,128)S(1)} %bitcast.5, f32[16,30]{1,0:T(8,128)S(1)} %bitcast.3, bf16[16,40,640]{2,1,0:T(8,128)(2,1)S(1)} %all_to_all.21.parts, ...), custom_call_target="tpu_custom_call" | custom-call | tf_op jit(solution)/shard_map/solve/pallas_call | solution.py:436
  50.9 22.6 %all_to_all.22.back.parts = bf16[16,40,896]{2,1,0:T(8,128)(2,1)S(1)} all-to-all(bf16[16,40,896]{2,1,0:T(8,128)(2,1)S(1)} %get-tuple-element.25), channel_id=1, replica_groups=mesh['row'=16,'dev'=16] {'dev'}, dimensions={0} | all-to-all | bytes 2293760 | tf_op jit(solution)/shard_map/all_to_all | solution.py:388
  73.5 1.0 %scatter_halo.1 = f32[4,40,128]{2,1,0:T(8,128)S(1)} custom-call(s32[1,16]{1,0:T(1,128)S(1)} %copy-done.1, s32[3,16]{1,0:T(4,128)S(1)} %get-tuple-element.18.table, bf16[16,40,896]{2,1,0:T(8,128)(2,1)S(1)} %all_to_all.22.back.parts), custom_call_target="tpu_custom_call" | custom-call | tf_op jit(solution)/shard_map/scatter_halo/pallas_call | solution.py:449
  74.5 0.0 copy-start
  74.5 2.1 %collective-permute-start.1 = (f32[4,40,128]{2,1,0:T(8,128)S(1)}, f32[4,40,128]{2,1,0:T(8,128)S(1)}, u32[]{:S(2)}, u32[]{:S(2)}) collective-permute-start(f32[4,40,128]{2,1,0:T(8,128)S(1)} %scatter_halo.1), channel_id=1, source_target_pairs={{8,24},{9,25},{10,26},{11,27},{12,28},{13,29},{14,30},{15,31},{16,... | collective-permute-start | bytes 245768 | tf_op jit(solution)/shard_map/ppermute | solution.py:369
  76.5 1.0 %scatter_own.1.own = f32[2,5,40,128]{3,2,1,0:T(8,128)S(1)} custom-call(s32[1,16]{1,0:T(1,128)S(1)} %copy-done.1, s32[3,16]{1,0:T(4,128)S(1)} %get-tuple-element.18.table, bf16[16,40,896]{2,1,0:T(8,128)(2,1)S(1)} %all_to_all.22.back.parts), custom_call_target="tpu_custom_call" | custom-call | flops 1000000 | bytes 1000000 | tf_op jit(solution)/shard_map/scatter_own/pallas_call | solution.py:460
  77.6 1.0 %collective-permute-done.1.halo = f32[4,40,128]{2,1,0:T(8,128)S(1)} collective-permute-done((f32[4,40,128]{2,1,0:T(8,128)S(1)}, f32[4,40,128]{2,1,0:T(8,128)S(1)}, u32[]{:S(2)}, u32[]{:S(2)}) %collective-permute-start.1) | collective-permute-done | bytes 81952 | tf_op jit(solution)/shard_map/ppermute | solution.py:369
  78.6 0.8 collect.1
  79.4 5.3 %all-to-all-start.3 = ((f32[16,32,128]{2,1,0:T(8,128)}), f32[16,32,128]{2,1,0:T(8,128)S(1)}, u32[]{:S(2)}, u32[]{:S(2)}) async-start(f32[16,32,128]{2,1,0:T(8,128)} %collect.1), calls=%async_computation.3 | async-start | bytes 524288 | tf_op jit(solution)/shard_map/all_to_all | solution.py:388
  84.7 0.0 copy-done
  84.7 0.1 regularize.1.smooth
  84.8 5.4 %second.1 = f32[2,3,40,2304]{3,2,1,0:T(8,128)} custom-call(s32[1]{0:T(128)} %bitcast.me, s32[3,16]{1,0:T(4,128)S(1)} %get-tuple-element.18.table, s32[1,30]{1,0:T(1,128)S(1)} %bitcast.6, f32[16,30]{1,0:T(8,128)S(1)} %bitcast.4, bf16[16,40,896]{2,1,0:T(8,128)(2,1)S(1)} %all_to_all.22.back.parts, f32[3,40,2304]{2,1,0:T(8,128)S(1)} %get-tuple-element.30.own), custom_call_target="tpu_custom_call" | custom-call | flops 20000000 | bytes 4000000 | tf_op jit(solution)/shard_map/second/pallas_call | solution.py:487
  90.2 3.9 %all-to-all-done.3.sums = f32[16,32,128]{2,1,0:T(8,128)S(1)} async-done(((f32[16,32,128]{2,1,0:T(8,128)}), f32[16,32,128]{2,1,0:T(8,128)S(1)}, u32[]{:S(2)}, u32[]{:S(2)}) %all-to-all-start.3) | async-done | bytes 262176 | tf_op jit(solution)/shard_map/all_to_all | solution.py:388
  94.1 0.9 join.1
  (1 shorter events, 0.0 us)
Async XLA Ops:
  0.6 22.0 %copy-start.1 = (s32[1,16]{1,0:T(1,128)S(1)}, s32[1,16]{1,0:T(1,128)}, u32[]{:S(2)}) copy-start(s32[1,16]{1,0:T(1,128)} %anchor.7) | copy-start | bytes 196
  0.6 22.0 %copy-start.3 = (s32[1,16]{1,0:T(1,128)S(1)}, s32[1,16]{1,0:T(1,128)}, u32[]{:S(2)}) copy-start(s32[1,16]{1,0:T(1,128)} %owner.3) | copy-start | bytes 196
  20.6 6.6 %collective-permute-start = (bf16[16,40,128]{2,1,0:T(8,128)(2,1)S(1)}, bf16[16,40,128]{2,1,0:T(8,128)(2,1)S(1)}, u32[]{:S(2)}, u32[]{:S(2)}) collective-permute-start(bf16[16,40,128]{2,1,0:T(8,128)(2,1)S(1)} %slice.4), channel_id=1, source_target_pairs={{0,16},{1,17},{4,20},{5,21},{8,24},{9,25},{12,28},{13,29},{16,32},... | collective-permute-start | bytes 491528 | tf_op jit(solution)/shard_map/ppermute | solution.py:369
  28.7 17.4 %copy-start.2 = (f32[1,16,30]{2,1,0:T(8,128)S(1)}, f32[1,16,30]{2,1,0:T(8,128)}, u32[]{:S(2)}) copy-start(f32[1,16,30]{2,1,0:T(8,128)} %param.11) | copy-start | bytes 5764
  28.7 17.4 %copy-start.4 = (s32[30]{0:T(128)S(1)}, s32[30]{0:T(128)}, u32[]{:S(2)}) copy-start(s32[30]{0:T(128)} %param.10) | copy-start | bytes 364
  74.5 10.3 %copy-start = (bf16[64,1024]{1,0:T(8,128)(2,1)S(1)}, bf16[64,1024]{1,0:T(8,128)(2,1)}, u32[]{:S(2)}) copy-start(bf16[64,1024]{1,0:T(8,128)(2,1)} %conductivity.2) | copy-start | bytes 393220
  74.5 4.1 %collective-permute-start.1 = (f32[4,40,128]{2,1,0:T(8,128)S(1)}, f32[4,40,128]{2,1,0:T(8,128)S(1)}, u32[]{:S(2)}, u32[]{:S(2)}) collective-permute-start(f32[4,40,128]{2,1,0:T(8,128)S(1)} %scatter_halo.1), channel_id=1, source_target_pairs={{8,24},{9,25},{10,26},{11,27},{12,28},{13,29},{14,30},{15,31},{16,... | collective-permute-start | bytes 245768 | tf_op jit(solution)/shard_map/ppermute | solution.py:369
  79.4 14.7 %all-to-all-start.3 = ((f32[16,32,128]{2,1,0:T(8,128)}), f32[16,32,128]{2,1,0:T(8,128)S(1)}, u32[]{:S(2)}, u32[]{:S(2)}) async-start(f32[16,32,128]{2,1,0:T(8,128)} %collect.1), calls=%async_computation.3 | async-start | bytes 524288 | tf_op jit(solution)/shard_map/all_to_all | solution.py:388

commit v7 on v6

--- a/solution.py
+++ b/solution.py
@@ -336,26 +336,32 @@
             out[4 * g + n] = v
 
 
-def join_kernel(me, sums, smooth, out):
+def join_kernel(me, sums, smooth, out_to, out, sems):
+    deep = pltpu.make_async_copy(smooth.at[FZ:, :], out_to.at[FZ:, :], sems.at[0])
+    deep.start()
+    copies = [deep]
     lane = lane_iota(FZ)
     base = TX * (me[0] % 4)
-    made = []
-    for v in range(8):
-        halves = []
-        for n in range(2):
-            top = turn(sums[2 * v + n], 64 * n - base)
-            even, odd = (turn(sums[2 * v + n, 8 * m : 8 * m + 8], 64 * n + 32 + 32 * m - base) for m in range(2))
-            halves.append(jnp.concatenate([top, jnp.where(lane[:8] % 64 < TX, even, odd)], 0))
-        made.append(jnp.where(lane < 64, halves[0], halves[1]))
-    for j in range(N_DEV):
-        v = (24 + j) // 4 if j < 8 else (j - 8) // 4
-        at = TX * (j % 4) - base
-        halo = jnp.concatenate([turn(sums[j], at - 64), turn(sums[j, 16:24], at - 96)], 0)
-        made[v] = made[v] + jnp.where(lane // TX == j % 4, halo, 0.0)
-    for v in range(8):
-        at = slice(128 * v, 128 * v + 128)
-        out[:FZ, at] = smooth[:FZ, at] + made[v]
-    out[FZ:, :] = smooth[FZ:, :]
+    for order, (first, last) in enumerate(((2, 6), (0, 2), (6, 8))):
+        for v in range(first, last):
+            halves = []
+            for n in range(2):
+                top = turn(sums[2 * v + n], 64 * n - base)
+                even, odd = (turn(sums[2 * v + n, 8 * m : 8 * m + 8], 64 * n + 32 + 32 * m - base) for m in range(2))
+                halves.append(jnp.concatenate([top, jnp.where(lane[:8] % 64 < TX, even, odd)], 0))
+            made = jnp.where(lane < 64, halves[0], halves[1])
+            for j in range(N_DEV):
+                if v == ((24 + j) // 4 if j < 8 else (j - 8) // 4):
+                    at = TX * (j % 4) - base
+                    halo = jnp.concatenate([turn(sums[j], at - 64), turn(sums[j, 16:24], at - 96)], 0)
+                    made = made + jnp.where(lane // TX == j % 4, halo, 0.0)
+            lanes = slice(128 * v, 128 * v + 128)
+            out[:, lanes] = smooth[:FZ, lanes] + made
+        lanes = slice(128 * first, 128 * last)
+        copies.append(pltpu.make_async_copy(out.at[:, lanes], out_to.at[:FZ, lanes], sems.at[1 + order]))
+        copies[-1].start()
+    for copy in copies:
+        copy.wait()
 
 
 def to_neighbours(array, goes_up):
@@ -499,7 +505,8 @@
         join_kernel,
         out_shape=jax.ShapeDtypeStruct(conductivity.shape, F32),
         in_specs=[SMEM, VMEM, VMEM],
-        out_specs=VMEM,
+        out_specs=ANY,
+        scratch_shapes=[pltpu.VMEM((FZ, TX * TY), F32), pltpu.SemaphoreType.DMA((4,))],
         compiler_params=PARAMS,
         name="join",
     )(me, columns, smooth)

time: 95.5 us -> 95.5 us (level)
  Pallas kernels: 19.7 us -> 16.2 us
  waiting for transfers between devices: 7.03 us -> 10.5 us
    all_to_all x1, waiting for transfers between devices: 3.86 us -> 7.33 us  [exchange(): return lax.all_to_all(blocks, 'dev', 0, 0, tiled=True)]
    pallas_call x1, Pallas kernels: 5.4 us -> 1.94 us  [per_device(): pl.pallas_call(second_kernel, out_shape=jax.ShapeDtypeStruct((MOST, 3, FZ...]
  transfers between devices with their start and end apart: 3 -> 3, of which waited for: 3 -> 3; matrix products, arithmetic and copies ran while one was open for 0% -> 0% of each run, Pallas kernels for 9% -> 6%
where the time goes in v7:
time: 95.5 us; the launch traced here: 95 us
  blocking collectives  58.2 us (61%)
  Pallas kernels  16.2 us (17%)
  waiting for transfers between devices  10.5 us (11%)
  starting transfers between devices  9.28 us (10%)
    all_to_all x3, blocking collectives, exchange(): return lax.all_to_all(blocks, 'dev', 0, 0, tiled=True)  58.2 us
    all_to_all x1, waiting for transfers between devices, exchange(): return lax.all_to_all(blocks, 'dev', 0, 0, tiled=True)  7.33 us
    all_to_all x1, starting transfers between devices, exchange(): return lax.all_to_all(blocks, 'dev', 0, 0, tiled=True)  5.31 us
    pallas_call x1, Pallas kernels, per_device(): pl.pallas_call(solve_kernel, out_shape=(jax.ShapeDtypeStruct((3, FZ, LANE...  4.78 us
    ppermute x2, starting transfers between devices, to_neighbours(): return lax.ppermute(array, ('row', 'dev'), pairs)  3.97 us
    ppermute x2, waiting for transfers between devices, to_neighbours(): return lax.ppermute(array, ('row', 'dev'), pairs)  3.17 us
    pallas_call x1, Pallas kernels, per_device(): pl.pallas_call(cut_own_kernel, out_shape=(jax.ShapeDtypeStruct((N_DEV, FZ...  2.51 us
    pallas_call x1, Pallas kernels, per_device(): pl.pallas_call(second_kernel, out_shape=jax.ShapeDtypeStruct((MOST, 3, FZ...  1.94 us
  transfers between devices with their start and end apart: 3, of which 3 were waited for; matrix products, arithmetic and copies ran while one was open for 0% of the time, Pallas kernels for 6%

profile of v7, /device:TPU:96, one launch (start us, length us, event | category | flops | bytes accessed | tf_op | source)
XLA Modules:
  0.0 95.0 jit_solution(816233660693490032)
XLA Ops:
  0.6 0.0 copy-start.1
  0.6 0.0 copy-start.3
  0.6 1.8 %tile.1 = bf16[16,40,384]{2,1,0:T(8,128)(2,1)} custom-call(bf16[3,64,1024]{2,1,0:T(8,128)(2,1)} %primary.1, bf16[64,1024]{1,0:T(8,128)(2,1)} %conductivity.2), custom_call_target="tpu_custom_call" | custom-call | tf_op jit(solution)/shard_map/tile/pallas_call | solution.py:400
  2.4 18.2 %all_to_all.20.tiles = bf16[16,40,384]{2,1,0:T(8,128)(2,1)S(1)} all-to-all(bf16[16,40,384]{2,1,0:T(8,128)(2,1)} %tile.1), channel_id=1, replica_groups=mesh['row'=16,'dev'=16] {'dev'}, dimensions={0} | all-to-all | bytes 983040 | tf_op jit(solution)/shard_map/all_to_all | solution.py:394
  20.6 1.9 %collective-permute-start = (bf16[16,40,128]{2,1,0:T(8,128)(2,1)S(1)}, bf16[16,40,128]{2,1,0:T(8,128)(2,1)S(1)}, u32[]{:S(2)}, u32[]{:S(2)}) collective-permute-start(bf16[16,40,128]{2,1,0:T(8,128)(2,1)S(1)} %slice.4), channel_id=1, source_target_pairs={{0,16},{1,17},{4,20},{5,21},{8,24},{9,25},{12,28},{13,29},{16,32},... | collective-permute-start | bytes 491528 | tf_op jit(solution)/shard_map/ppermute | solution.py:375
  22.6 0.0 copy-done.1
  22.6 0.0 copy-done.3
  22.6 2.5 %cut_own.1 = (bf16[16,40,384]{2,1,0:T(8,128)(2,1)S(1)}, bf16[16,40,640]{2,1,0:T(8,128)(2,1)S(1)}, s32[3,16]{1,0:T(4,128)S(1)}) custom-call(s32[1,16]{1,0:T(1,128)S(1)} %copy-done.1, s32[1,16]{1,0:T(1,128)S(1)} %copy-done.3, bf16[16,40,384]{2,1,0:T(8,128)(2,1)S(1)} %all_to_all.20.tiles), custom_call_target="tpu_custom_call" | custom-call | flops 1000000 | bytes 1000000 | tf_op jit(solution)/shard_map/cut_own/pallas_call | solution.py:416
  25.1 2.2 %collective-permute-done.tiles = bf16[16,40,128]{2,1,0:T(8,128)(2,1)S(1)} collective-permute-done((bf16[16,40,128]{2,1,0:T(8,128)(2,1)S(1)}, bf16[16,40,128]{2,1,0:T(8,128)(2,1)S(1)}, u32[]{:S(2)}, u32[]{:S(2)}) %collective-permute-start) | collective-permute-done | bytes 163872 | tf_op jit(solution)/shard_map/ppermute | solution.py:375
  27.3 1.4 %cut_halo.1 = (bf16[16,40,640]{2,1,0:T(8,128)(2,1)S(1)}, bf16[17,40,640]{2,1,0:T(8,128)(2,1)S(1)}) custom-call(s32[1,16]{1,0:T(1,128)S(1)} %copy-done.1, s32[1,16]{1,0:T(1,128)S(1)} %copy-done.3, s32[3,16]{1,0:T(4,128)S(1)} %get-tuple-element.18.table, bf16[16,40,128]{2,1,0:T(8,128)(2,1)S(1)} %collective-permute-done.tiles, ...), custom_call_target="tpu_custom_call", output_to_operand_aliasing={{0}: (5, {})} | custom-call | tf_op jit(solution)/shard_map/cut_halo/pallas_call | solution.py:430
  28.7 0.0 copy-start.2
  28.7 0.0 copy-start.4
  28.7 17.4 %all_to_all.21.parts = bf16[16,40,640]{2,1,0:T(8,128)(2,1)S(1)} all-to-all(bf16[16,40,640]{2,1,0:T(8,128)(2,1)S(1)} %get-tuple-element.23), channel_id=1, replica_groups=mesh['row'=16,'dev'=16] {'dev'}, dimensions={0} | all-to-all | bytes 1638400 | tf_op jit(solution)/shard_map/all_to_all | solution.py:394
  46.1 0.0 copy-done.2
  46.1 0.0 copy-done.4
  46.1 4.8 %solve.1 = (f32[3,40,2304]{2,1,0:T(8,128)S(1)}, bf16[16,40,896]{2,1,0:T(8,128)(2,1)S(1)}) custom-call(s32[1]{0:T(128)} %bitcast.me, s32[3,16]{1,0:T(4,128)S(1)} %get-tuple-element.18.table, s32[1,30]{1,0:T(1,128)S(1)} %bitcast.5, f32[16,30]{1,0:T(8,128)S(1)} %bitcast.3, bf16[16,40,640]{2,1,0:T(8,128)(2,1)S(1)} %all_to_all.21.parts, ...), custom_call_target="tpu_custom_call" | custom-call | tf_op jit(solution)/shard_map/solve/pallas_call | solution.py:442
  50.9 22.6 %all_to_all.22.back.parts = bf16[16,40,896]{2,1,0:T(8,128)(2,1)S(1)} all-to-all(bf16[16,40,896]{2,1,0:T(8,128)(2,1)S(1)} %get-tuple-element.25), channel_id=1, replica_groups=mesh['row'=16,'dev'=16] {'dev'}, dimensions={0} | all-to-all | bytes 2293760 | tf_op jit(solution)/shard_map/all_to_all | solution.py:394
  73.5 1.0 %scatter_halo.1 = f32[4,40,128]{2,1,0:T(8,128)S(1)} custom-call(s32[1,16]{1,0:T(1,128)S(1)} %copy-done.1, s32[3,16]{1,0:T(4,128)S(1)} %get-tuple-element.18.table, bf16[16,40,896]{2,1,0:T(8,128)(2,1)S(1)} %all_to_all.22.back.parts), custom_call_target="tpu_custom_call" | custom-call | tf_op jit(solution)/shard_map/scatter_halo/pallas_call | solution.py:455
  74.5 0.0 copy-start
  74.5 2.1 %collective-permute-start.1 = (f32[4,40,128]{2,1,0:T(8,128)S(1)}, f32[4,40,128]{2,1,0:T(8,128)S(1)}, u32[]{:S(2)}, u32[]{:S(2)}) collective-permute-start(f32[4,40,128]{2,1,0:T(8,128)S(1)} %scatter_halo.1), channel_id=1, source_target_pairs={{8,24},{9,25},{10,26},{11,27},{12,28},{13,29},{14,30},{15,31},{16,... | collective-permute-start | bytes 245768 | tf_op jit(solution)/shard_map/ppermute | solution.py:375
  76.5 1.0 %scatter_own.1.own = f32[2,5,40,128]{3,2,1,0:T(8,128)S(1)} custom-call(s32[1,16]{1,0:T(1,128)S(1)} %copy-done.1, s32[3,16]{1,0:T(4,128)S(1)} %get-tuple-element.18.table, bf16[16,40,896]{2,1,0:T(8,128)(2,1)S(1)} %all_to_all.22.back.parts), custom_call_target="tpu_custom_call" | custom-call | flops 1000000 | bytes 1000000 | tf_op jit(solution)/shard_map/scatter_own/pallas_call | solution.py:466
  77.6 1.0 %collective-permute-done.1.halo = f32[4,40,128]{2,1,0:T(8,128)S(1)} collective-permute-done((f32[4,40,128]{2,1,0:T(8,128)S(1)}, f32[4,40,128]{2,1,0:T(8,128)S(1)}, u32[]{:S(2)}, u32[]{:S(2)}) %collective-permute-start.1) | collective-permute-done | bytes 81952 | tf_op jit(solution)/shard_map/ppermute | solution.py:375
  78.6 0.8 collect.1
  79.4 5.3 %all-to-all-start.3 = ((f32[16,32,128]{2,1,0:T(8,128)}), f32[16,32,128]{2,1,0:T(8,128)S(1)}, u32[]{:S(2)}, u32[]{:S(2)}) async-start(f32[16,32,128]{2,1,0:T(8,128)} %collect.1), calls=%async_computation.3 | async-start | bytes 524288 | tf_op jit(solution)/shard_map/all_to_all | solution.py:394
  84.7 0.0 copy-done
  84.7 0.1 regularize.1.smooth
  84.8 1.9 %second.1 = f32[2,3,40,2304]{3,2,1,0:T(8,128)} custom-call(s32[1]{0:T(128)} %bitcast.me, s32[3,16]{1,0:T(4,128)S(1)} %get-tuple-element.18.table, s32[1,30]{1,0:T(1,128)S(1)} %bitcast.6, f32[16,30]{1,0:T(8,128)S(1)} %bitcast.4, bf16[16,40,896]{2,1,0:T(8,128)(2,1)S(1)} %all_to_all.22.back.parts, f32[3,40,2304]{2,1,0:T(8,128)S(1)} %get-tuple-element.30.own), custom_call_target="tpu_custom_call" | custom-call | flops 20000000 | bytes 4000000 | tf_op jit(solution)/shard_map/second/pallas_call | solution.py:493
  86.8 7.3 %all-to-all-done.3.sums = f32[16,32,128]{2,1,0:T(8,128)S(1)} async-done(((f32[16,32,128]{2,1,0:T(8,128)}), f32[16,32,128]{2,1,0:T(8,128)S(1)}, u32[]{:S(2)}, u32[]{:S(2)}) %all-to-all-start.3) | async-done | bytes 262176 | tf_op jit(solution)/shard_map/all_to_all | solution.py:394
  94.1 0.9 join.1
  (1 shorter events, 0.0 us)
Async XLA Ops:
  0.6 22.0 %copy-start.1 = (s32[1,16]{1,0:T(1,128)S(1)}, s32[1,16]{1,0:T(1,128)}, u32[]{:S(2)}) copy-start(s32[1,16]{1,0:T(1,128)} %anchor.7) | copy-start | bytes 196
  0.6 22.0 %copy-start.3 = (s32[1,16]{1,0:T(1,128)S(1)}, s32[1,16]{1,0:T(1,128)}, u32[]{:S(2)}) copy-start(s32[1,16]{1,0:T(1,128)} %owner.3) | copy-start | bytes 196
  20.6 6.6 %collective-permute-start = (bf16[16,40,128]{2,1,0:T(8,128)(2,1)S(1)}, bf16[16,40,128]{2,1,0:T(8,128)(2,1)S(1)}, u32[]{:S(2)}, u32[]{:S(2)}) collective-permute-start(bf16[16,40,128]{2,1,0:T(8,128)(2,1)S(1)} %slice.4), channel_id=1, source_target_pairs={{0,16},{1,17},{4,20},{5,21},{8,24},{9,25},{12,28},{13,29},{16,32},... | collective-permute-start | bytes 491528 | tf_op jit(solution)/shard_map/ppermute | solution.py:375
  28.7 17.4 %copy-start.2 = (f32[1,16,30]{2,1,0:T(8,128)S(1)}, f32[1,16,30]{2,1,0:T(8,128)}, u32[]{:S(2)}) copy-start(f32[1,16,30]{2,1,0:T(8,128)} %param.11) | copy-start | bytes 5764
  28.7 17.4 %copy-start.4 = (s32[30]{0:T(128)S(1)}, s32[30]{0:T(128)}, u32[]{:S(2)}) copy-start(s32[30]{0:T(128)} %param.10) | copy-start | bytes 364
  74.5 10.3 %copy-start = (bf16[64,1024]{1,0:T(8,128)(2,1)S(1)}, bf16[64,1024]{1,0:T(8,128)(2,1)}, u32[]{:S(2)}) copy-start(bf16[64,1024]{1,0:T(8,128)(2,1)} %conductivity.2) | copy-start | bytes 393220
  74.5 4.1 %collective-permute-start.1 = (f32[4,40,128]{2,1,0:T(8,128)S(1)}, f32[4,40,128]{2,1,0:T(8,128)S(1)}, u32[]{:S(2)}, u32[]{:S(2)}) collective-permute-start(f32[4,40,128]{2,1,0:T(8,128)S(1)} %scatter_halo.1), channel_id=1, source_target_pairs={{8,24},{9,25},{10,26},{11,27},{12,28},{13,29},{14,30},{15,31},{16,... | collective-permute-start | bytes 245768 | tf_op jit(solution)/shard_map/ppermute | solution.py:375
  79.4 14.7 %all-to-all-start.3 = ((f32[16,32,128]{2,1,0:T(8,128)}), f32[16,32,128]{2,1,0:T(8,128)S(1)}, u32[]{:S(2)}, u32[]{:S(2)}) async-start(f32[16,32,128]{2,1,0:T(8,128)} %collect.1), calls=%async_computation.3 | async-start | bytes 524288 | tf_op jit(solution)/shard_map/all_to_all | solution.py:394
